TPU v7x, 512 devices: a whole 4x8x8 slice. The times are simulated.
512 devices in a mesh: inner: 32 (over y_hi, x, core), outer: 16 (over z, y_lo).
Axes of the slice: x: 4, y: 8 (y_hi: 4, y_lo: 2; y = y_hi * 2 + y_lo), z: 8, core: 2. Of those that a mesh axis runs over, the one named last changes fastest.
Arguments:
- query: bfloat16 [196608, 512], P(('inner', 'outer')), may hold values from -6 to 6
- keys: bfloat16 [196608, 512], P(('inner', 'outer')), may hold values from -6 to 6
- values: bfloat16 [196608, 512], P(('inner', 'outer')), may hold values from -6 to 6
- output: bfloat16 [196608, 512], P(('inner', 'outer')), may hold values from -4 to 4
- grad_output: bfloat16 [196608, 512], P(('inner', 'outer')), may hold values from -6 to 6
- log_sum_exp: float32 [8, 196608], P(None, ('inner', 'outer')), may hold values from 4 to 6
- order: int32 [512, 384], P(('inner', 'outer')), may hold values from 0 to 383, each once within a row
- layout: int32 [512, 3], P(('inner', 'outer')), may hold values 0 or 1
Outputs:
- grad_query: bfloat16 [196608, 512], P(('inner', 'outer'))
- grad_keys: bfloat16 [196608, 512], P(('inner', 'outer'))
- grad_values: bfloat16 [196608, 512], P(('inner', 'outer'))
Inputs may be any that keep to these rules, and one draw needn't show every extreme that they name: `order`: each row is a permutation of 0 to 383. `layout`: entries [b, d - 1] with b < d are ignored.
All inputs are finite; a program needn't handle non-finite values. No bound on the sum of `layout` on one device may be relied on, other than what follows from the above.
Results may differ from a plain program's by a relative error of at most 0.0049.
Values may be sent and summed in bfloat16 or wider, within the bound.
No kernel may reach another device: no remote copies, remote signals or barrier semaphores. Data moves between devices by JAX's collectives and lax.ppermute only.
A program may use at most 64 MiB of HBM per device.

v0:
```python
import jax
import jax.numpy as jnp
from jax import lax
from jax.sharding import PartitionSpec as P

SCALE = 0.125


def passed_along(block, axis, distance):
    devices = range(lax.axis_size(axis))
    route = [(i - distance, i) for i in devices if i - distance in devices]
    return lax.ppermute(block, axis, route)


def tile_grads(query, keys, values, dout, lse, delta, visible):
    f32 = jnp.float32
    scores = jnp.einsum("qhd,khd->hqk", query, keys, preferred_element_type=f32) * SCALE
    probs = jnp.where(visible, jnp.exp(scores - lse[:, :, None]), f32(0.0))
    probs_low = probs.astype(jnp.bfloat16)
    dprobs = jnp.einsum("qhd,khd->hqk", dout, values, preferred_element_type=f32)
    dscores = (probs * (dprobs - delta[:, :, None])).astype(jnp.bfloat16)
    grad_v = jnp.einsum("hqk,qhd->khd", probs_low, dout, preferred_element_type=f32)
    grad_q = SCALE * jnp.einsum("hqk,khd->qhd", dscores, keys, preferred_element_type=f32)
    grad_k = SCALE * jnp.einsum("hqk,qhd->khd", dscores, query, preferred_element_type=f32)
    return (grad_q, grad_k, grad_v)


def per_device(query, keys, values, output, grad_output, log_sum_exp, order, layout):
    rows, width = query.shape
    heads = log_sum_exp.shape[0]
    size = width // heads
    shape = (rows, heads, size)
    q = query.reshape(shape)
    k = keys.reshape(shape)
    v = values.reshape(shape)
    dout = grad_output.reshape(shape)
    delta = jnp.sum(dout.astype(jnp.float32) * output.reshape(shape).astype(jnp.float32), axis=2).T
    block = lax.axis_index(("inner", "outer"))
    window = layout.shape[1]
    rank = order[0]
    diag_visible = (rank[:, None] >= rank[None, :])[None]
    grad_q, grad_k, grad_v = tile_grads(q, k, v, dout, log_sum_exp, delta, diag_visible)
    for dist in range(1, window + 1):
        k_far, v_far = passed_along((k, v), ("inner", "outer"), dist)
        remote_valid = jnp.logical_and(layout[0, dist - 1] > 0, block >= dist)
        part_q, part_k, part_v = tile_grads(q, k_far, v_far, dout, log_sum_exp, delta, remote_valid)
        grad_q = grad_q + part_q
        home_k, home_v = passed_along((part_k, part_v), ("inner", "outer"), -dist)
        grad_k = grad_k + home_k
        grad_v = grad_v + home_v
    flat = (rows, width)
    return (
        grad_q.astype(jnp.bfloat16).reshape(flat),
        grad_k.astype(jnp.bfloat16).reshape(flat),
        grad_v.astype(jnp.bfloat16).reshape(flat),
    )


def solution(mesh):
    return jax.shard_map(
        per_device,
        mesh=mesh,
        in_specs=(
            P(("inner", "outer"), None),
            P(("inner", "outer"), None),
            P(("inner", "outer"), None),
            P(("inner", "outer"), None),
            P(("inner", "outer"), None),
            P(None, ("inner", "outer")),
            P(("inner", "outer"), None),
            P(("inner", "outer"), None),
        ),
        out_specs=(
            P(("inner", "outer"), None),
            P(("inner", "outer"), None),
            P(("inner", "outer"), None),
        ),
        check_vma=False,
    )
```

profile of v0, /device:TPU:47, one launch (start us, length us, event | category | flops | bytes accessed | tf_op | source)
XLA Modules:
  0.0 219.5 jit_solution(8876311795196829228)
XLA Ops:
  0.6 1.9 copy.35
  2.5 6.7 %collective-permute-start.5 = (bf16[384,8,64]{0,2,1:T(8,128)(2,1)}, bf16[384,8,64]{0,2,1:T(8,128)(2,1)}, u32[]{:S(2)}, u32[]{:S(2)}) collective-permute-start(bf16[384,8,64]{0,2,1:T(8,128)(2,1)} %bitcast.3), channel_id=1, source_target_pairs={{0,3},{1,4},{2,5},{3,6},{4,7},{5,8},{6,9},{7,10},{8,11},{9,12},{10... | collective-permute-start | bytes 1179656 | tf_op jit(solution)/shard_map/ppermute | solution.py:12
  9.3 4.0 %collective-permute-start.3 = (bf16[384,8,64]{0,2,1:T(8,128)(2,1)}, bf16[384,8,64]{0,2,1:T(8,128)(2,1)}, u32[]{:S(2)}, u32[]{:S(2)}) collective-permute-start(bf16[384,8,64]{0,2,1:T(8,128)(2,1)} %bitcast.3), channel_id=1, source_target_pairs={{0,2},{1,3},{2,4},{3,5},{4,6},{5,7},{6,8},{7,9},{8,10},{9,11},{10,... | collective-permute-start | bytes 1179656 | tf_op jit(solution)/shard_map/ppermute | solution.py:12
  13.3 2.3 %collective-permute-start.1 = (bf16[384,8,64]{0,2,1:T(8,128)(2,1)}, bf16[384,8,64]{0,2,1:T(8,128)(2,1)}, u32[]{:S(2)}, u32[]{:S(2)}) collective-permute-start(bf16[384,8,64]{0,2,1:T(8,128)(2,1)} %bitcast.3), channel_id=1, source_target_pairs={{0,1},{1,2},{2,3},{3,4},{4,5},{5,6},{6,7},{7,8},{8,9},{9,10},{10,1... | collective-permute-start | bytes 1179656 | tf_op jit(solution)/shard_map/ppermute | solution.py:12
  16.8 6.9 %collective-permute-start.4 = (bf16[384,8,64]{0,2,1:T(8,128)(2,1)S(1)}, bf16[384,8,64]{0,2,1:T(8,128)(2,1)}, u32[]{:S(2)}, u32[]{:S(2)}) collective-permute-start(bf16[384,8,64]{0,2,1:T(8,128)(2,1)S(1)} %bitcast.101), channel_id=1, source_target_pairs={{0,3},{1,4},{2,5},{3,6},{4,7},{5,8},{6,9},{7,10},{8,11},{9,12},{10... | collective-permute-start | bytes 1179656 | tf_op jit(solution)/shard_map/ppermute | solution.py:12
  23.7 2.3 %collective-permute-start = (bf16[384,8,64]{0,2,1:T(8,128)(2,1)S(1)}, bf16[384,8,64]{0,2,1:T(8,128)(2,1)}, u32[]{:S(2)}, u32[]{:S(2)}) collective-permute-start(bf16[384,8,64]{0,2,1:T(8,128)(2,1)S(1)} %bitcast.102), channel_id=1, source_target_pairs={{0,1},{1,2},{2,3},{3,4},{4,5},{5,6},{6,7},{7,8},{8,9},{9,10},{10,1... | collective-permute-start | bytes 1179656 | tf_op jit(solution)/shard_map/ppermute | solution.py:12
  32.2 3.4 %multiply_convert_fusion.3 = bf16[8,384,384]{2,1,0:T(8,128)(2,1)S(1)} fusion(f32[8,384,384]{2,1,0:T(8,128)S(1)} %fusion.61, f32[8,384]{1,0:T(8,128)S(1)} %bitcast.109, f32[8,384]{1,0:T(8,128)S(1)} %copy-done.4, pred[384,384]{1,0:T(8,128)(4,1)S(1)} %copy-done.3, bf16[384,8,64]{0,2,1:T(8,128)(2,1)S(1)} %bitcast.93, bf16[384,8,64]{0,2,1:T(8,128)(2,1)} %bitcast.3), kind=kOutput, calls=%fused_computation.6 | convolution fusion | flops 158072832 | bytes 8036352 | tf_op jit(solution)/shard_map/qhd,khd->hqk/dot_general | solution.py:20
  35.6 1.8 fusion.62
  40.0 23.6 %collective-permute-done = bf16[384,8,64]{0,2,1:T(8,128)(2,1)} collective-permute-done((bf16[384,8,64]{0,2,1:T(8,128)(2,1)S(1)}, bf16[384,8,64]{0,2,1:T(8,128)(2,1)}, u32[]{:S(2)}, u32[]{:S(2)}) %collective-permute-start) | collective-permute-done | bytes 393248 | tf_op jit(solution)/shard_map/ppermute | solution.py:12
  63.6 1.9 collective-permute-start.2
  65.5 1.8 fusion.63
  67.3 2.9 %multiply_convert_fusion.2 = bf16[8,384,384]{2,1,0:T(8,128)(2,1)S(1)} fusion(f32[8,384,384]{2,1,0:T(8,128)S(1)} %fusion.63, f32[8,384]{1,0:T(8,128)S(1)} %bitcast.110, f32[8,384]{1,0:T(8,128)S(1)} %copy-done.4, pred[]{:T(512)S(6)} %and.11, bf16[384,8,64]{0,2,1:T(8,128)(2,1)S(1)} %bitcast.94, bf16[384,8,64]{0,2,1:T(8,128)(2,1)} %collective-permute-done.1), kind=kOutput, calls=%fused_computation.4 | convolution fusion | flops 158072832 | bytes 7888897 | tf_op jit(solution)/shard_map/qhd,khd->hqk/dot_general | solution.py:20
  70.7 8.3 %collective-permute-start.6 = (f32[384,8,64]{0,2,1:T(8,128)S(1)}, f32[384,8,64]{0,2,1:T(8,128)S(1)}, u32[]{:S(2)}, u32[]{:S(2)}) collective-permute-start(f32[384,8,64]{0,2,1:T(8,128)S(1)} %fusion.21), channel_id=1, source_target_pairs={{1,0},{2,1},{3,2},{4,3},{5,4},{6,5},{7,6},{8,7},{9,8},{10,9},{11,1... | collective-permute-start | bytes 2359304 | tf_op jit(solution)/shard_map/ppermute | solution.py:12
  79.1 2.0 fusion.28
  81.1 6.6 %collective-permute-start.9 = (f32[384,8,64]{0,2,1:T(8,128)}, f32[384,8,64]{0,2,1:T(8,128)}, u32[]{:S(2)}, u32[]{:S(2)}) collective-permute-start(f32[384,8,64]{0,2,1:T(8,128)} %fusion.28), channel_id=1, source_target_pairs={{1,0},{2,1},{3,2},{4,3},{5,4},{6,5},{7,6},{8,7},{9,8},{10,9},{11,1... | collective-permute-start | bytes 2359304 | tf_op jit(solution)/shard_map/ppermute | solution.py:12
  88.5 2.0 fusion.31
  90.5 2.9 %multiply_convert_fusion.1 = bf16[8,384,384]{2,1,0:T(8,128)(2,1)S(1)} fusion(f32[8,384,384]{2,1,0:T(8,128)S(1)} %fusion.64, f32[8,384]{1,0:T(8,128)S(1)} %bitcast.111, f32[8,384]{1,0:T(8,128)S(1)} %copy-done.4, pred[]{:T(512)S(6)} %and.12, bf16[384,8,64]{0,2,1:T(8,128)(2,1)S(1)} %bitcast.97, bf16[384,8,64]{0,2,1:T(8,128)(2,1)} %collective-permute-done.3), kind=kOutput, calls=%fused_computation.2 | convolution fusion | flops 158072832 | bytes 7888897 | tf_op jit(solution)/shard_map/qhd,khd->hqk/dot_general | solution.py:20
  93.4 1.4 fusion.20
  94.8 2.8 %collective-permute-start.7 = (f32[384,8,64]{0,2,1:T(8,128)}, f32[384,8,64]{0,2,1:T(8,128)}, u32[]{:S(2)}, u32[]{:S(2)}) collective-permute-start(f32[384,8,64]{0,2,1:T(8,128)} %fusion.20), channel_id=1, source_target_pairs={{2,0},{3,1},{4,2},{5,3},{6,4},{7,5},{8,6},{9,7},{10,8},{11,9},{12,... | collective-permute-start | bytes 2359304 | tf_op jit(solution)/shard_map/ppermute | solution.py:12
  97.6 3.9 %collective-permute-start.10 = (f32[384,8,64]{0,2,1:T(8,128)}, f32[384,8,64]{0,2,1:T(8,128)}, u32[]{:S(2)}, u32[]{:S(2)}) collective-permute-start(f32[384,8,64]{0,2,1:T(8,128)} %fusion.31), channel_id=1, source_target_pairs={{2,0},{3,1},{4,2},{5,3},{6,4},{7,5},{8,6},{9,7},{10,8},{11,9},{12,... | collective-permute-start | bytes 2359304 | tf_op jit(solution)/shard_map/ppermute | solution.py:12
  101.5 1.8 fusion.65
  103.4 2.9 %multiply_convert_fusion = bf16[8,384,384]{2,1,0:T(8,128)(2,1)S(1)} fusion(f32[8,384,384]{2,1,0:T(8,128)S(1)} %fusion.65, f32[8,384]{1,0:T(8,128)S(1)} %bitcast.112, f32[8,384]{1,0:T(8,128)S(1)} %copy-done.4, pred[]{:T(512)S(6)} %and.13, bf16[384,8,64]{0,2,1:T(8,128)(2,1)S(1)} %bitcast.98, bf16[384,8,64]{0,2,1:T(8,128)(2,1)} %collective-permute-done.5), kind=kOutput, calls=%fused_computation | convolution fusion | flops 158072832 | bytes 7888897 | tf_op jit(solution)/shard_map/qhd,khd->hqk/dot_general | solution.py:20
  106.3 1.4 fusion.19
  107.7 2.8 %collective-permute-start.8 = (f32[384,8,64]{0,2,1:T(8,128)}, f32[384,8,64]{0,2,1:T(8,128)}, u32[]{:S(2)}, u32[]{:S(2)}) collective-permute-start(f32[384,8,64]{0,2,1:T(8,128)} %fusion.19), channel_id=1, source_target_pairs={{3,0},{4,1},{5,2},{6,3},{7,4},{8,5},{9,6},{10,7},{11,8},{12,9},{13... | collective-permute-start | bytes 2359304 | tf_op jit(solution)/shard_map/ppermute | solution.py:12
  110.5 2.0 fusion.34
  112.5 1.9 convolution_add_fusion.1
  114.5 2.8 %collective-permute-start.11 = (f32[384,8,64]{0,2,1:T(8,128)}, f32[384,8,64]{0,2,1:T(8,128)}, u32[]{:S(2)}, u32[]{:S(2)}) collective-permute-start(f32[384,8,64]{0,2,1:T(8,128)} %fusion.34), channel_id=1, source_target_pairs={{3,0},{4,1},{5,2},{6,3},{7,4},{8,5},{9,6},{10,7},{11,8},{12,9},{13... | collective-permute-start | bytes 2359304 | tf_op jit(solution)/shard_map/ppermute | solution.py:12
  117.3 1.9 fusion.66
  121.2 76.3 %collective-permute-done.7 = f32[384,8,64]{0,2,1:T(8,128)} collective-permute-done((f32[384,8,64]{0,2,1:T(8,128)}, f32[384,8,64]{0,2,1:T(8,128)}, u32[]{:S(2)}, u32[]{:S(2)}) %collective-permute-start.7) | collective-permute-done | bytes 786464 | tf_op jit(solution)/shard_map/ppermute | solution.py:12
  197.5 2.2 fusion.49
  200.6 13.7 %collective-permute-done.10 = f32[384,8,64]{0,2,1:T(8,128)} collective-permute-done((f32[384,8,64]{0,2,1:T(8,128)}, f32[384,8,64]{0,2,1:T(8,128)}, u32[]{:S(2)}, u32[]{:S(2)}) %collective-permute-start.10) | collective-permute-done | bytes 786464 | tf_op jit(solution)/shard_map/ppermute | solution.py:12
  214.3 4.3 %fusion.46 = bf16[384,8,64]{0,2,1:T(8,128)(2,1)S(1)} fusion(f32[384,8,64]{0,2,1:T(8,128)} %collective-permute-done.11, f32[384,8,64]{0,2,1:T(8,128)} %collective-permute-done.10, f32[384,8,64]{0,2,1:T(8,128)} %collective-permute-done.9, bf16[384,8,64]{0,2,1:T(8,128)(2,1)S(1)} %bitcast.100, f32[8,384,384]{2,1,0:T(8,128)} %copy-done, ...), kind=kOutput, calls=%fused_computation.42 | convolution fusion | flops 156499968 | bytes 8024064 | tf_op jit(solution)/shard_map/hqk,qhd->khd/dot_general | solution.py:22
  (40 shorter events, 13.0 us)
Async XLA Ops:
  2.5 29.6 %copy-start.4 = (f32[8,384]{1,0:T(8,128)S(1)}, f32[8,384]{1,0:T(8,128)}, u32[]{:S(2)}) copy-start(f32[8,384]{1,0:T(8,128)} %param.13) | copy-start | bytes 36868
  2.5 100.8 %collective-permute-start.5 = (bf16[384,8,64]{0,2,1:T(8,128)(2,1)}, bf16[384,8,64]{0,2,1:T(8,128)(2,1)}, u32[]{:S(2)}, u32[]{:S(2)}) collective-permute-start(bf16[384,8,64]{0,2,1:T(8,128)(2,1)} %bitcast.3), channel_id=1, source_target_pairs={{0,3},{1,4},{2,5},{3,6},{4,7},{5,8},{6,9},{7,10},{8,11},{9,12},{10... | collective-permute-start | bytes 1179656 | tf_op jit(solution)/shard_map/ppermute | solution.py:12
  9.3 81.3 %collective-permute-start.3 = (bf16[384,8,64]{0,2,1:T(8,128)(2,1)}, bf16[384,8,64]{0,2,1:T(8,128)(2,1)}, u32[]{:S(2)}, u32[]{:S(2)}) collective-permute-start(bf16[384,8,64]{0,2,1:T(8,128)(2,1)} %bitcast.3), channel_id=1, source_target_pairs={{0,2},{1,3},{2,4},{3,5},{4,6},{5,7},{6,8},{7,9},{8,10},{9,11},{10,... | collective-permute-start | bytes 1179656 | tf_op jit(solution)/shard_map/ppermute | solution.py:12
  13.3 54.0 %collective-permute-start.1 = (bf16[384,8,64]{0,2,1:T(8,128)(2,1)}, bf16[384,8,64]{0,2,1:T(8,128)(2,1)}, u32[]{:S(2)}, u32[]{:S(2)}) collective-permute-start(bf16[384,8,64]{0,2,1:T(8,128)(2,1)} %bitcast.3), channel_id=1, source_target_pairs={{0,1},{1,2},{2,3},{3,4},{4,5},{5,6},{6,7},{7,8},{8,9},{9,10},{10,1... | collective-permute-start | bytes 1179656 | tf_op jit(solution)/shard_map/ppermute | solution.py:12
  16.8 80.8 %collective-permute-start.4 = (bf16[384,8,64]{0,2,1:T(8,128)(2,1)S(1)}, bf16[384,8,64]{0,2,1:T(8,128)(2,1)}, u32[]{:S(2)}, u32[]{:S(2)}) collective-permute-start(bf16[384,8,64]{0,2,1:T(8,128)(2,1)S(1)} %bitcast.101), channel_id=1, source_target_pairs={{0,3},{1,4},{2,5},{3,6},{4,7},{5,8},{6,9},{7,10},{8,11},{9,12},{10... | collective-permute-start | bytes 1179656 | tf_op jit(solution)/shard_map/ppermute | solution.py:12
  23.7 39.8 %collective-permute-start = (bf16[384,8,64]{0,2,1:T(8,128)(2,1)S(1)}, bf16[384,8,64]{0,2,1:T(8,128)(2,1)}, u32[]{:S(2)}, u32[]{:S(2)}) collective-permute-start(bf16[384,8,64]{0,2,1:T(8,128)(2,1)S(1)} %bitcast.102), channel_id=1, source_target_pairs={{0,1},{1,2},{2,3},{3,4},{4,5},{5,6},{6,7},{7,8},{8,9},{9,10},{10,1... | collective-permute-start | bytes 1179656 | tf_op jit(solution)/shard_map/ppermute | solution.py:12
  31.2 1.0 copy-start.3
  32.0 3.6 %copy-start = (f32[8,384,384]{2,1,0:T(8,128)}, f32[8,384,384]{2,1,0:T(8,128)S(1)}, u32[]{:S(2)}) copy-start(f32[8,384,384]{2,1,0:T(8,128)S(1)} %fusion.61) | copy-start | bytes 14155780
  32.2 5.3 %copy-start.5 = (f32[384,8]{0,1:T(8,128)}, f32[384,8]{0,1:T(8,128)S(1)}, u32[]{:S(2)}) copy-start(f32[384,8]{0,1:T(8,128)S(1)} %fusion.51) | copy-start | bytes 36868
  32.2 5.3 %copy-start.7 = (s32[1,3]{1,0:T(1,128)S(1)}, s32[1,3]{1,0:T(1,128)}, u32[]{:S(2)}) copy-start(s32[1,3]{1,0:T(1,128)} %param.15) | copy-start | bytes 40
  40.0 27.3 %copy-start.6 = (f32[384,8]{0,1:T(8,128)S(1)}, f32[384,8]{0,1:T(8,128)}, u32[]{:S(2)}) copy-start(f32[384,8]{0,1:T(8,128)} %copy-done.5) | copy-start | bytes 36868
  63.6 17.5 %collective-permute-start.2 = (bf16[384,8,64]{0,2,1:T(8,128)(2,1)S(1)}, bf16[384,8,64]{0,2,1:T(8,128)(2,1)S(1)}, u32[]{:S(2)}, u32[]{:S(2)}) collective-permute-start(bf16[384,8,64]{0,2,1:T(8,128)(2,1)S(1)} %bitcast.105), channel_id=1, source_target_pairs={{0,2},{1,3},{2,4},{3,5},{4,6},{5,7},{6,8},{7,9},{8,10},{9,11},{10,... | collective-permute-start | bytes 1179656 | tf_op jit(solution)/shard_map/ppermute | solution.py:12
  70.7 43.7 %collective-permute-start.6 = (f32[384,8,64]{0,2,1:T(8,128)S(1)}, f32[384,8,64]{0,2,1:T(8,128)S(1)}, u32[]{:S(2)}, u32[]{:S(2)}) collective-permute-start(f32[384,8,64]{0,2,1:T(8,128)S(1)} %fusion.21), channel_id=1, source_target_pairs={{1,0},{2,1},{3,2},{4,3},{5,4},{6,5},{7,6},{8,7},{9,8},{10,9},{11,1... | collective-permute-start | bytes 2359304 | tf_op jit(solution)/shard_map/ppermute | solution.py:12
  81.1 119.5 %collective-permute-start.9 = (f32[384,8,64]{0,2,1:T(8,128)}, f32[384,8,64]{0,2,1:T(8,128)}, u32[]{:S(2)}, u32[]{:S(2)}) collective-permute-start(f32[384,8,64]{0,2,1:T(8,128)} %fusion.28), channel_id=1, source_target_pairs={{1,0},{2,1},{3,2},{4,3},{5,4},{6,5},{7,6},{8,7},{9,8},{10,9},{11,1... | collective-permute-start | bytes 2359304 | tf_op jit(solution)/shard_map/ppermute | solution.py:12
  94.8 102.7 %collective-permute-start.7 = (f32[384,8,64]{0,2,1:T(8,128)}, f32[384,8,64]{0,2,1:T(8,128)}, u32[]{:S(2)}, u32[]{:S(2)}) collective-permute-start(f32[384,8,64]{0,2,1:T(8,128)} %fusion.20), channel_id=1, source_target_pairs={{2,0},{3,1},{4,2},{5,3},{6,4},{7,5},{8,6},{9,7},{10,8},{11,9},{12,... | collective-permute-start | bytes 2359304 | tf_op jit(solution)/shard_map/ppermute | solution.py:12
  97.6 116.6 %collective-permute-start.10 = (f32[384,8,64]{0,2,1:T(8,128)}, f32[384,8,64]{0,2,1:T(8,128)}, u32[]{:S(2)}, u32[]{:S(2)}) collective-permute-start(f32[384,8,64]{0,2,1:T(8,128)} %fusion.31), channel_id=1, source_target_pairs={{2,0},{3,1},{4,2},{5,3},{6,4},{7,5},{8,6},{9,7},{10,8},{11,9},{12,... | collective-permute-start | bytes 2359304 | tf_op jit(solution)/shard_map/ppermute | solution.py:12
  106.3 6.2 %copy-start.1 = (f32[8,384,64]{1,2,0:T(8,128)S(1)}, f32[8,384,64]{1,2,0:T(8,128)}, u32[]{:S(2)}) copy-start(f32[8,384,64]{1,2,0:T(8,128)} %fusion.62) | copy-start | bytes 2359300
  107.7 89.8 %collective-permute-start.8 = (f32[384,8,64]{0,2,1:T(8,128)}, f32[384,8,64]{0,2,1:T(8,128)}, u32[]{:S(2)}, u32[]{:S(2)}) collective-permute-start(f32[384,8,64]{0,2,1:T(8,128)} %fusion.19), channel_id=1, source_target_pairs={{3,0},{4,1},{5,2},{6,3},{7,4},{8,5},{9,6},{10,7},{11,8},{12,9},{13... | collective-permute-start | bytes 2359304 | tf_op jit(solution)/shard_map/ppermute | solution.py:12
  114.5 5.8 %copy-start.2 = (f32[384,8,64]{0,2,1:T(8,128)}, f32[384,8,64]{0,2,1:T(8,128)S(1)}, u32[]{:S(2)}) copy-start(f32[384,8,64]{0,2,1:T(8,128)S(1)} %collective-permute-done.6) | copy-start | bytes 2359300
  114.5 99.8 %collective-permute-start.11 = (f32[384,8,64]{0,2,1:T(8,128)}, f32[384,8,64]{0,2,1:T(8,128)}, u32[]{:S(2)}, u32[]{:S(2)}) collective-permute-start(f32[384,8,64]{0,2,1:T(8,128)} %fusion.34), channel_id=1, source_target_pairs={{3,0},{4,1},{5,2},{6,3},{7,4},{8,5},{9,6},{10,7},{11,8},{12,9},{13... | collective-permute-start | bytes 2359304 | tf_op jit(solution)/shard_map/ppermute | solution.py:12
where the time goes:
time: 221 us; the launch traced here: 219 us
  waiting for transfers between devices  114 us (52%)
  starting transfers between devices  51.4 us (23%)
  matrix products  39.8 us (18%)
  local copies, waits for them, and re-layouts  10.2 us (5%)
  between operations  2.89 us (1%)
    ppermute x12, waiting for transfers between devices, passed_along(): return lax.ppermute(block, axis, route)  114 us
    ppermute x12, starting transfers between devices, passed_along(): return lax.ppermute(block, axis, route)  51.4 us
    dot_general x4, matrix products, tile_grads(): jnp.einsum('qhd,khd->hqk', dout, values, preferred_element_type=f32)  12.1 us
    dot_general x4, matrix products, tile_grads(): jnp.einsum('hqk,qhd->khd', probs_low, dout, preferred_element_type=f32)  10.3 us
    unnamed x24, local copies, waits for them, and re-layouts  9.6 us
    dot_general x4, matrix products, tile_grads(): jnp.einsum('hqk,khd->qhd', dscores, keys, preferred_element_type=f32)  6.68 us
    dot_general x4, matrix products, tile_grads(): jnp.einsum('hqk,qhd->khd', dscores, query, preferred_element_type=f32)  5.43 us
    dot_general x4, matrix products, tile_grads(): jnp.einsum('qhd,khd->hqk', query, keys, preferred_element_type=f32) * SCALE  5.26 us
  transfers between devices with their start and end apart: 12, of which 3 were waited for; matrix products, arithmetic and copies ran while one was open for 20% of the time, Pallas kernels for 0%

commit v1 on v0

v1 whole, which is shorter than its diff:
```python
import functools
import math

import jax
import jax.numpy as jnp
from jax import lax
from jax.experimental import pallas as pl
from jax.experimental.pallas import tpu as pltpu
from jax.sharding import PartitionSpec as P

AXES = ("inner", "outer")
HEADS = 8
SIZE = 64
PAIR = 2 * SIZE
CHUNKS = 2
DIRECT = False
COST = 8
HC = HEADS // CHUNKS
WC = HC * SIZE
EXP_SCALE = 0.125 / math.log(2.0)
HIDDEN = -1e30
f32 = jnp.float32
bf16 = jnp.bfloat16

VIS = 48


def dot(a, b, ca, cb):
    return lax.dot_general(a, b, (((ca,), (cb,)), ((), ())), preferred_element_type=f32)


def pieces(x):
    a = x.astype(bf16)
    r = x - a.astype(f32)
    b = r.astype(bf16)
    c = (r - b.astype(f32)).astype(bf16)
    return a, b, c


def pack_kernel(blk, layout, lse, *refs):
    far, outs, near, sems = refs[:5], refs[5 : 5 + 2 * CHUNKS], refs[-6:-1], refs[-1]
    copies = [pltpu.make_async_copy(far[i], near[i], sems.at[i]) for i in range(5)]
    for copy in copies:
        copy.start()
    for copy in copies:
        copy.wait()
    q, k, v, o, do = near
    rows = q.shape[0]
    qs, ks = outs[:CHUNKS], outs[CHUNKS:]
    for c in range(CHUNKS):
        w = slice(c * WC, (c + 1) * WC)
        ks[c][:, :WC] = k[:, w]
        ks[c][:, WC:] = v[:, w]
        qs[c][:, :WC] = q[:, w]
        qs[c][:, WC : 2 * WC] = do[:, w]
    lane = lax.broadcasted_iota(jnp.int32, (1, 128), 1)
    prod = do[...].astype(f32) * o[...].astype(f32)
    hi = prod.astype(bf16)
    lo = (prod - hi.astype(f32)).astype(bf16)
    feat = lax.broadcasted_iota(jnp.int32, (HEADS * SIZE, 128), 0) // SIZE
    flane = lax.broadcasted_iota(jnp.int32, (HEADS * SIZE, 128), 1)
    pick = jnp.where((flane % 8 == feat) & (flane >= 24) & (flane < 48), 1.0, 0.0).astype(bf16)
    delta = dot(hi, pick, 1, 0) + dot(lo, pick, 1, 0)
    d1, d2, d3 = (x.astype(f32) for x in pieces(delta))
    dpart = jnp.where(lane < 32, d1, jnp.where(lane < 40, d2, d3))
    l1, l2, l3 = (x.astype(f32) for x in pieces(lse[...] * 8.0))
    stack = jnp.concatenate([l1, l2, l3, jnp.zeros_like(l1)], 0).astype(bf16)
    r = lax.broadcasted_iota(jnp.int32, (32, 128), 0)
    c = lax.broadcasted_iota(jnp.int32, (32, 128), 1)
    eye = jnp.where((r == c) & (r < 24), 1.0, 0.0).astype(bf16)
    lpart = dot(stack, eye, 0, 0)
    vis = jnp.zeros((1, 128), f32)
    for d in (1, 2, 3):
        seen = jnp.logical_and(layout[0, d - 1] > 0, blk[0] >= d)
        vis = jnp.where((lane == VIS + d - 1) & jnp.logical_not(seen), f32(HIDDEN), vis)
    aux = jnp.where(lane < 24, lpart, jnp.where(lane < 48, dpart, jnp.broadcast_to(vis, (rows, 128))))
    qs[0][:, 2 * WC :] = aux.astype(bf16)


def tile(q, aux, kv, c, hp, dist, rank_row=None, rank_col=None):
    at = pl.ds(pl.multiple_of(hp * PAIR, PAIR), PAIR)
    at2 = pl.ds(pl.multiple_of(WC + hp * PAIR, PAIR), PAIR)
    qp, dop, kp, vp = q[:, at], q[:, at2], kv[:, at], kv[:, at2]
    lane = lax.broadcasted_iota(jnp.int32, (1, PAIR), 1)
    half = lax.broadcasted_iota(jnp.int32, qp.shape, 1) // SIZE
    qa = jnp.concatenate([qp, aux], 1)
    da = jnp.concatenate([dop, aux], 1)
    km, qm, dm, pb, db = [], [], [], [], []
    for h in range(2):
        head = c * HC + hp * 2 + h
        sel = jnp.where((lane % 8 == head) & (lane < 24), -1.0, 0.0)
        if dist is not None:
            sel = jnp.where(lane == VIS - 1 + dist, 1.0, sel)
        sel_d = jnp.where((lane % 8 == head) & (lane >= 24) & (lane < 48), -1.0, 0.0)
        mine = half == h
        zero = jnp.zeros_like(kp)
        km.append(jnp.where(mine, kp, zero))
        vm = jnp.where(mine, vp, zero)
        qm.append(jnp.where(mine, qp, zero))
        dm.append(jnp.where(mine, dop, zero))
        s = dot(jnp.concatenate([km[h], jnp.broadcast_to(sel, kp.shape).astype(bf16)], 1), qa, 1, 1)
        dp = dot(jnp.concatenate([vm, jnp.broadcast_to(sel_d, kp.shape).astype(bf16)], 1), da, 1, 1)
        p = jnp.exp2(s * EXP_SCALE)
        if rank_row is not None:
            p = jnp.where(rank_row >= rank_col, p, 0.0)
        pb.append(p.astype(bf16))
        db.append((p * dp).astype(bf16))
    dv = dot(jnp.concatenate(pb, 1), jnp.concatenate(dm, 0), 1, 0)
    dk = dot(jnp.concatenate(db, 1), jnp.concatenate(qm, 0), 1, 0)
    dq = dot(jnp.concatenate(db, 0), jnp.concatenate(km, 0), 0, 0)
    return dq, dk, dv


def pairs(body):
    def step(hp, _):
        body(hp, pl.ds(pl.multiple_of(hp * PAIR, PAIR), PAIR), pl.ds(pl.multiple_of(WC + hp * PAIR, PAIR), PAIR))
        return 0

    lax.fori_loop(0, HC // 2, step, 0)


def diag_kernel(c, q, aux, kv, rank_row, rank_col, dq, dkv):
    def body(hp, at, at2):
        x, y, z = tile(q, aux[...], kv, c, hp, None, rank_row[...], rank_col[...])
        dq[:, at] = x
        dkv[:, at] = y
        dkv[:, at2] = z

    pairs(body)


def cross_kernel(c, odd, q0, a0, q1, a1, k0, k1, dq, dkv, *refs):
    before, (dq_out, dkv_out, dq1, dkv1) = refs[:-4], refs[-4:]
    near = jnp.where(odd[0] == 0, 3, 1)
    base = 0
    for part in before:
        dq1[:, base : base + WC] = part[...]
        base += WC

    def body(hp, at, at2):
        x, y, z = tile(q0, a0[...], k1, c, hp, 2)
        dq_out[:, at] = dq[:, at] + x
        x, y2, z2 = tile(q1, a1[...], k1, c, hp, near)
        dkv1[:, at] = y + y2
        dkv1[:, at2] = z + z2
        to = pl.ds(pl.multiple_of(base + hp * PAIR, PAIR), PAIR)

        @pl.when(odd[0] == 0)
        def _():
            x3, y3, z3 = tile(q1, a1[...], k0, c, hp, 1)
            dq1[:, to] = ((x + x3) * 0.125).astype(bf16)
            dkv_out[:, at] = dkv[:, at] + y3
            dkv_out[:, at2] = dkv[:, at2] + z3

        @pl.when(odd[0] != 0)
        def _():
            dq1[:, to] = (x * 0.125).astype(bf16)
            dkv_out[:, at] = dkv[:, at]
            dkv_out[:, at2] = dkv[:, at2]

    pairs(body)


def last_kernel(c, odd, q2, a2, k1, dkv1, *refs):
    before, (dq2, out) = refs[:-2], refs[-2:]
    base = 0
    for part in before:
        dq2[:, base : base + WC] = part[...]
        base += WC

    def body(hp, at, at2):
        to = pl.ds(pl.multiple_of(base + hp * PAIR, PAIR), PAIR)

        @pl.when(odd[0] != 0)
        def _():
            x, y, z = tile(q2, a2[...], k1, c, hp, 3)
            dq2[:, to] = (x * 0.125).astype(bf16)
            out[:, at] = ((dkv1[:, at] + y) * 0.125).astype(bf16)
            out[:, at2] = (dkv1[:, at2] + z).astype(bf16)

        @pl.when(odd[0] == 0)
        def _():
            dq2[:, to] = jnp.zeros((dq2.shape[0], PAIR), bf16)
            out[:, at] = (dkv1[:, at] * 0.125).astype(bf16)
            out[:, at2] = dkv1[:, at2].astype(bf16)

    pairs(body)


def sum_kernel(*refs):
    dqs, dkvs, backs, (r1, r2, gq, gk, gv) = refs[:CHUNKS], refs[CHUNKS : 2 * CHUNKS], refs[2 * CHUNKS : 3 * CHUNKS], refs[3 * CHUNKS :]
    for c in range(CHUNKS):
        w = slice(c * WC, (c + 1) * WC)
        gq[:, w] = (dqs[c][...] * 0.125 + r1[:, w].astype(f32) + r2[:, w].astype(f32)).astype(bf16)
        gk[:, w] = (dkvs[c][:, :WC] * 0.125 + backs[c][:, :WC].astype(f32)).astype(bf16)
        gv[:, w] = (dkvs[c][:, WC:] + backs[c][:, WC:].astype(f32)).astype(bf16)


VM = pl.BlockSpec(memory_space=pltpu.VMEM)
SM = pl.BlockSpec(memory_space=pltpu.SMEM)


def call(kernel, outs, n_smem, args, scratch=(), flops=0, n_far=0):
    near = len(args) - n_smem - n_far
    return pl.pallas_call(
        kernel,
        out_shape=outs,
        in_specs=[SM] * n_smem + [VM] * near + [pl.BlockSpec(memory_space=pltpu.HBM)] * n_far,
        out_specs=[VM] * len(outs),
        scratch_shapes=list(scratch),
        cost_estimate=pl.CostEstimate(flops=flops, bytes_accessed=4 << 20, transcendentals=0),
        compiler_params=pltpu.CompilerParams(vmem_limit_bytes=16 << 20),
    )(*args)


def per_device(query, keys, values, output, grad_output, log_sum_exp, order, layout):
    rows = query.shape[0]
    n = lax.axis_size(AXES)
    block = lax.axis_index(AXES)
    blk = jnp.reshape(block, (1,)).astype(jnp.int32)
    odd = blk % 2

    def arr(cols, kind):
        return jax.ShapeDtypeStruct((rows, cols), kind)

    def shifted(x, by, keep=lambda i: True):
        return lax.ppermute(x, AXES, [(i - by, i) for i in range(n) if 0 <= i - by < n and keep(i)])

    def swapped(x):
        return lax.ppermute(x, AXES, [(i ^ 1, i) for i in range(n)])

    tile_flops = COST * 5 * 2 * rows * rows * SIZE * HEADS
    qw = [2 * WC + (128 if c == 0 else 0) for c in range(CHUNKS)]
    packed = call(
        pack_kernel,
        [arr(w, bf16) for w in qw] + [arr(2 * WC, bf16)] * CHUNKS,
        2,
        (blk, layout, log_sum_exp, query, keys, values, output, grad_output),
        scratch=[pltpu.VMEM((rows, HEADS * SIZE), bf16)] * 5 + [pltpu.SemaphoreType.DMA((5,))],
        flops=1 << 20,
        n_far=5,
    )
    q0, k0 = packed[:CHUNKS], packed[CHUNKS:]
    k1, q1 = [], []
    for c in range(CHUNKS):
        q1.append(swapped(q0[c]))
        k1.append(shifted(k0[c], 2))
    q2 = [shifted(q1[c], -2, lambda i: i % 2 == 1) for c in range(CHUNKS)]
    if DIRECT:
        q2[-1] = lax.ppermute(q0[-1], AXES, [(i + 1, i) for i in range(1, n - 1, 2)])
    rank_row, rank_col = order, jnp.reshape(order, (rows, 1))
    a0, a1, a2 = (x[0][:, 2 * WC :] for x in (q0, q1, q2))
    dqs, dkvs, back_kv, dq1, dq2 = [], [], [], (), ()
    for c in range(CHUNKS):
        dq, dkv = call(
            functools.partial(diag_kernel, c),
            [arr(WC, f32), arr(2 * WC, f32)],
            0,
            (q0[c], a0, k0[c], rank_row, rank_col),
            flops=tile_flops // CHUNKS,
        )
        dq, dkv, x, dkv1 = call(
            functools.partial(cross_kernel, c),
            [arr(WC, f32), arr(2 * WC, f32), arr((c + 1) * WC, bf16), arr(2 * WC, f32)],
            1,
            (odd, q0[c], a0, q1[c], a1, k0[c], k1[c], dq, dkv, *dq1),
            flops=3 * tile_flops // CHUNKS,
        )
        dq1 = (x,)
        dqs.append(dq)
        dkvs.append(dkv)
        x, send = call(
            functools.partial(last_kernel, c),
            [arr((c + 1) * WC, bf16), arr(2 * WC, bf16)],
            1,
            (odd, q2[c], a2, k1[c], dkv1, *dq2),
            flops=tile_flops // CHUNKS,
        )
        dq2 = (x,)
        back_kv.append(shifted(send, -2))
    back_q1 = swapped(dq1[0])
    back_q2 = lax.ppermute(dq2[0], AXES, [(i, i + 1) for i in range(1, n - 1, 2)])
    return tuple(
        call(sum_kernel, [arr(HEADS * SIZE, bf16)] * 3, 0, (*dqs, *dkvs, *back_kv, back_q1, back_q2), flops=1 << 20)
    )


def solution(mesh):
    rows = P(AXES, None)
    return jax.shard_map(
        per_device,
        mesh=mesh,
        in_specs=(rows, rows, rows, rows, rows, P(None, AXES), rows, rows),
        out_specs=(rows, rows, rows),
        check_vma=False,
    )
```

time: 221 us -> 105 us (0.48)
  the two profiles are of different devices: /device:TPU:47 before, /device:TPU:40 now
where the time goes in v1:
time: 105 us; the launch traced here: 104 us
  starting transfers between devices  57.7 us (55%)
  Pallas kernels  24.7 us (24%)
  waiting for transfers between devices  14.2 us (14%)
  local copies, waits for them, and re-layouts  6.5 us (6%)
    ppermute x6, starting transfers between devices, shifted(): lax.ppermute(x, AXES, [(i - by, i) for i in range(n) if 0 <= i - by < n a...  48.4 us
    pallas_call x8, Pallas kernels, call(): pl.pallas_call(kernel, out_shape=outs, in_specs=[SM] * n_smem + [VM] * ne...  24.7 us
    ppermute x3, starting transfers between devices, swapped(): return lax.ppermute(x, AXES, [(i ^ 1, i) for i in range(n)])  7.94 us
    ppermute x6, waiting for transfers between devices, shifted(): lax.ppermute(x, AXES, [(i - by, i) for i in range(n) if 0 <= i - by < n a...  7.65 us
    unnamed x16, local copies, waits for them, and re-layouts  6.34 us
    ppermute x1, waiting for transfers between devices, per_device(): lax.ppermute(dq2[0], AXES, [(i, i + 1) for i in range(1, n - 1, 2)])  4.21 us
    ppermute x3, waiting for transfers between devices, swapped(): return lax.ppermute(x, AXES, [(i ^ 1, i) for i in range(n)])  2.37 us
  transfers between devices with their start and end apart: 10, of which 5 were waited for; matrix products, arithmetic and copies ran while one was open for 0% of the time, Pallas kernels for 20%

profile of v1, /device:TPU:40, one launch (start us, length us, event | category | flops | bytes accessed | tf_op | source)
XLA Modules:
  0.0 104.0 jit_solution(2053193807543559176)
XLA Ops:
  0.7 0.7 copy-done.5
  1.3 1.0 copy-done
  2.3 1.0 copy-done.1
  3.3 1.0 copy-done.2
  4.3 1.0 copy-done.3
  5.3 1.0 copy-done.4
  6.3 2.7 %shard_map.103 = (bf16[384,640]{1,0:T(8,128)(2,1)S(1)}, bf16[384,512]{1,0:T(8,128)(2,1)S(1)}, bf16[384,512]{1,0:T(8,128)(2,1)}, bf16[384,512]{1,0:T(8,128)(2,1)S(1)}) custom-call(s32[1]{0:T(128)} %bitcast.blk, s32[1,3]{1,0:T(1,128)S(1)} %copy-done.7, f32[8,384]{1,0:T(8,128)S(1)} %copy-done.5, bf16[384,512]{1,0:T(8,128)(2,1)S(1)} %copy-done, ...), custom_call_target="tpu_custom_call" | custom-call | flops 1048576 | bytes 4194304 | tf_op jit(solution)/shard_map/pallas_call | solution.py:205
  9.1 3.3 %collective-permute-start = (bf16[384,640]{1,0:T(8,128)(2,1)S(1)}, bf16[384,640]{1,0:T(8,128)(2,1)S(1)}, u32[]{:S(2)}, u32[]{:S(2)}) collective-permute-start(bf16[384,640]{1,0:T(8,128)(2,1)S(1)} %get-tuple-element.23.q.q0), channel_id=1, source_target_pairs={{1,0},{0,1},{3,2},{2,3},{5,4},{4,5},{7,6},{6,7},{9,8},{8,9},{11,10... | collective-permute-start | bytes 1474568 | tf_op jit(solution)/shard_map/ppermute | solution.py:230
  12.3 4.3 %collective-permute-start.1 = (bf16[384,512]{1,0:T(8,128)(2,1)}, bf16[384,512]{1,0:T(8,128)(2,1)S(1)}, u32[]{:S(2)}, u32[]{:S(2)}) collective-permute-start(bf16[384,512]{1,0:T(8,128)(2,1)} %get-tuple-element.24.kv.k0), channel_id=1, source_target_pairs={{0,2},{1,3},{2,4},{3,5},{4,6},{5,7},{6,8},{7,9},{8,10},{9,11},{10,... | collective-permute-start | bytes 1179656 | tf_op jit(solution)/shard_map/ppermute | solution.py:227
  16.6 2.6 %collective-permute-start.2 = (bf16[384,512]{1,0:T(8,128)(2,1)S(1)}, bf16[384,512]{1,0:T(8,128)(2,1)S(1)}, u32[]{:S(2)}, u32[]{:S(2)}) collective-permute-start(bf16[384,512]{1,0:T(8,128)(2,1)S(1)} %get-tuple-element.28.q.q0), channel_id=1, source_target_pairs={{1,0},{0,1},{3,2},{2,3},{5,4},{4,5},{7,6},{6,7},{9,8},{8,9},{11,10... | collective-permute-start | bytes 1179656 | tf_op jit(solution)/shard_map/ppermute | solution.py:230
  19.2 4.3 %collective-permute-start.3 = (bf16[384,512]{1,0:T(8,128)(2,1)S(1)}, bf16[384,512]{1,0:T(8,128)(2,1)S(1)}, u32[]{:S(2)}, u32[]{:S(2)}) collective-permute-start(bf16[384,512]{1,0:T(8,128)(2,1)S(1)} %get-tuple-element.29.kv.k0), channel_id=1, source_target_pairs={{0,2},{1,3},{2,4},{3,5},{4,6},{5,7},{6,8},{7,9},{8,10},{9,11},{10,... | collective-permute-start | bytes 1179656 | tf_op jit(solution)/shard_map/ppermute | solution.py:227
  23.5 0.0 copy-start.6
  23.5 0.7 copy-done.6
  24.2 0.1 copy.11.rank_col
  24.3 3.3 %shard_map.104 = (f32[384,256]{1,0:T(8,128)S(1)}, f32[384,512]{1,0:T(8,128)S(1)}) custom-call(bf16[384,640]{1,0:T(8,128)(2,1)S(1)} %get-tuple-element.23.q.q0, bf16[384,128]{1,0:T(8,128)(2,1)S(1)} %slice.9.aux.a0, bf16[384,512]{1,0:T(8,128)(2,1)} %get-tuple-element.24.kv.k0, s32[1,384]{1,0:T(1,128)S(1)} %copy-done.6, s32[384,1]{1,0:T(8,128)S(1)} %copy.11.rank_col), custom_call_target="tpu_custom_call" | custom-call | flops 3019898880 | bytes 4194304 | tf_op jit(solution)/shard_map/pallas_call | solution.py:205
  27.7 2.3 %shard_map.106 = (f32[384,256]{1,0:T(8,128)S(1)}, f32[384,512]{1,0:T(8,128)S(1)}) custom-call(bf16[384,512]{1,0:T(8,128)(2,1)S(1)} %get-tuple-element.28.q.q0, bf16[384,128]{1,0:T(8,128)(2,1)S(1)} %slice.9.aux.a0, bf16[384,512]{1,0:T(8,128)(2,1)S(1)} %get-tuple-element.29.kv.k0, s32[1,384]{1,0:T(1,128)S(1)} %copy-done.6, s32[384,1]{1,0:T(8,128)S(1)} %copy.11.rank_col), custom_call_target="tpu_custom_call" | custom-call | flops 3019898880 | bytes 4194304 | tf_op jit(solution)/shard_map/pallas_call | solution.py:205
  30.0 2.4 %collective-permute-done.2.q1 = bf16[384,512]{1,0:T(8,128)(2,1)S(1)} collective-permute-done((bf16[384,512]{1,0:T(8,128)(2,1)S(1)}, bf16[384,512]{1,0:T(8,128)(2,1)S(1)}, u32[]{:S(2)}, u32[]{:S(2)}) %collective-permute-start.2) | collective-permute-done | bytes 393248 | tf_op jit(solution)/shard_map/ppermute | solution.py:230
  32.3 25.9 %collective-permute-start.6 = (bf16[384,512]{1,0:T(8,128)(2,1)S(1)}, bf16[384,512]{1,0:T(8,128)(2,1)S(1)}, u32[]{:S(2)}, u32[]{:S(2)}) collective-permute-start(bf16[384,512]{1,0:T(8,128)(2,1)S(1)} %collective-permute-done.2.q1), channel_id=1, source_target_pairs={{3,1},{5,3},{7,5},{9,7},{11,9},{13,11},{15,13},{17,15},{19,17},{21... | collective-permute-start | bytes 1179656 | tf_op jit(solution)/shard_map/ppermute | solution.py:227
  58.2 1.9 %collective-permute-start.4 = (bf16[384,640]{1,0:T(8,128)(2,1)S(1)}, bf16[384,640]{1,0:T(8,128)(2,1)S(1)}, u32[]{:S(2)}, u32[]{:S(2)}) collective-permute-start(bf16[384,640]{1,0:T(8,128)(2,1)S(1)} %collective-permute-done.q1), channel_id=1, source_target_pairs={{3,1},{5,3},{7,5},{9,7},{11,9},{13,11},{15,13},{17,15},{19,17},{21... | collective-permute-start | bytes 1474568 | tf_op jit(solution)/shard_map/ppermute | solution.py:227
  60.2 5.6 %shard_map.105 = (f32[384,256]{1,0:T(8,128)S(1)}, f32[384,512]{1,0:T(8,128)S(1)}, bf16[384,256]{1,0:T(8,128)(2,1)S(1)}, f32[384,512]{1,0:T(8,128)S(1)}) custom-call(s32[1]{0:T(128)S(6)} %select_n.7.odd, bf16[384,640]{1,0:T(8,128)(2,1)S(1)} %get-tuple-element.23.q.q0, bf16[384,128]{1,0:T(8,128)(2,1)S(1)} %slice.9.aux.a0, ...), custom_call_target="tpu_custom_call" | custom-call | flops 9059696640 | bytes 4194304 | tf_op jit(solution)/shard_map/pallas_call | solution.py:205
  65.9 4.7 %shard_map.107 = (f32[384,256]{1,0:T(8,128)S(1)}, f32[384,512]{1,0:T(8,128)S(1)}, bf16[384,512]{1,0:T(8,128)(2,1)S(1)}, f32[384,512]{1,0:T(8,128)S(1)}) custom-call(s32[1]{0:T(128)S(6)} %select_n.7.odd, bf16[384,512]{1,0:T(8,128)(2,1)S(1)} %get-tuple-element.28.q.q0, bf16[384,128]{1,0:T(8,128)(2,1)S(1)} %slice.9.aux.a0, ...), custom_call_target="tpu_custom_call" | custom-call | flops 9059696640 | bytes 4194304 | tf_op jit(solution)/shard_map/pallas_call | solution.py:205
  70.5 2.1 %collective-permute-start.8 = (bf16[384,512]{1,0:T(8,128)(2,1)S(1)}, bf16[384,512]{1,0:T(8,128)(2,1)S(1)}, u32[]{:S(2)}, u32[]{:S(2)}) collective-permute-start(bf16[384,512]{1,0:T(8,128)(2,1)S(1)} %get-tuple-element.41), channel_id=1, source_target_pairs={{1,0},{0,1},{3,2},{2,3},{5,4},{4,5},{7,6},{6,7},{9,8},{8,9},{11,10... | collective-permute-start | bytes 1179656 | tf_op jit(solution)/shard_map/ppermute | solution.py:230
  72.6 1.4 %collective-permute-done.4.q2 = bf16[384,640]{1,0:T(8,128)(2,1)S(1)} collective-permute-done((bf16[384,640]{1,0:T(8,128)(2,1)S(1)}, bf16[384,640]{1,0:T(8,128)(2,1)S(1)}, u32[]{:S(2)}, u32[]{:S(2)}) %collective-permute-start.4) | collective-permute-done | bytes 491552 | tf_op jit(solution)/shard_map/ppermute | solution.py:227
  74.1 2.4 %shard_map.108 = (bf16[384,256]{1,0:T(8,128)(2,1)S(1)}, bf16[384,512]{1,0:T(8,128)(2,1)S(1)}) custom-call(s32[1]{0:T(128)S(6)} %select_n.7.odd, bf16[384,640]{1,0:T(8,128)(2,1)S(1)} %collective-permute-done.4.q2, bf16[384,128]{1,0:T(8,128)(2,1)S(1)} %slice.13.a2, bf16[384,512]{1,0:T(8,128)(2,1)S(1)} %collective-permute-done.1.k1, ...), custom_call_target="tpu_custom_call" | custom-call | flops 3019898880 | bytes 4194304 | tf_op jit(solution)/shard_map/pallas_call | solution.py:205
  76.5 2.4 %shard_map.109 = (bf16[384,512]{1,0:T(8,128)(2,1)S(1)}, bf16[384,512]{1,0:T(8,128)(2,1)S(1)}) custom-call(s32[1]{0:T(128)S(6)} %select_n.7.odd, bf16[384,512]{1,0:T(8,128)(2,1)S(1)} %collective-permute-done.6.q2, bf16[384,128]{1,0:T(8,128)(2,1)S(1)} %slice.13.a2, bf16[384,512]{1,0:T(8,128)(2,1)S(1)} %collective-permute-done.3.k1, ...), custom_call_target="tpu_custom_call" | custom-call | flops 3019898880 | bytes 4194304 | tf_op jit(solution)/shard_map/pallas_call | solution.py:205
  78.9 10.2 %collective-permute-start.7 = (bf16[384,512]{1,0:T(8,128)(2,1)S(1)}, bf16[384,512]{1,0:T(8,128)(2,1)S(1)}, u32[]{:S(2)}, u32[]{:S(2)}) collective-permute-start(bf16[384,512]{1,0:T(8,128)(2,1)S(1)} %get-tuple-element.40), channel_id=1, source_target_pairs={{2,0},{3,1},{4,2},{5,3},{6,4},{7,5},{8,6},{9,7},{10,8},{11,9},{12,... | collective-permute-start | bytes 1179656 | tf_op jit(solution)/shard_map/ppermute | solution.py:227
  89.0 1.3 %collective-permute-start.9 = (bf16[384,512]{1,0:T(8,128)(2,1)S(1)}, bf16[384,512]{1,0:T(8,128)(2,1)S(1)}, u32[]{:S(2)}, u32[]{:S(2)}) collective-permute-start(bf16[384,512]{1,0:T(8,128)(2,1)S(1)} %get-tuple-element.42), channel_id=1, source_target_pairs={{1,2},{3,4},{5,6},{7,8},{9,10},{11,12},{13,14},{15,16},{17,18},{19... | collective-permute-start | bytes 1179656 | tf_op jit(solution)/shard_map/ppermute | solution.py:282
  90.4 1.9 %collective-permute-start.5 = (bf16[384,512]{1,0:T(8,128)(2,1)S(1)}, bf16[384,512]{1,0:T(8,128)(2,1)S(1)}, u32[]{:S(2)}, u32[]{:S(2)}) collective-permute-start(bf16[384,512]{1,0:T(8,128)(2,1)S(1)} %get-tuple-element.37), channel_id=1, source_target_pairs={{2,0},{3,1},{4,2},{5,3},{6,4},{7,5},{8,6},{9,7},{10,8},{11,9},{12,... | collective-permute-start | bytes 1179656 | tf_op jit(solution)/shard_map/ppermute | solution.py:227
  92.3 2.0 %collective-permute-done.7.refs_5_ = bf16[384,512]{1,0:T(8,128)(2,1)S(1)} collective-permute-done((bf16[384,512]{1,0:T(8,128)(2,1)S(1)}, bf16[384,512]{1,0:T(8,128)(2,1)S(1)}, u32[]{:S(2)}, u32[]{:S(2)}) %collective-permute-start.7) | collective-permute-done | bytes 393248 | tf_op jit(solution)/shard_map/ppermute | solution.py:227
  94.3 4.2 %collective-permute-done.9.refs_7_ = bf16[384,512]{1,0:T(8,128)(2,1)S(1)} collective-permute-done((bf16[384,512]{1,0:T(8,128)(2,1)S(1)}, bf16[384,512]{1,0:T(8,128)(2,1)S(1)}, u32[]{:S(2)}, u32[]{:S(2)}) %collective-permute-start.9) | collective-permute-done | bytes 393248 | tf_op jit(solution)/shard_map/ppermute | solution.py:282
  98.5 4.2 %collective-permute-done.5.refs_4_ = bf16[384,512]{1,0:T(8,128)(2,1)S(1)} collective-permute-done((bf16[384,512]{1,0:T(8,128)(2,1)S(1)}, bf16[384,512]{1,0:T(8,128)(2,1)S(1)}, u32[]{:S(2)}, u32[]{:S(2)}) %collective-permute-start.5) | collective-permute-done | bytes 393248 | tf_op jit(solution)/shard_map/ppermute | solution.py:227
  102.7 1.2 %shard_map.110 = (bf16[384,512]{1,0:T(8,128)(2,1)}, bf16[384,512]{1,0:T(8,128)(2,1)}, bf16[384,512]{1,0:T(8,128)(2,1)}) custom-call(f32[384,256]{1,0:T(8,128)S(1)} %get-tuple-element.27.refs_0_, f32[384,256]{1,0:T(8,128)S(1)} %get-tuple-element.33.refs_1_, f32[384,512]{1,0:T(8,128)S(1)} %get-tuple-element.34.refs_2_, ...), custom_call_target="tpu_custom_call" | custom-call | flops 1048576 | bytes 4194304 | tf_op jit(solution)/shard_map/pallas_call | solution.py:205
  (16 shorter events, 0.1 us)
Async XLA Ops:
  0.6 0.7 copy-start.5
  0.6 0.7 copy-start.7
  1.3 1.0 copy-start
  2.3 1.0 copy-start.1
  3.3 1.0 copy-start.2
  4.3 1.0 copy-start.3
  5.3 1.0 copy-start.4
  9.1 49.2 %collective-permute-start = (bf16[384,640]{1,0:T(8,128)(2,1)S(1)}, bf16[384,640]{1,0:T(8,128)(2,1)S(1)}, u32[]{:S(2)}, u32[]{:S(2)}) collective-permute-start(bf16[384,640]{1,0:T(8,128)(2,1)S(1)} %get-tuple-element.23.q.q0), channel_id=1, source_target_pairs={{1,0},{0,1},{3,2},{2,3},{5,4},{4,5},{7,6},{6,7},{9,8},{8,9},{11,10... | collective-permute-start | bytes 1474568 | tf_op jit(solution)/shard_map/ppermute | solution.py:230
  12.3 47.8 %collective-permute-start.1 = (bf16[384,512]{1,0:T(8,128)(2,1)}, bf16[384,512]{1,0:T(8,128)(2,1)S(1)}, u32[]{:S(2)}, u32[]{:S(2)}) collective-permute-start(bf16[384,512]{1,0:T(8,128)(2,1)} %get-tuple-element.24.kv.k0), channel_id=1, source_target_pairs={{0,2},{1,3},{2,4},{3,5},{4,6},{5,7},{6,8},{7,9},{8,10},{9,11},{10,... | collective-permute-start | bytes 1179656 | tf_op jit(solution)/shard_map/ppermute | solution.py:227
  16.6 15.7 %collective-permute-start.2 = (bf16[384,512]{1,0:T(8,128)(2,1)S(1)}, bf16[384,512]{1,0:T(8,128)(2,1)S(1)}, u32[]{:S(2)}, u32[]{:S(2)}) collective-permute-start(bf16[384,512]{1,0:T(8,128)(2,1)S(1)} %get-tuple-element.28.q.q0), channel_id=1, source_target_pairs={{1,0},{0,1},{3,2},{2,3},{5,4},{4,5},{7,6},{6,7},{9,8},{8,9},{11,10... | collective-permute-start | bytes 1179656 | tf_op jit(solution)/shard_map/ppermute | solution.py:230
  19.2 46.6 %collective-permute-start.3 = (bf16[384,512]{1,0:T(8,128)(2,1)S(1)}, bf16[384,512]{1,0:T(8,128)(2,1)S(1)}, u32[]{:S(2)}, u32[]{:S(2)}) collective-permute-start(bf16[384,512]{1,0:T(8,128)(2,1)S(1)} %get-tuple-element.29.kv.k0), channel_id=1, source_target_pairs={{0,2},{1,3},{2,4},{3,5},{4,6},{5,7},{6,8},{7,9},{8,10},{9,11},{10,... | collective-permute-start | bytes 1179656 | tf_op jit(solution)/shard_map/ppermute | solution.py:227
  23.5 0.7 copy-start.6
  32.3 44.1 %collective-permute-start.6 = (bf16[384,512]{1,0:T(8,128)(2,1)S(1)}, bf16[384,512]{1,0:T(8,128)(2,1)S(1)}, u32[]{:S(2)}, u32[]{:S(2)}) collective-permute-start(bf16[384,512]{1,0:T(8,128)(2,1)S(1)} %collective-permute-done.2.q1), channel_id=1, source_target_pairs={{3,1},{5,3},{7,5},{9,7},{11,9},{13,11},{15,13},{17,15},{19,17},{21... | collective-permute-start | bytes 1179656 | tf_op jit(solution)/shard_map/ppermute | solution.py:227
  58.2 15.8 %collective-permute-start.4 = (bf16[384,640]{1,0:T(8,128)(2,1)S(1)}, bf16[384,640]{1,0:T(8,128)(2,1)S(1)}, u32[]{:S(2)}, u32[]{:S(2)}) collective-permute-start(bf16[384,640]{1,0:T(8,128)(2,1)S(1)} %collective-permute-done.q1), channel_id=1, source_target_pairs={{3,1},{5,3},{7,5},{9,7},{11,9},{13,11},{15,13},{17,15},{19,17},{21... | collective-permute-start | bytes 1474568 | tf_op jit(solution)/shard_map/ppermute | solution.py:227
  70.5 21.8 %collective-permute-start.8 = (bf16[384,512]{1,0:T(8,128)(2,1)S(1)}, bf16[384,512]{1,0:T(8,128)(2,1)S(1)}, u32[]{:S(2)}, u32[]{:S(2)}) collective-permute-start(bf16[384,512]{1,0:T(8,128)(2,1)S(1)} %get-tuple-element.41), channel_id=1, source_target_pairs={{1,0},{0,1},{3,2},{2,3},{5,4},{4,5},{7,6},{6,7},{9,8},{8,9},{11,10... | collective-permute-start | bytes 1179656 | tf_op jit(solution)/shard_map/ppermute | solution.py:230
  78.9 15.4 %collective-permute-start.7 = (bf16[384,512]{1,0:T(8,128)(2,1)S(1)}, bf16[384,512]{1,0:T(8,128)(2,1)S(1)}, u32[]{:S(2)}, u32[]{:S(2)}) collective-permute-start(bf16[384,512]{1,0:T(8,128)(2,1)S(1)} %get-tuple-element.40), channel_id=1, source_target_pairs={{2,0},{3,1},{4,2},{5,3},{6,4},{7,5},{8,6},{9,7},{10,8},{11,9},{12,... | collective-permute-start | bytes 1179656 | tf_op jit(solution)/shard_map/ppermute | solution.py:227
  89.0 9.5 %collective-permute-start.9 = (bf16[384,512]{1,0:T(8,128)(2,1)S(1)}, bf16[384,512]{1,0:T(8,128)(2,1)S(1)}, u32[]{:S(2)}, u32[]{:S(2)}) collective-permute-start(bf16[384,512]{1,0:T(8,128)(2,1)S(1)} %get-tuple-element.42), channel_id=1, source_target_pairs={{1,2},{3,4},{5,6},{7,8},{9,10},{11,12},{13,14},{15,16},{17,18},{19... | collective-permute-start | bytes 1179656 | tf_op jit(solution)/shard_map/ppermute | solution.py:282
  90.4 12.4 %collective-permute-start.5 = (bf16[384,512]{1,0:T(8,128)(2,1)S(1)}, bf16[384,512]{1,0:T(8,128)(2,1)S(1)}, u32[]{:S(2)}, u32[]{:S(2)}) collective-permute-start(bf16[384,512]{1,0:T(8,128)(2,1)S(1)} %get-tuple-element.37), channel_id=1, source_target_pairs={{2,0},{3,1},{4,2},{5,3},{6,4},{7,5},{8,6},{9,7},{10,8},{11,9},{12,... | collective-permute-start | bytes 1179656 | tf_op jit(solution)/shard_map/ppermute | solution.py:227

commit v2 on v1

v2 whole, which is shorter than its diff:
```python
import functools
import math

import jax
import jax.numpy as jnp
from jax import lax
from jax.experimental import pallas as pl
from jax.experimental.pallas import tpu as pltpu
from jax.sharding import PartitionSpec as P

AXES = ("inner", "outer")
HEADS = 8
SIZE = 64
PAIR = 2 * SIZE
CHUNKS = 2
COST = 8
SPAN = 128
HC = HEADS // CHUNKS
WC = HC * SIZE
EXP_SCALE = 0.125 / math.log(2.0)
HIDDEN = -1e30
f32 = jnp.float32
bf16 = jnp.bfloat16

VIS = 48


def dot(a, b, ca, cb):
    return lax.dot_general(a, b, (((ca,), (cb,)), ((), ())), preferred_element_type=f32)


def pieces(x):
    a = x.astype(bf16)
    r = x - a.astype(f32)
    b = r.astype(bf16)
    c = (r - b.astype(f32)).astype(bf16)
    return a, b, c


def pack_q(blk, layout, lse, order, everything, *outs):
    q, do, o = (everything.at[:, i * HEADS * SIZE : (i + 1) * HEADS * SIZE] for i in range(3))
    qs, rank = outs[:CHUNKS], outs[CHUNKS]
    rows = q.shape[0]
    for c in range(CHUNKS):
        w = slice(c * WC, (c + 1) * WC)
        qs[c][:, :WC] = q[:, w]
        qs[c][:, WC : 2 * WC] = do[:, w]
    lane = lax.broadcasted_iota(jnp.int32, (1, 128), 1)
    prod = do[...].astype(f32) * o[...].astype(f32)
    hi = prod.astype(bf16)
    lo = (prod - hi.astype(f32)).astype(bf16)
    feat = lax.broadcasted_iota(jnp.int32, (HEADS * SIZE, 128), 0) // SIZE
    flane = lax.broadcasted_iota(jnp.int32, (HEADS * SIZE, 128), 1)
    pick = jnp.where((flane % 8 == feat) & (flane >= 24) & (flane < 48), 1.0, 0.0).astype(bf16)
    delta = dot(hi, pick, 1, 0) + dot(lo, pick, 1, 0)
    d1, d2, d3 = (x.astype(f32) for x in pieces(delta))
    dpart = jnp.where(lane < 32, d1, jnp.where(lane < 40, d2, d3))
    l1, l2, l3 = (x.astype(f32) for x in pieces(lse[...] * 8.0))
    stack = jnp.concatenate([l1, l2, l3, jnp.zeros_like(l1)], 0).astype(bf16)
    r = lax.broadcasted_iota(jnp.int32, (32, 128), 0)
    c = lax.broadcasted_iota(jnp.int32, (32, 128), 1)
    eye = jnp.where((r == c) & (r < 24), 1.0, 0.0).astype(bf16)
    lpart = dot(stack, eye, 0, 0)
    vis = jnp.zeros((1, 128), f32)
    for d in (1, 2, 3):
        seen = jnp.logical_and(layout[0, d - 1] > 0, blk[0] >= d)
        vis = jnp.where((lane == VIS + d - 1) & jnp.logical_not(seen), f32(HIDDEN), vis)
    aux = jnp.where(lane < 24, lpart, jnp.where(lane < 48, dpart, jnp.broadcast_to(vis, (rows, 128))))
    qs[0][:, 2 * WC :] = aux.astype(bf16)
    rank[...] = jnp.broadcast_to(order[...].astype(f32), rank.shape)


def tile(q, aux, kv, c, hp, dist, rank_row=None, rank_col=None):
    at = pl.ds(pl.multiple_of(hp * PAIR, PAIR), PAIR)
    at2 = pl.ds(pl.multiple_of(WC + hp * PAIR, PAIR), PAIR)
    at_k = pl.ds(pl.multiple_of(c * WC + hp * PAIR, PAIR), PAIR)
    at_v = pl.ds(pl.multiple_of((CHUNKS + c) * WC + hp * PAIR, PAIR), PAIR)
    qp, dop, kp, vp = q[:, at], q[:, at2], kv[:, at_k], kv[:, at_v]
    lane = lax.broadcasted_iota(jnp.int32, (1, PAIR), 1)
    half = lax.broadcasted_iota(jnp.int32, qp.shape, 1) // SIZE
    qa = jnp.concatenate([qp, aux], 1)
    da = jnp.concatenate([dop, aux], 1)
    km, qm, dm, pb, db = [], [], [], [], []
    for h in range(2):
        head = c * HC + hp * 2 + h
        sel = jnp.where((lane % 8 == head) & (lane < 24), -1.0, 0.0)
        if dist is not None:
            sel = jnp.where(lane == VIS - 1 + dist, 1.0, sel)
        sel_d = jnp.where((lane % 8 == head) & (lane >= 24) & (lane < 48), -1.0, 0.0)
        mine = half == h
        zero = jnp.zeros_like(kp)
        km.append(jnp.where(mine, kp, zero))
        vm = jnp.where(mine, vp, zero)
        qm.append(jnp.where(mine, qp, zero))
        dm.append(jnp.where(mine, dop, zero))
        s = dot(jnp.concatenate([km[h], jnp.broadcast_to(sel, kp.shape).astype(bf16)], 1), qa, 1, 1)
        dp = dot(jnp.concatenate([vm, jnp.broadcast_to(sel_d, kp.shape).astype(bf16)], 1), da, 1, 1)
        p = jnp.exp2(s * EXP_SCALE)
        if rank_row is not None:
            p = jnp.where(rank_row >= rank_col, p, 0.0)
        pb.append(p.astype(bf16))
        db.append((p * dp).astype(bf16))
    dv = dot(jnp.concatenate(pb, 1), jnp.concatenate(dm, 0), 1, 0)
    dk = dot(jnp.concatenate(db, 1), jnp.concatenate(qm, 0), 1, 0)
    dq = dot(jnp.concatenate(db, 0), jnp.concatenate(km, 0), 0, 0)
    return dq, dk, dv


def pairs(body):
    def step(hp, _):
        body(hp, pl.ds(pl.multiple_of(hp * PAIR, PAIR), PAIR), pl.ds(pl.multiple_of(WC + hp * PAIR, PAIR), PAIR))
        return 0

    lax.fori_loop(0, HC // 2, step, 0)


def diag_kernel(c, q, qa, kv, rank, dq, dkv):
    rank_col = jnp.broadcast_to(rank[:1], (128, rank.shape[1])).T[:, :1]

    def body(hp, at, at2):
        x, y, z = tile(q, qa[:, 2 * WC :], kv, c, hp, None, rank[:1], rank_col)
        dq[:, at] = x
        dkv[:, at] = y
        dkv[:, at2] = z

    pairs(body)


def cross_kernel(c, odd, q0, a0, q1, a1, k0, k1, dq, dkv, *refs):
    before, (dq_out, dkv_out, dq1, dkv1) = refs[:-4], refs[-4:]
    near = jnp.where(odd[0] & 1 == 0, 3, 1)

    base = 0
    for part in before:
        dq1[:, base : base + WC] = part[...]
        base += WC

    def body(hp, at, at2):
        x, y, z = tile(q0, a0[:, 2 * WC :], k1, c, hp, 2)
        dq_out[:, at] = dq[:, at] + x
        x, y2, z2 = tile(q1, a1[:, 2 * WC :], k1, c, hp, near)
        dkv1[:, at] = y + y2
        dkv1[:, at2] = z + z2
        to = pl.ds(pl.multiple_of(base + hp * PAIR, PAIR), PAIR)

        @pl.when(odd[0] & 1 == 0)
        def _():
            x3, y3, z3 = tile(q1, a1[:, 2 * WC :], k0, c, hp, 1)
            dq1[:, to] = ((x + x3) * 0.125).astype(bf16)
            dkv_out[:, at] = dkv[:, at] + y3
            dkv_out[:, at2] = dkv[:, at2] + z3

        @pl.when(odd[0] & 1 != 0)
        def _():
            dq1[:, to] = (x * 0.125).astype(bf16)
            dkv_out[:, at] = dkv[:, at]
            dkv_out[:, at2] = dkv[:, at2]

    pairs(body)


def last_kernel(c, odd, q2_far, a2_far, k1, edge, dkv1, *refs):
    before, (dq2, out, q2) = refs[:-3], refs[-3:]
    a2 = q2 if c == 0 else a2_far

    @pl.when(odd[0] & 8 != 0)
    def _():
        q2[...] = edge[...]


    base = 0
    for part in before:
        dq2[:, base : base + WC] = part[...]
        base += WC

    def body(hp, at, at2):
        to = pl.ds(pl.multiple_of(base + hp * PAIR, PAIR), PAIR)

        @pl.when(odd[0] & 1 != 0)
        def _():
            x, y, z = tile(q2, a2[:, 2 * WC :], k1, c, hp, 3)
            dq2[:, to] = (x * 0.125).astype(bf16)
            out[:, at] = ((dkv1[:, at] + y) * 0.125).astype(bf16)
            out[:, at2] = (dkv1[:, at2] + z).astype(bf16)

        @pl.when(odd[0] & 1 == 0)
        def _():
            dq2[:, to] = jnp.zeros((dq2.shape[0], PAIR), bf16)
            out[:, at] = (dkv1[:, at] * 0.125).astype(bf16)
            out[:, at2] = dkv1[:, at2].astype(bf16)

    pairs(body)


def first_sum(dq_a, dq_b, dkv, r1, r2, back, gq, gk, gv):
    far = r1[...].astype(f32) + r2[...].astype(f32)
    gq[:, :WC] = (dq_a[...] * 0.125 + far[:, :WC]).astype(bf16)
    gq[:, WC:] = (dq_b[...] * 0.125 + far[:, WC:]).astype(bf16)
    gk[...] = (dkv[:, :WC] * 0.125 + back[:, :WC].astype(f32)).astype(bf16)
    gv[...] = (dkv[:, WC:] + back[:, WC:].astype(f32)).astype(bf16)


def last_sum(pk, pv, dkv, back, gk, gv):
    gk[:, :WC] = pk[...]
    gv[:, :WC] = pv[...]
    gk[:, WC:] = (dkv[:, :WC] * 0.125 + back[:, :WC].astype(f32)).astype(bf16)
    gv[:, WC:] = (dkv[:, WC:] + back[:, WC:].astype(f32)).astype(bf16)


VM = pl.BlockSpec(memory_space=pltpu.VMEM)
SM = pl.BlockSpec(memory_space=pltpu.SMEM)


def call(kernel, outs, n_smem, args, scratch=(), flops=0, n_far=0, vmem=16, alias=None):
    near = len(args) - n_smem - n_far
    return pl.pallas_call(
        kernel,
        out_shape=outs,
        in_specs=[SM] * n_smem + [VM] * near + [pl.BlockSpec(memory_space=pltpu.HBM)] * n_far,
        out_specs=[VM] * len(outs),
        scratch_shapes=list(scratch),
        input_output_aliases=alias or {},
        cost_estimate=pl.CostEstimate(flops=flops, bytes_accessed=1 << 10, transcendentals=0),
        compiler_params=pltpu.CompilerParams(vmem_limit_bytes=vmem << 20),
    )(*args)


def per_device(query, keys, values, output, grad_output, log_sum_exp, order, layout):
    rows = query.shape[0]
    n = lax.axis_size(AXES)
    block = lax.axis_index(AXES)
    blk = jnp.reshape(block, (1,)).astype(jnp.int32)
    parity, place = block % 2, block % SPAN
    takes = jnp.where((place == SPAN - 1) & (block < n - 1), 8, 0)
    odd = jnp.reshape(parity + takes, (1,)).astype(jnp.int32)
    edges = range(SPAN, n, SPAN)

    def arr(cols, kind):
        return jax.ShapeDtypeStruct((rows, cols), kind)

    def shifted(x, by, keep=lambda i: True):
        return lax.ppermute(x, AXES, [(i - by, i) for i in range(n) if 0 <= i - by < n and keep(i)])

    def swapped(x):
        return lax.ppermute(x, AXES, [(i ^ 1, i) for i in range(n)])

    tile_flops = COST * 5 * 2 * rows * rows * SIZE * HEADS
    qw = [2 * WC + (128 if c == 0 else 0) for c in range(CHUNKS)]
    kv = jnp.concatenate([keys, values], 1)
    k1 = shifted(kv, 2)
    kv, query = lax.optimization_barrier((kv, query))
    *q0, rank = call(
        pack_q,
        [arr(w, bf16) for w in qw] + [jax.ShapeDtypeStruct((8, rows), f32)],
        2,
        (blk, layout, log_sum_exp, order, jnp.concatenate([query, grad_output, output], 1)),
    )
    q1 = [swapped(q0[c]) for c in range(CHUNKS)]
    edge = [lax.ppermute(q0[c], AXES, [(s, s - 1) for s in edges]) for c in range(CHUNKS)]
    a0 = q0[0]
    dqs, dkvs, back_kv, dq1, dq2, parts = [], [], [], (), (), []
    diag = []
    for c in range(CHUNKS):
        diag.append(
            call(
                functools.partial(diag_kernel, c),
                [arr(WC, f32), arr(2 * WC, f32)],
                0,
                (q0[c], a0, kv, rank),
                flops=tile_flops // CHUNKS,
            )
        )
    q1[0], diag = lax.optimization_barrier((q1[0], diag))
    q2 = [shifted(q1[0], -2, lambda i: i % 2 == 1 and i % SPAN != SPAN - 1)]
    a1 = q1[0]
    for c in range(CHUNKS):
        dq, dkv = diag[c]
        dq, dkv, x, dkv1 = call(
            functools.partial(cross_kernel, c),
            [arr(WC, f32), arr(2 * WC, f32), arr((c + 1) * WC, bf16), arr(2 * WC, f32)],
            1,
            (odd, q0[c], a0, q1[c], a1, kv, k1, dq, dkv, *dq1),
            flops=3 * tile_flops // CHUNKS,
        )
        dq1 = (x,)
        dqs.append(dq)
        dkvs.append(dkv)
        parts.append(dkv1)
        if c == 0:
            q1[1], dq1 = lax.optimization_barrier((q1[1], dq1))
            q2.append(shifted(q1[1], -2, lambda i: i % 2 == 1 and i % SPAN != SPAN - 1))
    back_q1 = swapped(dq1[0])
    q2[0], tail = lax.optimization_barrier((q2[0], dq1[0]))
    for c in range(CHUNKS):
        dkv1 = parts[c]
        x, send, q2[c] = call(
            functools.partial(last_kernel, c),
            [arr((c + 1) * WC, bf16), arr(2 * WC, bf16), arr(qw[c], bf16)],
            1,
            (odd, q2[c], q2[0], k1, edge[c], dkv1, *dq2),
            flops=0,
            alias={1: 2},
        )
        dq2 = (x,)
        back_kv.append(shifted(send, -2))
    back_q2 = lax.ppermute(dq2[0], AXES, [(i, i + 1) for i in range(1, n - 1, 2)])
    gq, pk, pv = call(
        first_sum,
        [arr(HEADS * SIZE, bf16), arr(WC, bf16), arr(WC, bf16)],
        0,
        (*dqs, dkvs[0], back_q1, back_q2, back_kv[0]),
        flops=20 << 30,
    )
    gk, gv = call(last_sum, [arr(HEADS * SIZE, bf16)] * 2, 0, (pk, pv, dkvs[1], back_kv[1]), flops=1 << 20)
    return gq, gk, gv


def solution(mesh):
    rows = P(AXES, None)
    return jax.shard_map(
        per_device,
        mesh=mesh,
        in_specs=(rows, rows, rows, rows, rows, P(None, AXES), rows, rows),
        out_specs=(rows, rows, rows),
        check_vma=False,
    )
```

time: 105 us -> 91.2 us (0.87)
  starting transfers between devices: 57.7 us -> 50 us
  local copies, waits for them, and re-layouts: 6.5 us -> 2.83 us
  waiting for transfers between devices: 14.2 us -> 12.2 us
    ppermute x6 -> x5, starting transfers between devices: 48.4 us -> 24 us  [shifted(): lax.ppermute(x, AXES, [(i - by, i) for i in range(n) if 0 <= i - by < n a...]
    ppermute x3, starting transfers between devices: 7.94 us -> 23.3 us  [swapped(): return lax.ppermute(x, AXES, [(i ^ 1, i) for i in range(n)])]
    unnamed x16 -> x14, local copies, waits for them, and re-layouts: 6.34 us -> 1.79 us
    ppermute x1, waiting for transfers between devices: 4.21 us -> 7.91 us  [per_device(): lax.ppermute(dq2[0], AXES, [(i, i + 1) for i in range(1, n - 1, 2)])]
    ppermute x6 -> x5, waiting for transfers between devices: 7.65 us -> 4.27 us  [shifted(): lax.ppermute(x, AXES, [(i - by, i) for i in range(n) if 0 <= i - by < n a...]
    ppermute x3, waiting for transfers between devices: 2.37 us -> 0.01 us  [swapped(): return lax.ppermute(x, AXES, [(i ^ 1, i) for i in range(n)])]
    ppermute x0 -> x2, starting transfers between devices: none -> 1.38 us  [per_device(): lax.ppermute(q0[c], AXES, [(s, s - 1) for s in edges])]
    pallas_call x8 -> x9, Pallas kernels: 24.7 us -> 24.7 us  [call(): pl.pallas_call(kernel, out_shape=outs, in_specs=[SM] * n_smem + [VM] * ne...]
  transfers between devices with their start and end apart: 10 -> 11, of which waited for: 5 -> 3; matrix products, arithmetic and copies ran while one was open for 0% -> 0% of each run, Pallas kernels for 20% -> 26%
where the time goes in v2:
time: 91.2 us; the launch traced here: 90.7 us
  starting transfers between devices  50 us (55%)
  Pallas kernels  24.7 us (27%)
  waiting for transfers between devices  12.2 us (13%)
  local copies, waits for them, and re-layouts  2.83 us (3%)
  between operations  0.97 us (1%)
    pallas_call x9, Pallas kernels, call(): pl.pallas_call(kernel, out_shape=outs, in_specs=[SM] * n_smem + [VM] * ne...  24.7 us
    ppermute x5, starting transfers between devices, shifted(): lax.ppermute(x, AXES, [(i - by, i) for i in range(n) if 0 <= i - by < n a...  24 us
    ppermute x3, starting transfers between devices, swapped(): return lax.ppermute(x, AXES, [(i ^ 1, i) for i in range(n)])  23.3 us
    ppermute x1, waiting for transfers between devices, per_device(): lax.ppermute(dq2[0], AXES, [(i, i + 1) for i in range(1, n - 1, 2)])  7.91 us
    ppermute x5, waiting for transfers between devices, shifted(): lax.ppermute(x, AXES, [(i - by, i) for i in range(n) if 0 <= i - by < n a...  4.27 us
  transfers between devices with their start and end apart: 11, of which 3 were waited for; matrix products, arithmetic and copies ran while one was open for 0% of the time, Pallas kernels for 26%

profile of v2, /device:TPU:40, one launch (start us, length us, event | category | flops | bytes accessed | tf_op | source)
XLA Modules:
  0.0 90.7 jit_solution(13243122860632271280)
XLA Ops:
  0.7 1.1 %constant_dynamic-update-slice_fusion.1 = bf16[384,1024]{1,0:T(8,128)(2,1)S(1)} fusion(bf16[384,512]{1,0:T(8,128)(2,1)} %param.9), kind=kLoop, calls=%fused_computation.2 | loop fusion | bytes 786432
  1.8 1.0 %constant_dynamic-update-slice_fusion.kv.k0 = bf16[384,1024]{1,0:T(8,128)(2,1)S(1)} fusion(bf16[384,1024]{1,0:T(8,128)(2,1)S(1)} %constant_dynamic-update-slice_fusion.1, bf16[384,512]{1,0:T(8,128)(2,1)} %param.10), kind=kLoop, calls=%fused_computation.1 | loop fusion | bytes 786432 | tf_op jit(solution)/shard_map/concatenate | solution.py:249
  2.8 4.3 %collective-permute-start.1 = (bf16[384,1024]{1,0:T(8,128)(2,1)S(1)}, bf16[384,1024]{1,0:T(8,128)(2,1)S(1)}, u32[]{:S(2)}, u32[]{:S(2)}) collective-permute-start(bf16[384,1024]{1,0:T(8,128)(2,1)S(1)} %constant_dynamic-update-slice_fusion.kv.k0), channel_id=1, source_target_pairs={{0,2},{1,3},{2,4},{3,5},{4,6},{5,7},{6,8},{7,9},{8,10},{9,11},{10,... | collective-permute-start | bytes 2359304 | tf_op jit(solution)/shard_map/ppermute | solution.py:242
  7.2 0.0 copy-start
  7.2 0.0 copy-start.1
  7.2 0.0 copy-start.2
  7.2 0.1 pad_maximum_fusion.everything
  7.3 0.6 copy-done
  7.9 1.7 %shard_map.103 = (bf16[384,640]{1,0:T(8,128)(2,1)S(1)}, bf16[384,512]{1,0:T(8,128)(2,1)}, f32[8,384]{1,0:T(8,128)S(1)}) custom-call(s32[1]{0:T(128)} %bitcast.1.blk, s32[1,3]{1,0:T(1,128)S(1)} %copy-done.2, f32[8,384]{1,0:T(8,128)S(1)} %copy-done, s32[1,384]{1,0:T(1,128)S(1)} %copy-done.1, bf16[384,1536]{1,0:T(8,128)(2,1)S(1)} %pad_maximum_fusion.everything), custom_call_target="tpu_custom_call" | custom-call | bytes 1024 | tf_op jit(solution)/shard_map/pallas_call | solution.py:216
  9.6 3.2 %collective-permute-start = (bf16[384,640]{1,0:T(8,128)(2,1)S(1)}, bf16[384,640]{1,0:T(8,128)(2,1)S(1)}, u32[]{:S(2)}, u32[]{:S(2)}) collective-permute-start(bf16[384,640]{1,0:T(8,128)(2,1)S(1)} %get-tuple-element.39.q.qa.q0.a0), channel_id=1, source_target_pairs={{1,0},{0,1},{3,2},{2,3},{5,4},{4,5},{7,6},{6,7},{9,8},{8,9},{11,10... | collective-permute-start | bytes 1474568 | tf_op jit(solution)/shard_map/ppermute | solution.py:245
  12.9 0.7 collective-permute-start.6
  13.6 11.5 %collective-permute-start.2 = (bf16[384,512]{1,0:T(8,128)(2,1)}, bf16[384,512]{1,0:T(8,128)(2,1)}, u32[]{:S(2)}, u32[]{:S(2)}) collective-permute-start(bf16[384,512]{1,0:T(8,128)(2,1)} %get-tuple-element.44.q.q0), channel_id=1, source_target_pairs={{1,0},{0,1},{3,2},{2,3},{5,4},{4,5},{7,6},{6,7},{9,8},{8,9},{11,10... | collective-permute-start | bytes 1179656 | tf_op jit(solution)/shard_map/ppermute | solution.py:245
  25.1 0.7 collective-permute-start.7
  25.8 3.4 %shard_map.105 = (f32[384,256]{1,0:T(8,128)S(1)}, f32[384,512]{1,0:T(8,128)S(1)}) custom-call(bf16[384,512]{1,0:T(8,128)(2,1)} %get-tuple-element.44.q.q0, bf16[384,640]{1,0:T(8,128)(2,1)S(1)} %get-tuple-element.39.q.qa.q0.a0, bf16[384,1024]{1,0:T(8,128)(2,1)S(1)} %constant_dynamic-update-slice_fusion.kv.k0, f32[8,384]{1,0:T(8,128)S(1)} %get-tuple-element.41.rank), custom_call_target="tpu_custom_call" | custom-call | flops 3019898880 | bytes 1024 | tf_op jit(solution)/shard_map/pallas_call | solution.py:216
  29.3 2.4 %shard_map.104 = (f32[384,256]{1,0:T(8,128)S(1)}, f32[384,512]{1,0:T(8,128)S(1)}) custom-call(bf16[384,640]{1,0:T(8,128)(2,1)S(1)} %get-tuple-element.39.q.qa.q0.a0, bf16[384,640]{1,0:T(8,128)(2,1)S(1)} %get-tuple-element.39.q.qa.q0.a0, bf16[384,1024]{1,0:T(8,128)(2,1)S(1)} %constant_dynamic-update-slice_fusion.kv.k0, f32[8,384]{1,0:T(8,128)S(1)} %get-tuple-element.41.rank), custom_call_target="tpu_custom_call" | custom-call | flops 3019898880 | bytes 1024 | tf_op jit(solution)/shard_map/pallas_call | solution.py:216
  31.7 1.3 %collective-permute-start.5 = (bf16[384,640]{1,0:T(8,128)(2,1)S(1)}, bf16[384,640]{1,0:T(8,128)(2,1)S(1)}, u32[]{:S(2)}, u32[]{:S(2)}) collective-permute-start(bf16[384,640]{1,0:T(8,128)(2,1)S(1)} %collective-permute-done.q1.a1), channel_id=1, source_target_pairs={{3,1},{5,3},{7,5},{9,7},{11,9},{13,11},{15,13},{17,15},{19,17},{21... | collective-permute-start | bytes 1474568 | tf_op jit(solution)/shard_map/ppermute | solution.py:242
  33.0 0.2 collective-permute-done.1.k1
  33.2 4.6 %shard_map.106 = (f32[384,256]{1,0:T(8,128)S(1)}, f32[384,512]{1,0:T(8,128)S(1)}, bf16[384,256]{1,0:T(8,128)(2,1)S(1)}, f32[384,512]{1,0:T(8,128)S(1)}) custom-call(s32[1]{0:T(128)} %bitcast.odd, bf16[384,640]{1,0:T(8,128)(2,1)S(1)} %get-tuple-element.39.q.qa.q0.a0, bf16[384,640]{1,0:T(8,128)(2,1)S(1)} %get-tuple-element.39.q.qa.q0.a0, ...), custom_call_target="tpu_custom_call" | custom-call | flops 9059696640 | bytes 1024 | tf_op jit(solution)/shard_map/pallas_call | solution.py:216
  37.9 0.0 collective-permute-done.2.q1
  37.9 1.3 %collective-permute-start.4 = (bf16[384,512]{1,0:T(8,128)(2,1)}, bf16[384,512]{1,0:T(8,128)(2,1)S(1)}, u32[]{:S(2)}, u32[]{:S(2)}) collective-permute-start(bf16[384,512]{1,0:T(8,128)(2,1)} %collective-permute-done.2.q1), channel_id=1, source_target_pairs={{3,1},{5,3},{7,5},{9,7},{11,9},{13,11},{15,13},{17,15},{19,17},{21... | collective-permute-start | bytes 1179656 | tf_op jit(solution)/shard_map/ppermute | solution.py:242
  39.2 5.8 %shard_map.107 = (f32[384,256]{1,0:T(8,128)S(1)}, f32[384,512]{1,0:T(8,128)S(1)}, bf16[384,512]{1,0:T(8,128)(2,1)S(1)}, f32[384,512]{1,0:T(8,128)S(1)}) custom-call(s32[1]{0:T(128)} %bitcast.odd, bf16[384,512]{1,0:T(8,128)(2,1)} %get-tuple-element.44.q.q0, bf16[384,640]{1,0:T(8,128)(2,1)S(1)} %get-tuple-element.39.q.qa.q0.a0, ...), custom_call_target="tpu_custom_call" | custom-call | flops 9059696640 | bytes 1024 | tf_op jit(solution)/shard_map/pallas_call | solution.py:216
  45.0 8.5 %collective-permute-start.3 = (bf16[384,512]{1,0:T(8,128)(2,1)S(1)}, bf16[384,512]{1,0:T(8,128)(2,1)S(1)}, u32[]{:S(2)}, u32[]{:S(2)}) collective-permute-start(bf16[384,512]{1,0:T(8,128)(2,1)S(1)} %get-tuple-element.58), channel_id=1, source_target_pairs={{1,0},{0,1},{3,2},{2,3},{5,4},{4,5},{7,6},{6,7},{9,8},{8,9},{11,10... | collective-permute-start | bytes 1179656 | tf_op jit(solution)/shard_map/ppermute | solution.py:245
  53.5 0.0 collective-permute-done.5.a2_far
  53.6 2.4 %shard_map.108 = (bf16[384,256]{1,0:T(8,128)(2,1)S(1)}, bf16[384,512]{1,0:T(8,128)(2,1)S(1)}, bf16[384,640]{1,0:T(8,128)(2,1)S(1)}) custom-call(s32[1]{0:T(128)} %bitcast.odd, bf16[384,640]{1,0:T(8,128)(2,1)S(1)} %copy.14.q2_far, bf16[384,640]{1,0:T(8,128)(2,1)S(1)} %collective-permute-done.5.a2_far, ...), custom_call_target="tpu_custom_call", output_to_operand_aliasing={{2}: (1, {})} | custom-call | bytes 1024 | tf_op jit(solution)/shard_map/pallas_call | solution.py:216
  56.0 12.2 %collective-permute-start.9 = (bf16[384,512]{1,0:T(8,128)(2,1)S(1)}, bf16[384,512]{1,0:T(8,128)(2,1)S(1)}, u32[]{:S(2)}, u32[]{:S(2)}) collective-permute-start(bf16[384,512]{1,0:T(8,128)(2,1)S(1)} %get-tuple-element.65), channel_id=1, source_target_pairs={{2,0},{3,1},{4,2},{5,3},{6,4},{7,5},{8,6},{9,7},{10,8},{11,9},{12,... | collective-permute-start | bytes 1179656 | tf_op jit(solution)/shard_map/ppermute | solution.py:242
  68.1 2.4 %shard_map.109 = (bf16[384,512]{1,0:T(8,128)(2,1)S(1)}, bf16[384,512]{1,0:T(8,128)(2,1)S(1)}, bf16[384,512]{1,0:T(8,128)(2,1)S(1)}) custom-call(s32[1]{0:T(128)} %bitcast.odd, bf16[384,512]{1,0:T(8,128)(2,1)S(1)} %collective-permute-done.4.q2_far, bf16[384,640]{1,0:T(8,128)(2,1)S(1)} %get-tuple-element.61.a2_far, ...), custom_call_target="tpu_custom_call", output_to_operand_aliasing={{2}: (1, {})} | custom-call | bytes 1024 | tf_op jit(solution)/shard_map/pallas_call | solution.py:216
  70.6 1.3 %collective-permute-start.8 = (bf16[384,512]{1,0:T(8,128)(2,1)S(1)}, bf16[384,512]{1,0:T(8,128)(2,1)S(1)}, u32[]{:S(2)}, u32[]{:S(2)}) collective-permute-start(bf16[384,512]{1,0:T(8,128)(2,1)S(1)} %get-tuple-element.64), channel_id=1, source_target_pairs={{1,2},{3,4},{5,6},{7,8},{9,10},{11,12},{13,14},{15,16},{17,18},{19... | collective-permute-start | bytes 1179656 | tf_op jit(solution)/shard_map/ppermute | solution.py:306
  71.9 5.0 %collective-permute-start.10 = (bf16[384,512]{1,0:T(8,128)(2,1)S(1)}, bf16[384,512]{1,0:T(8,128)(2,1)S(1)}, u32[]{:S(2)}, u32[]{:S(2)}) collective-permute-start(bf16[384,512]{1,0:T(8,128)(2,1)S(1)} %get-tuple-element.70), channel_id=1, source_target_pairs={{2,0},{3,1},{4,2},{5,3},{6,4},{7,5},{8,6},{9,7},{10,8},{11,9},{12,... | collective-permute-start | bytes 1179656 | tf_op jit(solution)/shard_map/ppermute | solution.py:242
  76.9 7.9 %collective-permute-done.8.r2 = bf16[384,512]{1,0:T(8,128)(2,1)S(1)} collective-permute-done((bf16[384,512]{1,0:T(8,128)(2,1)S(1)}, bf16[384,512]{1,0:T(8,128)(2,1)S(1)}, u32[]{:S(2)}, u32[]{:S(2)}) %collective-permute-start.8) | collective-permute-done | bytes 393248 | tf_op jit(solution)/shard_map/ppermute | solution.py:306
  84.8 0.9 shard_map.110
  85.7 4.0 %collective-permute-done.10.back = bf16[384,512]{1,0:T(8,128)(2,1)S(1)} collective-permute-done((bf16[384,512]{1,0:T(8,128)(2,1)S(1)}, bf16[384,512]{1,0:T(8,128)(2,1)S(1)}, u32[]{:S(2)}, u32[]{:S(2)}) %collective-permute-start.10) | collective-permute-done | bytes 393248 | tf_op jit(solution)/shard_map/ppermute | solution.py:242
  89.8 1.0 %shard_map.111 = (bf16[384,512]{1,0:T(8,128)(2,1)}, bf16[384,512]{1,0:T(8,128)(2,1)}) custom-call(bf16[384,256]{1,0:T(8,128)(2,1)S(1)} %get-tuple-element.67.pk, bf16[384,256]{1,0:T(8,128)(2,1)S(1)} %get-tuple-element.68.pv, f32[384,512]{1,0:T(8,128)S(1)} %get-tuple-element.69.dkv, bf16[384,512]{1,0:T(8,128)(2,1)S(1)} %collective-permute-done.10.back), custom_call_target="tpu_custom_call" | custom-call | flops 1048576 | bytes 1024 | tf_op jit(solution)/shard_map/pallas_call | solution.py:216
  (15 shorter events, 0.1 us)
Async XLA Ops:
  0.6 6.5 %copy-start.5 = (bf16[384,512]{1,0:T(8,128)(2,1)S(1)}, bf16[384,512]{1,0:T(8,128)(2,1)}, u32[]{:S(2)}) copy-start(bf16[384,512]{1,0:T(8,128)(2,1)} %param.8) | copy-start | bytes 1179652
  0.6 6.5 %copy-start.3 = (bf16[384,512]{1,0:T(8,128)(2,1)S(1)}, bf16[384,512]{1,0:T(8,128)(2,1)}, u32[]{:S(2)}) copy-start(bf16[384,512]{1,0:T(8,128)(2,1)} %param.11) | copy-start | bytes 1179652
  0.7 6.5 %copy-start.4 = (bf16[384,512]{1,0:T(8,128)(2,1)S(1)}, bf16[384,512]{1,0:T(8,128)(2,1)}, u32[]{:S(2)}) copy-start(bf16[384,512]{1,0:T(8,128)(2,1)} %param.12) | copy-start | bytes 1179652
  2.8 30.4 %collective-permute-start.1 = (bf16[384,1024]{1,0:T(8,128)(2,1)S(1)}, bf16[384,1024]{1,0:T(8,128)(2,1)S(1)}, u32[]{:S(2)}, u32[]{:S(2)}) collective-permute-start(bf16[384,1024]{1,0:T(8,128)(2,1)S(1)} %constant_dynamic-update-slice_fusion.kv.k0), channel_id=1, source_target_pairs={{0,2},{1,3},{2,4},{3,5},{4,6},{5,7},{6,8},{7,9},{8,10},{9,11},{10,... | collective-permute-start | bytes 2359304 | tf_op jit(solution)/shard_map/ppermute | solution.py:242
  7.2 0.7 copy-start
  7.2 0.7 copy-start.1
  7.2 0.7 copy-start.2
  9.6 22.1 %collective-permute-start = (bf16[384,640]{1,0:T(8,128)(2,1)S(1)}, bf16[384,640]{1,0:T(8,128)(2,1)S(1)}, u32[]{:S(2)}, u32[]{:S(2)}) collective-permute-start(bf16[384,640]{1,0:T(8,128)(2,1)S(1)} %get-tuple-element.39.q.qa.q0.a0), channel_id=1, source_target_pairs={{1,0},{0,1},{3,2},{2,3},{5,4},{4,5},{7,6},{6,7},{9,8},{8,9},{11,10... | collective-permute-start | bytes 1474568 | tf_op jit(solution)/shard_map/ppermute | solution.py:245
  12.9 40.7 %collective-permute-start.6 = (bf16[384,640]{1,0:T(8,128)(2,1)S(1)}, bf16[384,640]{1,0:T(8,128)(2,1)S(1)}, u32[]{:S(2)}, u32[]{:S(2)}) collective-permute-start(bf16[384,640]{1,0:T(8,128)(2,1)S(1)} %get-tuple-element.39.q.qa.q0.a0), channel_id=1, source_target_pairs={{128,127},{256,255},{384,383}} | collective-permute-start | bytes 1474568 | tf_op jit(solution)/shard_map/ppermute | solution.py:259
  13.6 24.3 %collective-permute-start.2 = (bf16[384,512]{1,0:T(8,128)(2,1)}, bf16[384,512]{1,0:T(8,128)(2,1)}, u32[]{:S(2)}, u32[]{:S(2)}) collective-permute-start(bf16[384,512]{1,0:T(8,128)(2,1)} %get-tuple-element.44.q.q0), channel_id=1, source_target_pairs={{1,0},{0,1},{3,2},{2,3},{5,4},{4,5},{7,6},{6,7},{9,8},{8,9},{11,10... | collective-permute-start | bytes 1179656 | tf_op jit(solution)/shard_map/ppermute | solution.py:245
  25.1 43.0 %collective-permute-start.7 = (bf16[384,512]{1,0:T(8,128)(2,1)}, bf16[384,512]{1,0:T(8,128)(2,1)S(1)}, u32[]{:S(2)}, u32[]{:S(2)}) collective-permute-start(bf16[384,512]{1,0:T(8,128)(2,1)} %get-tuple-element.44.q.q0), channel_id=1, source_target_pairs={{128,127},{256,255},{384,383}} | collective-permute-start | bytes 1179656 | tf_op jit(solution)/shard_map/ppermute | solution.py:259
  31.7 21.8 %collective-permute-start.5 = (bf16[384,640]{1,0:T(8,128)(2,1)S(1)}, bf16[384,640]{1,0:T(8,128)(2,1)S(1)}, u32[]{:S(2)}, u32[]{:S(2)}) collective-permute-start(bf16[384,640]{1,0:T(8,128)(2,1)S(1)} %collective-permute-done.q1.a1), channel_id=1, source_target_pairs={{3,1},{5,3},{7,5},{9,7},{11,9},{13,11},{15,13},{17,15},{19,17},{21... | collective-permute-start | bytes 1474568 | tf_op jit(solution)/shard_map/ppermute | solution.py:242
  37.9 30.2 %collective-permute-start.4 = (bf16[384,512]{1,0:T(8,128)(2,1)}, bf16[384,512]{1,0:T(8,128)(2,1)S(1)}, u32[]{:S(2)}, u32[]{:S(2)}) collective-permute-start(bf16[384,512]{1,0:T(8,128)(2,1)} %collective-permute-done.2.q1), channel_id=1, source_target_pairs={{3,1},{5,3},{7,5},{9,7},{11,9},{13,11},{15,13},{17,15},{19,17},{21... | collective-permute-start | bytes 1179656 | tf_op jit(solution)/shard_map/ppermute | solution.py:242
  45.0 31.9 %collective-permute-start.3 = (bf16[384,512]{1,0:T(8,128)(2,1)S(1)}, bf16[384,512]{1,0:T(8,128)(2,1)S(1)}, u32[]{:S(2)}, u32[]{:S(2)}) collective-permute-start(bf16[384,512]{1,0:T(8,128)(2,1)S(1)} %get-tuple-element.58), channel_id=1, source_target_pairs={{1,0},{0,1},{3,2},{2,3},{5,4},{4,5},{7,6},{6,7},{9,8},{8,9},{11,10... | collective-permute-start | bytes 1179656 | tf_op jit(solution)/shard_map/ppermute | solution.py:245
  56.0 21.0 %collective-permute-start.9 = (bf16[384,512]{1,0:T(8,128)(2,1)S(1)}, bf16[384,512]{1,0:T(8,128)(2,1)S(1)}, u32[]{:S(2)}, u32[]{:S(2)}) collective-permute-start(bf16[384,512]{1,0:T(8,128)(2,1)S(1)} %get-tuple-element.65), channel_id=1, source_target_pairs={{2,0},{3,1},{4,2},{5,3},{6,4},{7,5},{8,6},{9,7},{10,8},{11,9},{12,... | collective-permute-start | bytes 1179656 | tf_op jit(solution)/shard_map/ppermute | solution.py:242
  70.6 14.2 %collective-permute-start.8 = (bf16[384,512]{1,0:T(8,128)(2,1)S(1)}, bf16[384,512]{1,0:T(8,128)(2,1)S(1)}, u32[]{:S(2)}, u32[]{:S(2)}) collective-permute-start(bf16[384,512]{1,0:T(8,128)(2,1)S(1)} %get-tuple-element.64), channel_id=1, source_target_pairs={{1,2},{3,4},{5,6},{7,8},{9,10},{11,12},{13,14},{15,16},{17,18},{19... | collective-permute-start | bytes 1179656 | tf_op jit(solution)/shard_map/ppermute | solution.py:306
  71.9 17.9 %collective-permute-start.10 = (bf16[384,512]{1,0:T(8,128)(2,1)S(1)}, bf16[384,512]{1,0:T(8,128)(2,1)S(1)}, u32[]{:S(2)}, u32[]{:S(2)}) collective-permute-start(bf16[384,512]{1,0:T(8,128)(2,1)S(1)} %get-tuple-element.70), channel_id=1, source_target_pairs={{2,0},{3,1},{4,2},{5,3},{6,4},{7,5},{8,6},{9,7},{10,8},{11,9},{12,... | collective-permute-start | bytes 1179656 | tf_op jit(solution)/shard_map/ppermute | solution.py:242

commit v3 on v2

--- a/solution.py
+++ b/solution.py
@@ -80,7 +80,8 @@
     half = lax.broadcasted_iota(jnp.int32, qp.shape, 1) // SIZE
     qa = jnp.concatenate([qp, aux], 1)
     da = jnp.concatenate([dop, aux], 1)
-    km, qm, dm, pb, db = [], [], [], [], []
+    km, qm, dm, vm, sels, seld = [], [], [], [], [], []
+    rows = qp.shape[0]
     for h in range(2):
         head = c * HC + hp * 2 + h
         sel = jnp.where((lane % 8 == head) & (lane < 24), -1.0, 0.0)
@@ -90,19 +91,23 @@
         mine = half == h
         zero = jnp.zeros_like(kp)
         km.append(jnp.where(mine, kp, zero))
-        vm = jnp.where(mine, vp, zero)
+        vm.append(jnp.where(mine, vp, zero))
         qm.append(jnp.where(mine, qp, zero))
         dm.append(jnp.where(mine, dop, zero))
-        s = dot(jnp.concatenate([km[h], jnp.broadcast_to(sel, kp.shape).astype(bf16)], 1), qa, 1, 1)
-        dp = dot(jnp.concatenate([vm, jnp.broadcast_to(sel_d, kp.shape).astype(bf16)], 1), da, 1, 1)
-        p = jnp.exp2(s * EXP_SCALE)
-        if rank_row is not None:
-            p = jnp.where(rank_row >= rank_col, p, 0.0)
-        pb.append(p.astype(bf16))
-        db.append((p * dp).astype(bf16))
+        sels.append(jnp.broadcast_to(sel, kp.shape).astype(bf16))
+        seld.append(jnp.broadcast_to(sel_d, kp.shape).astype(bf16))
+    k_both = jnp.concatenate(km, 0)
+    s = dot(jnp.concatenate([k_both, jnp.concatenate(sels, 0)], 1), qa, 1, 1)
+    dp = dot(jnp.concatenate([jnp.concatenate(vm, 0), jnp.concatenate(seld, 0)], 1), da, 1, 1)
+    p = jnp.exp2(s * EXP_SCALE)
+    if rank_row is not None:
+        seen = rank_row >= rank_col
+        p = jnp.where(jnp.concatenate([seen, seen], 0), p, 0.0)
+    p_low, ds = p.astype(bf16), (p * dp).astype(bf16)
+    pb, db = [p_low[:rows], p_low[rows:]], [ds[:rows], ds[rows:]]
     dv = dot(jnp.concatenate(pb, 1), jnp.concatenate(dm, 0), 1, 0)
     dk = dot(jnp.concatenate(db, 1), jnp.concatenate(qm, 0), 1, 0)
-    dq = dot(jnp.concatenate(db, 0), jnp.concatenate(km, 0), 0, 0)
+    dq = dot(k_both, ds, 0, 0).T
     return dq, dk, dv
 
 
@@ -289,8 +294,6 @@
         if c == 0:
             q1[1], dq1 = lax.optimization_barrier((q1[1], dq1))
             q2.append(shifted(q1[1], -2, lambda i: i % 2 == 1 and i % SPAN != SPAN - 1))
-    back_q1 = swapped(dq1[0])
-    q2[0], tail = lax.optimization_barrier((q2[0], dq1[0]))
     for c in range(CHUNKS):
         dkv1 = parts[c]
         x, send, q2[c] = call(
@@ -302,6 +305,9 @@
             alias={1: 2},
         )
         dq2 = (x,)
+        if c == 0:
+            dq1, dq2, q2[1] = lax.optimization_barrier((dq1, dq2, q2[1]))
+            back_q1 = swapped(dq1[0])
         back_kv.append(shifted(send, -2))
     back_q2 = lax.ppermute(dq2[0], AXES, [(i, i + 1) for i in range(1, n - 1, 2)])
     gq, pk, pv = call(

time: 91.2 us -> 91.8 us (level)
  starting transfers between devices: 50 us -> 53.4 us
  Pallas kernels: 24.7 us -> 22.8 us
    ppermute x5, starting transfers between devices: 24 us -> 34 us  [shifted(): lax.ppermute(x, AXES, [(i - by, i) for i in range(n) if 0 <= i - by < n a...]
    ppermute x3, starting transfers between devices: 23.3 us -> 16.7 us  [swapped(): return lax.ppermute(x, AXES, [(i ^ 1, i) for i in range(n)])]
    ppermute x1, waiting for transfers between devices: 7.91 us -> 4.21 us  [per_device(): lax.ppermute(dq2[0], AXES, [(i, i + 1) for i in range(1, n - 1, 2)])]
    ppermute x3, waiting for transfers between devices: 0.01 us -> 3.34 us  [swapped(): return lax.ppermute(x, AXES, [(i ^ 1, i) for i in range(n)])]
    pallas_call x9, Pallas kernels: 24.7 us -> 22.8 us  [call(): pl.pallas_call(kernel, out_shape=outs, in_specs=[SM] * n_smem + [VM] * ne...]
  transfers between devices with their start and end apart: 11 -> 11, of which waited for: 3 -> 4; matrix products, arithmetic and copies ran while one was open for 0% -> 0% of each run, Pallas kernels for 26% -> 24%
where the time goes in v3:
time: 91.8 us; the launch traced here: 91.3 us
  starting transfers between devices  53.4 us (58%)
  Pallas kernels  22.8 us (25%)
  waiting for transfers between devices  11.3 us (12%)
  local copies, waits for them, and re-layouts  2.83 us (3%)
  between operations  0.95 us (1%)
    ppermute x5, starting transfers between devices, shifted(): lax.ppermute(x, AXES, [(i - by, i) for i in range(n) if 0 <= i - by < n a...  34 us
    pallas_call x9, Pallas kernels, call(): pl.pallas_call(kernel, out_shape=outs, in_specs=[SM] * n_smem + [VM] * ne...  22.8 us
    ppermute x3, starting transfers between devices, swapped(): return lax.ppermute(x, AXES, [(i ^ 1, i) for i in range(n)])  16.7 us
    ppermute x1, waiting for transfers between devices, per_device(): lax.ppermute(dq2[0], AXES, [(i, i + 1) for i in range(1, n - 1, 2)])  4.21 us
    ppermute x5, waiting for transfers between devices, shifted(): lax.ppermute(x, AXES, [(i - by, i) for i in range(n) if 0 <= i - by < n a...  3.79 us
    ppermute x3, waiting for transfers between devices, swapped(): return lax.ppermute(x, AXES, [(i ^ 1, i) for i in range(n)])  3.34 us
  transfers between devices with their start and end apart: 11, of which 4 were waited for; matrix products, arithmetic and copies ran while one was open for 0% of the time, Pallas kernels for 24%

profile of v3, /device:TPU:40, one launch (start us, length us, event | category | flops | bytes accessed | tf_op | source)
XLA Modules:
  0.0 91.3 jit_solution(8296326003378591575)
XLA Ops:
  0.7 1.1 %constant_dynamic-update-slice_fusion.1 = bf16[384,1024]{1,0:T(8,128)(2,1)S(1)} fusion(bf16[384,512]{1,0:T(8,128)(2,1)} %param.9), kind=kLoop, calls=%fused_computation.2 | loop fusion | bytes 786432
  1.8 1.0 %constant_dynamic-update-slice_fusion.kv.k0 = bf16[384,1024]{1,0:T(8,128)(2,1)S(1)} fusion(bf16[384,1024]{1,0:T(8,128)(2,1)S(1)} %constant_dynamic-update-slice_fusion.1, bf16[384,512]{1,0:T(8,128)(2,1)} %param.10), kind=kLoop, calls=%fused_computation.1 | loop fusion | bytes 786432 | tf_op jit(solution)/shard_map/concatenate | solution.py:254
  2.8 4.3 %collective-permute-start.1 = (bf16[384,1024]{1,0:T(8,128)(2,1)S(1)}, bf16[384,1024]{1,0:T(8,128)(2,1)S(1)}, u32[]{:S(2)}, u32[]{:S(2)}) collective-permute-start(bf16[384,1024]{1,0:T(8,128)(2,1)S(1)} %constant_dynamic-update-slice_fusion.kv.k0), channel_id=1, source_target_pairs={{0,2},{1,3},{2,4},{3,5},{4,6},{5,7},{6,8},{7,9},{8,10},{9,11},{10,... | collective-permute-start | bytes 2359304 | tf_op jit(solution)/shard_map/ppermute | solution.py:247
  7.2 0.0 copy-start
  7.2 0.0 copy-start.1
  7.2 0.0 copy-start.2
  7.2 0.1 pad_maximum_fusion.everything
  7.3 0.6 copy-done
  7.9 1.7 %shard_map.103 = (bf16[384,640]{1,0:T(8,128)(2,1)S(1)}, bf16[384,512]{1,0:T(8,128)(2,1)}, f32[8,384]{1,0:T(8,128)S(1)}) custom-call(s32[1]{0:T(128)} %bitcast.1.blk, s32[1,3]{1,0:T(1,128)S(1)} %copy-done.2, f32[8,384]{1,0:T(8,128)S(1)} %copy-done, s32[1,384]{1,0:T(1,128)S(1)} %copy-done.1, bf16[384,1536]{1,0:T(8,128)(2,1)S(1)} %pad_maximum_fusion.everything), custom_call_target="tpu_custom_call" | custom-call | bytes 1024 | tf_op jit(solution)/shard_map/pallas_call | solution.py:221
  9.6 3.2 %collective-permute-start = (bf16[384,640]{1,0:T(8,128)(2,1)S(1)}, bf16[384,640]{1,0:T(8,128)(2,1)S(1)}, u32[]{:S(2)}, u32[]{:S(2)}) collective-permute-start(bf16[384,640]{1,0:T(8,128)(2,1)S(1)} %get-tuple-element.41.q.qa.q0.a0), channel_id=1, source_target_pairs={{1,0},{0,1},{3,2},{2,3},{5,4},{4,5},{7,6},{6,7},{9,8},{8,9},{11,10... | collective-permute-start | bytes 1474568 | tf_op jit(solution)/shard_map/ppermute | solution.py:250
  12.9 0.7 collective-permute-start.4
  13.6 11.5 %collective-permute-start.2 = (bf16[384,512]{1,0:T(8,128)(2,1)}, bf16[384,512]{1,0:T(8,128)(2,1)}, u32[]{:S(2)}, u32[]{:S(2)}) collective-permute-start(bf16[384,512]{1,0:T(8,128)(2,1)} %get-tuple-element.46.q.q0), channel_id=1, source_target_pairs={{1,0},{0,1},{3,2},{2,3},{5,4},{4,5},{7,6},{6,7},{9,8},{8,9},{11,10... | collective-permute-start | bytes 1179656 | tf_op jit(solution)/shard_map/ppermute | solution.py:250
  25.1 0.7 collective-permute-start.7
  25.8 2.3 %shard_map.104 = (f32[384,256]{1,0:T(8,128)S(1)}, f32[384,512]{1,0:T(8,128)S(1)}) custom-call(bf16[384,640]{1,0:T(8,128)(2,1)S(1)} %get-tuple-element.41.q.qa.q0.a0, bf16[384,640]{1,0:T(8,128)(2,1)S(1)} %get-tuple-element.41.q.qa.q0.a0, bf16[384,1024]{1,0:T(8,128)(2,1)S(1)} %constant_dynamic-update-slice_fusion.kv.k0, f32[8,384]{1,0:T(8,128)S(1)} %get-tuple-element.43.rank), custom_call_target="tpu_custom_call" | custom-call | flops 3019898880 | bytes 1024 | tf_op jit(solution)/shard_map/pallas_call | solution.py:221
  28.1 3.3 %shard_map.105 = (f32[384,256]{1,0:T(8,128)S(1)}, f32[384,512]{1,0:T(8,128)S(1)}) custom-call(bf16[384,512]{1,0:T(8,128)(2,1)} %get-tuple-element.46.q.q0, bf16[384,640]{1,0:T(8,128)(2,1)S(1)} %get-tuple-element.41.q.qa.q0.a0, bf16[384,1024]{1,0:T(8,128)(2,1)S(1)} %constant_dynamic-update-slice_fusion.kv.k0, f32[8,384]{1,0:T(8,128)S(1)} %get-tuple-element.43.rank), custom_call_target="tpu_custom_call" | custom-call | flops 3019898880 | bytes 1024 | tf_op jit(solution)/shard_map/pallas_call | solution.py:221
  31.5 0.0 collective-permute-done.q1.a1
  31.5 1.3 %collective-permute-start.3 = (bf16[384,640]{1,0:T(8,128)(2,1)S(1)}, bf16[384,640]{1,0:T(8,128)(2,1)S(1)}, u32[]{:S(2)}, u32[]{:S(2)}) collective-permute-start(bf16[384,640]{1,0:T(8,128)(2,1)S(1)} %collective-permute-done.q1.a1), channel_id=1, source_target_pairs={{3,1},{5,3},{7,5},{9,7},{11,9},{13,11},{15,13},{17,15},{19,17},{21... | collective-permute-start | bytes 1474568 | tf_op jit(solution)/shard_map/ppermute | solution.py:247
  32.8 0.5 collective-permute-done.1.k1
  33.2 4.0 %shard_map.106 = (f32[384,256]{1,0:T(8,128)S(1)}, f32[384,512]{1,0:T(8,128)S(1)}, bf16[384,256]{1,0:T(8,128)(2,1)S(1)}, f32[384,512]{1,0:T(8,128)S(1)}) custom-call(s32[1]{0:T(128)} %bitcast.odd, bf16[384,640]{1,0:T(8,128)(2,1)S(1)} %get-tuple-element.41.q.qa.q0.a0, bf16[384,640]{1,0:T(8,128)(2,1)S(1)} %get-tuple-element.41.q.qa.q0.a0, ...), custom_call_target="tpu_custom_call" | custom-call | flops 9059696640 | bytes 1024 | tf_op jit(solution)/shard_map/pallas_call | solution.py:221
  37.2 1.3 %collective-permute-start.5 = (bf16[384,512]{1,0:T(8,128)(2,1)}, bf16[384,512]{1,0:T(8,128)(2,1)S(1)}, u32[]{:S(2)}, u32[]{:S(2)}) collective-permute-start(bf16[384,512]{1,0:T(8,128)(2,1)} %collective-permute-done.2.q1), channel_id=1, source_target_pairs={{3,1},{5,3},{7,5},{9,7},{11,9},{13,11},{15,13},{17,15},{19,17},{21... | collective-permute-start | bytes 1179656 | tf_op jit(solution)/shard_map/ppermute | solution.py:247
  38.5 5.1 %shard_map.107 = (f32[384,256]{1,0:T(8,128)S(1)}, f32[384,512]{1,0:T(8,128)S(1)}, bf16[384,512]{1,0:T(8,128)(2,1)S(1)}, f32[384,512]{1,0:T(8,128)S(1)}) custom-call(s32[1]{0:T(128)} %bitcast.odd, bf16[384,512]{1,0:T(8,128)(2,1)} %get-tuple-element.46.q.q0, bf16[384,640]{1,0:T(8,128)(2,1)S(1)} %get-tuple-element.41.q.qa.q0.a0, ...), custom_call_target="tpu_custom_call" | custom-call | flops 9059696640 | bytes 1024 | tf_op jit(solution)/shard_map/pallas_call | solution.py:221
  43.7 2.2 %shard_map.108 = (bf16[384,256]{1,0:T(8,128)(2,1)S(1)}, bf16[384,512]{1,0:T(8,128)(2,1)S(1)}, bf16[384,640]{1,0:T(8,128)(2,1)S(1)}) custom-call(s32[1]{0:T(128)} %bitcast.odd, bf16[384,640]{1,0:T(8,128)(2,1)S(1)} %copy.14.q2_far, bf16[384,640]{1,0:T(8,128)(2,1)S(1)} %collective-permute-done.3.a2_far, ...), custom_call_target="tpu_custom_call", output_to_operand_aliasing={{2}: (1, {})} | custom-call | bytes 1024 | tf_op jit(solution)/shard_map/pallas_call | solution.py:221
  46.0 18.0 %collective-permute-start.9 = (bf16[384,512]{1,0:T(8,128)(2,1)S(1)}, bf16[384,512]{1,0:T(8,128)(2,1)S(1)}, u32[]{:S(2)}, u32[]{:S(2)}) collective-permute-start(bf16[384,512]{1,0:T(8,128)(2,1)S(1)} %get-tuple-element.69), channel_id=1, source_target_pairs={{2,0},{3,1},{4,2},{5,3},{6,4},{7,5},{8,6},{9,7},{10,8},{11,9},{12,... | collective-permute-start | bytes 1179656 | tf_op jit(solution)/shard_map/ppermute | solution.py:247
  64.0 1.9 %collective-permute-start.6 = (bf16[384,512]{1,0:T(8,128)(2,1)S(1)}, bf16[384,512]{1,0:T(8,128)(2,1)S(1)}, u32[]{:S(2)}, u32[]{:S(2)}) collective-permute-start(bf16[384,512]{1,0:T(8,128)(2,1)S(1)} %get-tuple-element.63), channel_id=1, source_target_pairs={{1,0},{0,1},{3,2},{2,3},{5,4},{4,5},{7,6},{6,7},{9,8},{8,9},{11,10... | collective-permute-start | bytes 1179656 | tf_op jit(solution)/shard_map/ppermute | solution.py:250
  66.0 2.2 %shard_map.109 = (bf16[384,512]{1,0:T(8,128)(2,1)S(1)}, bf16[384,512]{1,0:T(8,128)(2,1)S(1)}, bf16[384,512]{1,0:T(8,128)(2,1)S(1)}) custom-call(s32[1]{0:T(128)} %bitcast.odd, bf16[384,512]{1,0:T(8,128)(2,1)S(1)} %collective-permute-done.5.q2_far, bf16[384,640]{1,0:T(8,128)(2,1)S(1)} %get-tuple-element.65.a2_far, ...), custom_call_target="tpu_custom_call", output_to_operand_aliasing={{2}: (1, {})} | custom-call | bytes 1024 | tf_op jit(solution)/shard_map/pallas_call | solution.py:221
  68.2 1.3 %collective-permute-start.8 = (bf16[384,512]{1,0:T(8,128)(2,1)S(1)}, bf16[384,512]{1,0:T(8,128)(2,1)S(1)}, u32[]{:S(2)}, u32[]{:S(2)}) collective-permute-start(bf16[384,512]{1,0:T(8,128)(2,1)S(1)} %get-tuple-element.68), channel_id=1, source_target_pairs={{1,2},{3,4},{5,6},{7,8},{9,10},{11,12},{13,14},{15,16},{17,18},{19... | collective-permute-start | bytes 1179656 | tf_op jit(solution)/shard_map/ppermute | solution.py:312
  69.5 9.1 %collective-permute-start.10 = (bf16[384,512]{1,0:T(8,128)(2,1)S(1)}, bf16[384,512]{1,0:T(8,128)(2,1)S(1)}, u32[]{:S(2)}, u32[]{:S(2)}) collective-permute-start(bf16[384,512]{1,0:T(8,128)(2,1)S(1)} %get-tuple-element.74), channel_id=1, source_target_pairs={{2,0},{3,1},{4,2},{5,3},{6,4},{7,5},{8,6},{9,7},{10,8},{11,9},{12,... | collective-permute-start | bytes 1179656 | tf_op jit(solution)/shard_map/ppermute | solution.py:247
  78.6 3.3 %collective-permute-done.6.r1 = bf16[384,512]{1,0:T(8,128)(2,1)S(1)} collective-permute-done((bf16[384,512]{1,0:T(8,128)(2,1)S(1)}, bf16[384,512]{1,0:T(8,128)(2,1)S(1)}, u32[]{:S(2)}, u32[]{:S(2)}) %collective-permute-start.6) | collective-permute-done | bytes 393248 | tf_op jit(solution)/shard_map/ppermute | solution.py:250
  82.0 4.2 %collective-permute-done.8.r2 = bf16[384,512]{1,0:T(8,128)(2,1)S(1)} collective-permute-done((bf16[384,512]{1,0:T(8,128)(2,1)S(1)}, bf16[384,512]{1,0:T(8,128)(2,1)S(1)}, u32[]{:S(2)}, u32[]{:S(2)}) %collective-permute-start.8) | collective-permute-done | bytes 393248 | tf_op jit(solution)/shard_map/ppermute | solution.py:312
  86.2 0.9 shard_map.110
  87.1 3.3 %collective-permute-done.10.back = bf16[384,512]{1,0:T(8,128)(2,1)S(1)} collective-permute-done((bf16[384,512]{1,0:T(8,128)(2,1)S(1)}, bf16[384,512]{1,0:T(8,128)(2,1)S(1)}, u32[]{:S(2)}, u32[]{:S(2)}) %collective-permute-start.10) | collective-permute-done | bytes 393248 | tf_op jit(solution)/shard_map/ppermute | solution.py:247
  90.4 1.0 %shard_map.111 = (bf16[384,512]{1,0:T(8,128)(2,1)}, bf16[384,512]{1,0:T(8,128)(2,1)}) custom-call(bf16[384,256]{1,0:T(8,128)(2,1)S(1)} %get-tuple-element.71.pk, bf16[384,256]{1,0:T(8,128)(2,1)S(1)} %get-tuple-element.72.pv, f32[384,512]{1,0:T(8,128)S(1)} %get-tuple-element.73.dkv, bf16[384,512]{1,0:T(8,128)(2,1)S(1)} %collective-permute-done.10.back), custom_call_target="tpu_custom_call" | custom-call | flops 1048576 | bytes 1024 | tf_op jit(solution)/shard_map/pallas_call | solution.py:221
  (15 shorter events, 0.1 us)
Async XLA Ops:
  0.6 6.5 %copy-start.5 = (bf16[384,512]{1,0:T(8,128)(2,1)S(1)}, bf16[384,512]{1,0:T(8,128)(2,1)}, u32[]{:S(2)}) copy-start(bf16[384,512]{1,0:T(8,128)(2,1)} %param.8) | copy-start | bytes 1179652
  0.6 6.5 %copy-start.3 = (bf16[384,512]{1,0:T(8,128)(2,1)S(1)}, bf16[384,512]{1,0:T(8,128)(2,1)}, u32[]{:S(2)}) copy-start(bf16[384,512]{1,0:T(8,128)(2,1)} %param.11) | copy-start | bytes 1179652
  0.7 6.5 %copy-start.4 = (bf16[384,512]{1,0:T(8,128)(2,1)S(1)}, bf16[384,512]{1,0:T(8,128)(2,1)}, u32[]{:S(2)}) copy-start(bf16[384,512]{1,0:T(8,128)(2,1)} %param.12) | copy-start | bytes 1179652
  2.8 30.4 %collective-permute-start.1 = (bf16[384,1024]{1,0:T(8,128)(2,1)S(1)}, bf16[384,1024]{1,0:T(8,128)(2,1)S(1)}, u32[]{:S(2)}, u32[]{:S(2)}) collective-permute-start(bf16[384,1024]{1,0:T(8,128)(2,1)S(1)} %constant_dynamic-update-slice_fusion.kv.k0), channel_id=1, source_target_pairs={{0,2},{1,3},{2,4},{3,5},{4,6},{5,7},{6,8},{7,9},{8,10},{9,11},{10,... | collective-permute-start | bytes 2359304 | tf_op jit(solution)/shard_map/ppermute | solution.py:247
  7.2 0.7 copy-start
  7.2 0.7 copy-start.1
  7.2 0.7 copy-start.2
  9.6 21.9 %collective-permute-start = (bf16[384,640]{1,0:T(8,128)(2,1)S(1)}, bf16[384,640]{1,0:T(8,128)(2,1)S(1)}, u32[]{:S(2)}, u32[]{:S(2)}) collective-permute-start(bf16[384,640]{1,0:T(8,128)(2,1)S(1)} %get-tuple-element.41.q.qa.q0.a0), channel_id=1, source_target_pairs={{1,0},{0,1},{3,2},{2,3},{5,4},{4,5},{7,6},{6,7},{9,8},{8,9},{11,10... | collective-permute-start | bytes 1474568 | tf_op jit(solution)/shard_map/ppermute | solution.py:250
  12.9 30.9 %collective-permute-start.4 = (bf16[384,640]{1,0:T(8,128)(2,1)S(1)}, bf16[384,640]{1,0:T(8,128)(2,1)S(1)}, u32[]{:S(2)}, u32[]{:S(2)}) collective-permute-start(bf16[384,640]{1,0:T(8,128)(2,1)S(1)} %get-tuple-element.41.q.qa.q0.a0), channel_id=1, source_target_pairs={{128,127},{256,255},{384,383}} | collective-permute-start | bytes 1474568 | tf_op jit(solution)/shard_map/ppermute | solution.py:264
  13.6 23.7 %collective-permute-start.2 = (bf16[384,512]{1,0:T(8,128)(2,1)}, bf16[384,512]{1,0:T(8,128)(2,1)}, u32[]{:S(2)}, u32[]{:S(2)}) collective-permute-start(bf16[384,512]{1,0:T(8,128)(2,1)} %get-tuple-element.46.q.q0), channel_id=1, source_target_pairs={{1,0},{0,1},{3,2},{2,3},{5,4},{4,5},{7,6},{6,7},{9,8},{8,9},{11,10... | collective-permute-start | bytes 1179656 | tf_op jit(solution)/shard_map/ppermute | solution.py:250
  25.1 40.9 %collective-permute-start.7 = (bf16[384,512]{1,0:T(8,128)(2,1)}, bf16[384,512]{1,0:T(8,128)(2,1)S(1)}, u32[]{:S(2)}, u32[]{:S(2)}) collective-permute-start(bf16[384,512]{1,0:T(8,128)(2,1)} %get-tuple-element.46.q.q0), channel_id=1, source_target_pairs={{128,127},{256,255},{384,383}} | collective-permute-start | bytes 1179656 | tf_op jit(solution)/shard_map/ppermute | solution.py:264
  31.5 12.2 %collective-permute-start.3 = (bf16[384,640]{1,0:T(8,128)(2,1)S(1)}, bf16[384,640]{1,0:T(8,128)(2,1)S(1)}, u32[]{:S(2)}, u32[]{:S(2)}) collective-permute-start(bf16[384,640]{1,0:T(8,128)(2,1)S(1)} %collective-permute-done.q1.a1), channel_id=1, source_target_pairs={{3,1},{5,3},{7,5},{9,7},{11,9},{13,11},{15,13},{17,15},{19,17},{21... | collective-permute-start | bytes 1474568 | tf_op jit(solution)/shard_map/ppermute | solution.py:247
  37.2 26.8 %collective-permute-start.5 = (bf16[384,512]{1,0:T(8,128)(2,1)}, bf16[384,512]{1,0:T(8,128)(2,1)S(1)}, u32[]{:S(2)}, u32[]{:S(2)}) collective-permute-start(bf16[384,512]{1,0:T(8,128)(2,1)} %collective-permute-done.2.q1), channel_id=1, source_target_pairs={{3,1},{5,3},{7,5},{9,7},{11,9},{13,11},{15,13},{17,15},{19,17},{21... | collective-permute-start | bytes 1179656 | tf_op jit(solution)/shard_map/ppermute | solution.py:247
  46.0 32.6 %collective-permute-start.9 = (bf16[384,512]{1,0:T(8,128)(2,1)S(1)}, bf16[384,512]{1,0:T(8,128)(2,1)S(1)}, u32[]{:S(2)}, u32[]{:S(2)}) collective-permute-start(bf16[384,512]{1,0:T(8,128)(2,1)S(1)} %get-tuple-element.69), channel_id=1, source_target_pairs={{2,0},{3,1},{4,2},{5,3},{6,4},{7,5},{8,6},{9,7},{10,8},{11,9},{12,... | collective-permute-start | bytes 1179656 | tf_op jit(solution)/shard_map/ppermute | solution.py:247
  64.0 17.9 %collective-permute-start.6 = (bf16[384,512]{1,0:T(8,128)(2,1)S(1)}, bf16[384,512]{1,0:T(8,128)(2,1)S(1)}, u32[]{:S(2)}, u32[]{:S(2)}) collective-permute-start(bf16[384,512]{1,0:T(8,128)(2,1)S(1)} %get-tuple-element.63), channel_id=1, source_target_pairs={{1,0},{0,1},{3,2},{2,3},{5,4},{4,5},{7,6},{6,7},{9,8},{8,9},{11,10... | collective-permute-start | bytes 1179656 | tf_op jit(solution)/shard_map/ppermute | solution.py:250
  68.2 18.0 %collective-permute-start.8 = (bf16[384,512]{1,0:T(8,128)(2,1)S(1)}, bf16[384,512]{1,0:T(8,128)(2,1)S(1)}, u32[]{:S(2)}, u32[]{:S(2)}) collective-permute-start(bf16[384,512]{1,0:T(8,128)(2,1)S(1)} %get-tuple-element.68), channel_id=1, source_target_pairs={{1,2},{3,4},{5,6},{7,8},{9,10},{11,12},{13,14},{15,16},{17,18},{19... | collective-permute-start | bytes 1179656 | tf_op jit(solution)/shard_map/ppermute | solution.py:312
  69.5 20.9 %collective-permute-start.10 = (bf16[384,512]{1,0:T(8,128)(2,1)S(1)}, bf16[384,512]{1,0:T(8,128)(2,1)S(1)}, u32[]{:S(2)}, u32[]{:S(2)}) collective-permute-start(bf16[384,512]{1,0:T(8,128)(2,1)S(1)} %get-tuple-element.74), channel_id=1, source_target_pairs={{2,0},{3,1},{4,2},{5,3},{6,4},{7,5},{8,6},{9,7},{10,8},{11,9},{12,... | collective-permute-start | bytes 1179656 | tf_op jit(solution)/shard_map/ppermute | solution.py:247

commit v4 on v3

--- a/solution.py
+++ b/solution.py
@@ -174,42 +174,45 @@
 
 
     base = 0
-    for part in before:
-        dq2[:, base : base + WC] = part[...]
-        base += WC
+    if before:
+        base = WC
+        dq2[:, :WC] = before[0][...]
+        out[:, : 2 * WC] = before[1][...]
 
     def body(hp, at, at2):
         to = pl.ds(pl.multiple_of(base + hp * PAIR, PAIR), PAIR)
+        to_k = pl.ds(pl.multiple_of(2 * base + hp * PAIR, PAIR), PAIR)
+        to_v = pl.ds(pl.multiple_of(2 * base + WC + hp * PAIR, PAIR), PAIR)
 
         @pl.when(odd[0] & 1 != 0)
         def _():
             x, y, z = tile(q2, a2[:, 2 * WC :], k1, c, hp, 3)
             dq2[:, to] = (x * 0.125).astype(bf16)
-            out[:, at] = ((dkv1[:, at] + y) * 0.125).astype(bf16)
-            out[:, at2] = (dkv1[:, at2] + z).astype(bf16)
+            out[:, to_k] = ((dkv1[:, at] + y) * 0.125).astype(bf16)
+            out[:, to_v] = (dkv1[:, at2] + z).astype(bf16)
 
         @pl.when(odd[0] & 1 == 0)
         def _():
             dq2[:, to] = jnp.zeros((dq2.shape[0], PAIR), bf16)
-            out[:, at] = (dkv1[:, at] * 0.125).astype(bf16)
-            out[:, at2] = dkv1[:, at2].astype(bf16)
+            out[:, to_k] = (dkv1[:, at] * 0.125).astype(bf16)
+            out[:, to_v] = dkv1[:, at2].astype(bf16)
 
     pairs(body)
 
 
-def first_sum(dq_a, dq_b, dkv, r1, r2, back, gq, gk, gv):
+def sum_q(dq_a, dq_b, r1, r2, gq):
     far = r1[...].astype(f32) + r2[...].astype(f32)
     gq[:, :WC] = (dq_a[...] * 0.125 + far[:, :WC]).astype(bf16)
     gq[:, WC:] = (dq_b[...] * 0.125 + far[:, WC:]).astype(bf16)
-    gk[...] = (dkv[:, :WC] * 0.125 + back[:, :WC].astype(f32)).astype(bf16)
-    gv[...] = (dkv[:, WC:] + back[:, WC:].astype(f32)).astype(bf16)
-
-
-def last_sum(pk, pv, dkv, back, gk, gv):
-    gk[:, :WC] = pk[...]
-    gv[:, :WC] = pv[...]
-    gk[:, WC:] = (dkv[:, :WC] * 0.125 + back[:, :WC].astype(f32)).astype(bf16)
-    gv[:, WC:] = (dkv[:, WC:] + back[:, WC:].astype(f32)).astype(bf16)
+
+
+def sum_kv(dkv_a, dkv_b, back, gk, gv):
+    for c, dkv in enumerate((dkv_a, dkv_b)):
+        w = slice(c * WC, (c + 1) * WC)
+        k_at = slice(2 * c * WC, (2 * c + 1) * WC)
+        v_at = slice((2 * c + 1) * WC, (2 * c + 2) * WC)
+        gk[:, w] = (dkv[:, :WC] * 0.125 + back[:, k_at].astype(f32)).astype(bf16)
+        gv[:, w] = (dkv[:, WC:] + back[:, v_at].astype(f32)).astype(bf16)
 
 
 VM = pl.BlockSpec(memory_space=pltpu.VMEM)
@@ -298,26 +301,19 @@
         dkv1 = parts[c]
         x, send, q2[c] = call(
             functools.partial(last_kernel, c),
-            [arr((c + 1) * WC, bf16), arr(2 * WC, bf16), arr(qw[c], bf16)],
+            [arr((c + 1) * WC, bf16), arr(2 * (c + 1) * WC, bf16), arr(qw[c], bf16)],
             1,
             (odd, q2[c], q2[0], k1, edge[c], dkv1, *dq2),
             flops=0,
             alias={1: 2},
         )
-        dq2 = (x,)
-        if c == 0:
-            dq1, dq2, q2[1] = lax.optimization_barrier((dq1, dq2, q2[1]))
-            back_q1 = swapped(dq1[0])
-        back_kv.append(shifted(send, -2))
-    back_q2 = lax.ppermute(dq2[0], AXES, [(i, i + 1) for i in range(1, n - 1, 2)])
-    gq, pk, pv = call(
-        first_sum,
-        [arr(HEADS * SIZE, bf16), arr(WC, bf16), arr(WC, bf16)],
-        0,
-        (*dqs, dkvs[0], back_q1, back_q2, back_kv[0]),
-        flops=20 << 30,
-    )
-    gk, gv = call(last_sum, [arr(HEADS * SIZE, bf16)] * 2, 0, (pk, pv, dkvs[1], back_kv[1]), flops=1 << 20)
+        dq2 = (x, send)
+    x, send, dq1 = lax.optimization_barrier((x, send, dq1))
+    r1 = swapped(dq1[0])
+    r2 = lax.ppermute(x, AXES, [(i, i + 1) for i in range(1, n - 1, 2)])
+    back = shifted(send, -2)
+    (gq,) = call(sum_q, [arr(HEADS * SIZE, bf16)], 0, (*dqs, r1, r2), flops=20 << 30)
+    gk, gv = call(sum_kv, [arr(HEADS * SIZE, bf16)] * 2, 0, (*dkvs, back), flops=1 << 20)
     return gq, gk, gv
 
 

time: 91.8 us -> 93.1 us (1.014)
  the two profiles are of different devices: /device:TPU:40 before, /device:TPU:48 now
where the time goes in v4:
time: 93.1 us; the launch traced here: 92.6 us
  starting transfers between devices  44.8 us (48%)
  Pallas kernels  22.9 us (25%)
  waiting for transfers between devices  21.2 us (23%)
  local copies, waits for them, and re-layouts  2.83 us (3%)
  between operations  0.94 us (1%)
    pallas_call x9, Pallas kernels, call(): pl.pallas_call(kernel, out_shape=outs, in_specs=[SM] * n_smem + [VM] * ne...  22.9 us
    ppermute x4, starting transfers between devices, shifted(): lax.ppermute(x, AXES, [(i - by, i) for i in range(n) if 0 <= i - by < n a...  21 us
    ppermute x4, waiting for transfers between devices, shifted(): lax.ppermute(x, AXES, [(i - by, i) for i in range(n) if 0 <= i - by < n a...  15.4 us
    ppermute x2, starting transfers between devices, per_device(): lax.ppermute(q0[c], AXES, [(s, s - 1) for s in edges])  12.7 us
    ppermute x3, starting transfers between devices, swapped(): return lax.ppermute(x, AXES, [(i ^ 1, i) for i in range(n)])  9.7 us
    ppermute x1, waiting for transfers between devices, per_device(): r2 = lax.ppermute(x, AXES, [(i, i + 1) for i in range(1, n - 1, 2)])  5.73 us
  transfers between devices with their start and end apart: 10, of which 3 were waited for; matrix products, arithmetic and copies ran while one was open for 0% of the time, Pallas kernels for 23%

profile of v4, /device:TPU:48, one launch (start us, length us, event | category | flops | bytes accessed | tf_op | source)
XLA Modules:
  0.0 92.6 jit_solution(4032536359095583311)
XLA Ops:
  0.7 1.1 %constant_dynamic-update-slice_fusion.1 = bf16[384,1024]{1,0:T(8,128)(2,1)S(1)} fusion(bf16[384,512]{1,0:T(8,128)(2,1)} %param.9), kind=kLoop, calls=%fused_computation.2 | loop fusion | bytes 786432
  1.8 1.0 %constant_dynamic-update-slice_fusion.kv.k0 = bf16[384,1024]{1,0:T(8,128)(2,1)S(1)} fusion(bf16[384,1024]{1,0:T(8,128)(2,1)S(1)} %constant_dynamic-update-slice_fusion.1, bf16[384,512]{1,0:T(8,128)(2,1)} %param.10), kind=kLoop, calls=%fused_computation.1 | loop fusion | bytes 786432 | tf_op jit(solution)/shard_map/concatenate | solution.py:257
  2.8 4.3 %collective-permute-start.1 = (bf16[384,1024]{1,0:T(8,128)(2,1)S(1)}, bf16[384,1024]{1,0:T(8,128)(2,1)S(1)}, u32[]{:S(2)}, u32[]{:S(2)}) collective-permute-start(bf16[384,1024]{1,0:T(8,128)(2,1)S(1)} %constant_dynamic-update-slice_fusion.kv.k0), channel_id=1, source_target_pairs={{0,2},{1,3},{2,4},{3,5},{4,6},{5,7},{6,8},{7,9},{8,10},{9,11},{10,... | collective-permute-start | bytes 2359304 | tf_op jit(solution)/shard_map/ppermute | solution.py:250
  7.2 0.0 copy-start
  7.2 0.0 copy-start.1
  7.2 0.0 copy-start.2
  7.2 0.1 pad_maximum_fusion.everything
  7.3 0.6 copy-done
  7.9 1.7 %shard_map.103 = (bf16[384,640]{1,0:T(8,128)(2,1)S(1)}, bf16[384,512]{1,0:T(8,128)(2,1)}, f32[8,384]{1,0:T(8,128)S(1)}) custom-call(s32[1]{0:T(128)} %bitcast.1.blk, s32[1,3]{1,0:T(1,128)S(1)} %copy-done.2, f32[8,384]{1,0:T(8,128)S(1)} %copy-done, s32[1,384]{1,0:T(1,128)S(1)} %copy-done.1, bf16[384,1536]{1,0:T(8,128)(2,1)S(1)} %pad_maximum_fusion.everything), custom_call_target="tpu_custom_call" | custom-call | bytes 1024 | tf_op jit(solution)/shard_map/pallas_call | solution.py:224
  9.6 2.6 %collective-permute-start = (bf16[384,640]{1,0:T(8,128)(2,1)S(1)}, bf16[384,640]{1,0:T(8,128)(2,1)S(1)}, u32[]{:S(2)}, u32[]{:S(2)}) collective-permute-start(bf16[384,640]{1,0:T(8,128)(2,1)S(1)} %get-tuple-element.38.q.qa.q0.a0), channel_id=1, source_target_pairs={{1,0},{0,1},{3,2},{2,3},{5,4},{4,5},{7,6},{6,7},{9,8},{8,9},{11,10... | collective-permute-start | bytes 1474568 | tf_op jit(solution)/shard_map/ppermute | solution.py:253
  12.2 11.4 %collective-permute-start.5 = (bf16[384,640]{1,0:T(8,128)(2,1)S(1)}, bf16[384,640]{1,0:T(8,128)(2,1)S(1)}, u32[]{:S(2)}, u32[]{:S(2)}) collective-permute-start(bf16[384,640]{1,0:T(8,128)(2,1)S(1)} %get-tuple-element.38.q.qa.q0.a0), channel_id=1, source_target_pairs={{128,127},{256,255},{384,383}} | collective-permute-start | bytes 1474568 | tf_op jit(solution)/shard_map/ppermute | solution.py:267
  23.6 1.9 %collective-permute-start.2 = (bf16[384,512]{1,0:T(8,128)(2,1)}, bf16[384,512]{1,0:T(8,128)(2,1)}, u32[]{:S(2)}, u32[]{:S(2)}) collective-permute-start(bf16[384,512]{1,0:T(8,128)(2,1)} %get-tuple-element.43.q.q0), channel_id=1, source_target_pairs={{1,0},{0,1},{3,2},{2,3},{5,4},{4,5},{7,6},{6,7},{9,8},{8,9},{11,10... | collective-permute-start | bytes 1179656 | tf_op jit(solution)/shard_map/ppermute | solution.py:253
  25.5 1.3 %collective-permute-start.6 = (bf16[384,512]{1,0:T(8,128)(2,1)}, bf16[384,512]{1,0:T(8,128)(2,1)S(1)}, u32[]{:S(2)}, u32[]{:S(2)}) collective-permute-start(bf16[384,512]{1,0:T(8,128)(2,1)} %get-tuple-element.43.q.q0), channel_id=1, source_target_pairs={{128,127},{256,255},{384,383}} | collective-permute-start | bytes 1179656 | tf_op jit(solution)/shard_map/ppermute | solution.py:267
  26.9 2.3 %shard_map.104 = (f32[384,256]{1,0:T(8,128)S(1)}, f32[384,512]{1,0:T(8,128)S(1)}) custom-call(bf16[384,640]{1,0:T(8,128)(2,1)S(1)} %get-tuple-element.38.q.qa.q0.a0, bf16[384,640]{1,0:T(8,128)(2,1)S(1)} %get-tuple-element.38.q.qa.q0.a0, bf16[384,1024]{1,0:T(8,128)(2,1)S(1)} %constant_dynamic-update-slice_fusion.kv.k0, f32[8,384]{1,0:T(8,128)S(1)} %get-tuple-element.40.rank), custom_call_target="tpu_custom_call" | custom-call | flops 3019898880 | bytes 1024 | tf_op jit(solution)/shard_map/pallas_call | solution.py:224
  29.2 3.3 %shard_map.105 = (f32[384,256]{1,0:T(8,128)S(1)}, f32[384,512]{1,0:T(8,128)S(1)}) custom-call(bf16[384,512]{1,0:T(8,128)(2,1)} %get-tuple-element.43.q.q0, bf16[384,640]{1,0:T(8,128)(2,1)S(1)} %get-tuple-element.38.q.qa.q0.a0, bf16[384,1024]{1,0:T(8,128)(2,1)S(1)} %constant_dynamic-update-slice_fusion.kv.k0, f32[8,384]{1,0:T(8,128)S(1)} %get-tuple-element.40.rank), custom_call_target="tpu_custom_call" | custom-call | flops 3019898880 | bytes 1024 | tf_op jit(solution)/shard_map/pallas_call | solution.py:224
  32.6 0.0 collective-permute-done.q1.a1
  32.6 0.7 collective-permute-start.4
  33.3 4.4 %collective-permute-done.1.k1 = bf16[384,1024]{1,0:T(8,128)(2,1)S(1)} collective-permute-done((bf16[384,1024]{1,0:T(8,128)(2,1)S(1)}, bf16[384,1024]{1,0:T(8,128)(2,1)S(1)}, u32[]{:S(2)}, u32[]{:S(2)}) %collective-permute-start.1) | collective-permute-done | bytes 786464 | tf_op jit(solution)/shard_map/ppermute | solution.py:250
  37.7 6.1 %shard_map.106 = (f32[384,256]{1,0:T(8,128)S(1)}, f32[384,512]{1,0:T(8,128)S(1)}, bf16[384,256]{1,0:T(8,128)(2,1)S(1)}, f32[384,512]{1,0:T(8,128)S(1)}) custom-call(s32[1]{0:T(128)} %bitcast.odd, bf16[384,640]{1,0:T(8,128)(2,1)S(1)} %get-tuple-element.38.q.qa.q0.a0, bf16[384,640]{1,0:T(8,128)(2,1)S(1)} %get-tuple-element.38.q.qa.q0.a0, ...), custom_call_target="tpu_custom_call" | custom-call | flops 9059696640 | bytes 1024 | tf_op jit(solution)/shard_map/pallas_call | solution.py:224
  43.7 0.7 collective-permute-start.3
  44.4 7.2 %shard_map.107 = (f32[384,256]{1,0:T(8,128)S(1)}, f32[384,512]{1,0:T(8,128)S(1)}, bf16[384,512]{1,0:T(8,128)(2,1)S(1)}, f32[384,512]{1,0:T(8,128)S(1)}) custom-call(s32[1]{0:T(128)} %bitcast.odd, bf16[384,512]{1,0:T(8,128)(2,1)} %get-tuple-element.43.q.q0, bf16[384,640]{1,0:T(8,128)(2,1)S(1)} %get-tuple-element.38.q.qa.q0.a0, ...), custom_call_target="tpu_custom_call" | custom-call | flops 9059696640 | bytes 1024 | tf_op jit(solution)/shard_map/pallas_call | solution.py:224
  51.6 0.0 collective-permute-done.4.a2_far
  51.7 0.2 shard_map.108
  51.9 0.0 collective-permute-done.6.edge
  51.9 0.2 shard_map.109
  52.1 5.2 %collective-permute-start.7 = (bf16[384,512]{1,0:T(8,128)(2,1)S(1)}, bf16[384,512]{1,0:T(8,128)(2,1)S(1)}, u32[]{:S(2)}, u32[]{:S(2)}) collective-permute-start(bf16[384,512]{1,0:T(8,128)(2,1)S(1)} %get-tuple-element.64), channel_id=1, source_target_pairs={{1,0},{0,1},{3,2},{2,3},{5,4},{4,5},{7,6},{6,7},{9,8},{8,9},{11,10... | collective-permute-start | bytes 1179656 | tf_op jit(solution)/shard_map/ppermute | solution.py:253
  57.3 1.3 %collective-permute-start.8 = (bf16[384,512]{1,0:T(8,128)(2,1)S(1)}, bf16[384,512]{1,0:T(8,128)(2,1)S(1)}, u32[]{:S(2)}, u32[]{:S(2)}) collective-permute-start(bf16[384,512]{1,0:T(8,128)(2,1)S(1)} %get-tuple-element.65), channel_id=1, source_target_pairs={{1,2},{3,4},{5,6},{7,8},{9,10},{11,12},{13,14},{15,16},{17,18},{19... | collective-permute-start | bytes 1179656 | tf_op jit(solution)/shard_map/ppermute | solution.py:313
  58.6 15.4 %collective-permute-start.9 = (bf16[384,1024]{1,0:T(8,128)(2,1)S(1)}, bf16[384,1024]{1,0:T(8,128)(2,1)S(1)}, u32[]{:S(2)}, u32[]{:S(2)}) collective-permute-start(bf16[384,1024]{1,0:T(8,128)(2,1)S(1)} %get-tuple-element.68), channel_id=1, source_target_pairs={{2,0},{3,1},{4,2},{5,3},{6,4},{7,5},{8,6},{9,7},{10,8},{11,9},{12,... | collective-permute-start | bytes 2359304 | tf_op jit(solution)/shard_map/ppermute | solution.py:250
  74.0 5.7 %collective-permute-done.8.r2 = bf16[384,512]{1,0:T(8,128)(2,1)S(1)} collective-permute-done((bf16[384,512]{1,0:T(8,128)(2,1)S(1)}, bf16[384,512]{1,0:T(8,128)(2,1)S(1)}, u32[]{:S(2)}, u32[]{:S(2)}) %collective-permute-start.8) | collective-permute-done | bytes 393248 | tf_op jit(solution)/shard_map/ppermute | solution.py:313
  79.7 0.9 shard_map.110
  80.6 11.0 %collective-permute-done.9.back = bf16[384,1024]{1,0:T(8,128)(2,1)S(1)} collective-permute-done((bf16[384,1024]{1,0:T(8,128)(2,1)S(1)}, bf16[384,1024]{1,0:T(8,128)(2,1)S(1)}, u32[]{:S(2)}, u32[]{:S(2)}) %collective-permute-start.9) | collective-permute-done | bytes 786464 | tf_op jit(solution)/shard_map/ppermute | solution.py:250
  91.6 1.0 %shard_map.111 = (bf16[384,512]{1,0:T(8,128)(2,1)}, bf16[384,512]{1,0:T(8,128)(2,1)}) custom-call(f32[384,512]{1,0:T(8,128)S(1)} %get-tuple-element.66.dkv_a, f32[384,512]{1,0:T(8,128)S(1)} %get-tuple-element.67.dkv_b, bf16[384,1024]{1,0:T(8,128)(2,1)S(1)} %collective-permute-done.9.back), custom_call_target="tpu_custom_call" | custom-call | flops 1048576 | bytes 1024 | tf_op jit(solution)/shard_map/pallas_call | solution.py:224
  (13 shorter events, 0.1 us)
Async XLA Ops:
  0.6 6.5 %copy-start.5 = (bf16[384,512]{1,0:T(8,128)(2,1)S(1)}, bf16[384,512]{1,0:T(8,128)(2,1)}, u32[]{:S(2)}) copy-start(bf16[384,512]{1,0:T(8,128)(2,1)} %param.8) | copy-start | bytes 1179652
  0.6 6.5 %copy-start.3 = (bf16[384,512]{1,0:T(8,128)(2,1)S(1)}, bf16[384,512]{1,0:T(8,128)(2,1)}, u32[]{:S(2)}) copy-start(bf16[384,512]{1,0:T(8,128)(2,1)} %param.11) | copy-start | bytes 1179652
  0.7 6.5 %copy-start.4 = (bf16[384,512]{1,0:T(8,128)(2,1)S(1)}, bf16[384,512]{1,0:T(8,128)(2,1)}, u32[]{:S(2)}) copy-start(bf16[384,512]{1,0:T(8,128)(2,1)} %param.12) | copy-start | bytes 1179652
  2.8 34.8 %collective-permute-start.1 = (bf16[384,1024]{1,0:T(8,128)(2,1)S(1)}, bf16[384,1024]{1,0:T(8,128)(2,1)S(1)}, u32[]{:S(2)}, u32[]{:S(2)}) collective-permute-start(bf16[384,1024]{1,0:T(8,128)(2,1)S(1)} %constant_dynamic-update-slice_fusion.kv.k0), channel_id=1, source_target_pairs={{0,2},{1,3},{2,4},{3,5},{4,6},{5,7},{6,8},{7,9},{8,10},{9,11},{10,... | collective-permute-start | bytes 2359304 | tf_op jit(solution)/shard_map/ppermute | solution.py:250
  7.2 0.7 copy-start
  7.2 0.7 copy-start.1
  7.2 0.7 copy-start.2
  9.6 23.0 %collective-permute-start = (bf16[384,640]{1,0:T(8,128)(2,1)S(1)}, bf16[384,640]{1,0:T(8,128)(2,1)S(1)}, u32[]{:S(2)}, u32[]{:S(2)}) collective-permute-start(bf16[384,640]{1,0:T(8,128)(2,1)S(1)} %get-tuple-element.38.q.qa.q0.a0), channel_id=1, source_target_pairs={{1,0},{0,1},{3,2},{2,3},{5,4},{4,5},{7,6},{6,7},{9,8},{8,9},{11,10... | collective-permute-start | bytes 1474568 | tf_op jit(solution)/shard_map/ppermute | solution.py:253
  12.2 39.5 %collective-permute-start.5 = (bf16[384,640]{1,0:T(8,128)(2,1)S(1)}, bf16[384,640]{1,0:T(8,128)(2,1)S(1)}, u32[]{:S(2)}, u32[]{:S(2)}) collective-permute-start(bf16[384,640]{1,0:T(8,128)(2,1)S(1)} %get-tuple-element.38.q.qa.q0.a0), channel_id=1, source_target_pairs={{128,127},{256,255},{384,383}} | collective-permute-start | bytes 1474568 | tf_op jit(solution)/shard_map/ppermute | solution.py:267
  23.6 20.1 %collective-permute-start.2 = (bf16[384,512]{1,0:T(8,128)(2,1)}, bf16[384,512]{1,0:T(8,128)(2,1)}, u32[]{:S(2)}, u32[]{:S(2)}) collective-permute-start(bf16[384,512]{1,0:T(8,128)(2,1)} %get-tuple-element.43.q.q0), channel_id=1, source_target_pairs={{1,0},{0,1},{3,2},{2,3},{5,4},{4,5},{7,6},{6,7},{9,8},{8,9},{11,10... | collective-permute-start | bytes 1179656 | tf_op jit(solution)/shard_map/ppermute | solution.py:253
  25.5 26.3 %collective-permute-start.6 = (bf16[384,512]{1,0:T(8,128)(2,1)}, bf16[384,512]{1,0:T(8,128)(2,1)S(1)}, u32[]{:S(2)}, u32[]{:S(2)}) collective-permute-start(bf16[384,512]{1,0:T(8,128)(2,1)} %get-tuple-element.43.q.q0), channel_id=1, source_target_pairs={{128,127},{256,255},{384,383}} | collective-permute-start | bytes 1179656 | tf_op jit(solution)/shard_map/ppermute | solution.py:267
  32.6 19.0 %collective-permute-start.4 = (bf16[384,640]{1,0:T(8,128)(2,1)S(1)}, bf16[384,640]{1,0:T(8,128)(2,1)S(1)}, u32[]{:S(2)}, u32[]{:S(2)}) collective-permute-start(bf16[384,640]{1,0:T(8,128)(2,1)S(1)} %collective-permute-done.q1.a1), channel_id=1, source_target_pairs={{3,1},{5,3},{7,5},{9,7},{11,9},{13,11},{15,13},{17,15},{19,17},{21... | collective-permute-start | bytes 1474568 | tf_op jit(solution)/shard_map/ppermute | solution.py:250
  43.7 8.1 %collective-permute-start.3 = (bf16[384,512]{1,0:T(8,128)(2,1)}, bf16[384,512]{1,0:T(8,128)(2,1)S(1)}, u32[]{:S(2)}, u32[]{:S(2)}) collective-permute-start(bf16[384,512]{1,0:T(8,128)(2,1)} %collective-permute-done.2.q1), channel_id=1, source_target_pairs={{3,1},{5,3},{7,5},{9,7},{11,9},{13,11},{15,13},{17,15},{19,17},{21... | collective-permute-start | bytes 1179656 | tf_op jit(solution)/shard_map/ppermute | solution.py:250
  52.1 21.9 %collective-permute-start.7 = (bf16[384,512]{1,0:T(8,128)(2,1)S(1)}, bf16[384,512]{1,0:T(8,128)(2,1)S(1)}, u32[]{:S(2)}, u32[]{:S(2)}) collective-permute-start(bf16[384,512]{1,0:T(8,128)(2,1)S(1)} %get-tuple-element.64), channel_id=1, source_target_pairs={{1,0},{0,1},{3,2},{2,3},{5,4},{4,5},{7,6},{6,7},{9,8},{8,9},{11,10... | collective-permute-start | bytes 1179656 | tf_op jit(solution)/shard_map/ppermute | solution.py:253
  57.3 22.4 %collective-permute-start.8 = (bf16[384,512]{1,0:T(8,128)(2,1)S(1)}, bf16[384,512]{1,0:T(8,128)(2,1)S(1)}, u32[]{:S(2)}, u32[]{:S(2)}) collective-permute-start(bf16[384,512]{1,0:T(8,128)(2,1)S(1)} %get-tuple-element.65), channel_id=1, source_target_pairs={{1,2},{3,4},{5,6},{7,8},{9,10},{11,12},{13,14},{15,16},{17,18},{19... | collective-permute-start | bytes 1179656 | tf_op jit(solution)/shard_map/ppermute | solution.py:313
  58.6 33.0 %collective-permute-start.9 = (bf16[384,1024]{1,0:T(8,128)(2,1)S(1)}, bf16[384,1024]{1,0:T(8,128)(2,1)S(1)}, u32[]{:S(2)}, u32[]{:S(2)}) collective-permute-start(bf16[384,1024]{1,0:T(8,128)(2,1)S(1)} %get-tuple-element.68), channel_id=1, source_target_pairs={{2,0},{3,1},{4,2},{5,3},{6,4},{7,5},{8,6},{9,7},{10,8},{11,9},{12,... | collective-permute-start | bytes 2359304 | tf_op jit(solution)/shard_map/ppermute | solution.py:250

commit v5 on v3

--- a/solution.py
+++ b/solution.py
@@ -306,7 +306,7 @@
         )
         dq2 = (x,)
         if c == 0:
-            dq1, dq2, q2[1] = lax.optimization_barrier((dq1, dq2, q2[1]))
+            dq1, dq2 = lax.optimization_barrier((dq1, dq2))
             back_q1 = swapped(dq1[0])
         back_kv.append(shifted(send, -2))
     back_q2 = lax.ppermute(dq2[0], AXES, [(i, i + 1) for i in range(1, n - 1, 2)])

time: 91.8 us -> 89.5 us (0.975)
  waiting for transfers between devices: 11.3 us -> 9.34 us
    ppermute x5, starting transfers between devices: 34 us -> 29.1 us  [shifted(): lax.ppermute(x, AXES, [(i - by, i) for i in range(n) if 0 <= i - by < n a...]
    ppermute x3, starting transfers between devices: 16.7 us -> 21.3 us  [swapped(): return lax.ppermute(x, AXES, [(i ^ 1, i) for i in range(n)])]
    ppermute x3, waiting for transfers between devices: 3.34 us -> 0.01 us  [swapped(): return lax.ppermute(x, AXES, [(i ^ 1, i) for i in range(n)])]
    ppermute x5, waiting for transfers between devices: 3.79 us -> 5.18 us  [shifted(): lax.ppermute(x, AXES, [(i - by, i) for i in range(n) if 0 <= i - by < n a...]
  transfers between devices with their start and end apart: 11 -> 11, of which waited for: 4 -> 3; matrix products, arithmetic and copies ran while one was open for 0% -> 0% of each run, Pallas kernels for 24% -> 24%
where the time goes in v5:
time: 89.5 us; the launch traced here: 89.1 us
  starting transfers between devices  53.1 us (59%)
  Pallas kernels  22.8 us (25%)
  waiting for transfers between devices  9.34 us (10%)
  local copies, waits for them, and re-layouts  2.83 us (3%)
  between operations  0.96 us (1%)
    ppermute x5, starting transfers between devices, shifted(): lax.ppermute(x, AXES, [(i - by, i) for i in range(n) if 0 <= i - by < n a...  29.1 us
    pallas_call x9, Pallas kernels, call(): pl.pallas_call(kernel, out_shape=outs, in_specs=[SM] * n_smem + [VM] * ne...  22.8 us
    ppermute x3, starting transfers between devices, swapped(): return lax.ppermute(x, AXES, [(i ^ 1, i) for i in range(n)])  21.3 us
    ppermute x5, waiting for transfers between devices, shifted(): lax.ppermute(x, AXES, [(i - by, i) for i in range(n) if 0 <= i - by < n a...  5.18 us
    ppermute x1, waiting for transfers between devices, per_device(): lax.ppermute(dq2[0], AXES, [(i, i + 1) for i in range(1, n - 1, 2)])  4.14 us
  transfers between devices with their start and end apart: 11, of which 3 were waited for; matrix products, arithmetic and copies ran while one was open for 0% of the time, Pallas kernels for 24%

profile of v5, /device:TPU:40, one launch (start us, length us, event | category | flops | bytes accessed | tf_op | source)
XLA Modules:
  0.0 89.1 jit_solution(13060543867936302647)
XLA Ops:
  0.7 1.1 %constant_dynamic-update-slice_fusion.1 = bf16[384,1024]{1,0:T(8,128)(2,1)S(1)} fusion(bf16[384,512]{1,0:T(8,128)(2,1)} %param.9), kind=kLoop, calls=%fused_computation.2 | loop fusion | bytes 786432
  1.8 1.0 %constant_dynamic-update-slice_fusion.kv.k0 = bf16[384,1024]{1,0:T(8,128)(2,1)S(1)} fusion(bf16[384,1024]{1,0:T(8,128)(2,1)S(1)} %constant_dynamic-update-slice_fusion.1, bf16[384,512]{1,0:T(8,128)(2,1)} %param.10), kind=kLoop, calls=%fused_computation.1 | loop fusion | bytes 786432 | tf_op jit(solution)/shard_map/concatenate | solution.py:254
  2.8 4.3 %collective-permute-start.1 = (bf16[384,1024]{1,0:T(8,128)(2,1)S(1)}, bf16[384,1024]{1,0:T(8,128)(2,1)S(1)}, u32[]{:S(2)}, u32[]{:S(2)}) collective-permute-start(bf16[384,1024]{1,0:T(8,128)(2,1)S(1)} %constant_dynamic-update-slice_fusion.kv.k0), channel_id=1, source_target_pairs={{0,2},{1,3},{2,4},{3,5},{4,6},{5,7},{6,8},{7,9},{8,10},{9,11},{10,... | collective-permute-start | bytes 2359304 | tf_op jit(solution)/shard_map/ppermute | solution.py:247
  7.2 0.0 copy-start
  7.2 0.0 copy-start.1
  7.2 0.0 copy-start.2
  7.2 0.1 pad_maximum_fusion.everything
  7.3 0.6 copy-done
  7.9 1.7 %shard_map.103 = (bf16[384,640]{1,0:T(8,128)(2,1)S(1)}, bf16[384,512]{1,0:T(8,128)(2,1)}, f32[8,384]{1,0:T(8,128)S(1)}) custom-call(s32[1]{0:T(128)} %bitcast.1.blk, s32[1,3]{1,0:T(1,128)S(1)} %copy-done.2, f32[8,384]{1,0:T(8,128)S(1)} %copy-done, s32[1,384]{1,0:T(1,128)S(1)} %copy-done.1, bf16[384,1536]{1,0:T(8,128)(2,1)S(1)} %pad_maximum_fusion.everything), custom_call_target="tpu_custom_call" | custom-call | bytes 1024 | tf_op jit(solution)/shard_map/pallas_call | solution.py:221
  9.6 3.2 %collective-permute-start = (bf16[384,640]{1,0:T(8,128)(2,1)S(1)}, bf16[384,640]{1,0:T(8,128)(2,1)S(1)}, u32[]{:S(2)}, u32[]{:S(2)}) collective-permute-start(bf16[384,640]{1,0:T(8,128)(2,1)S(1)} %get-tuple-element.40.q.qa.q0.a0), channel_id=1, source_target_pairs={{1,0},{0,1},{3,2},{2,3},{5,4},{4,5},{7,6},{6,7},{9,8},{8,9},{11,10... | collective-permute-start | bytes 1474568 | tf_op jit(solution)/shard_map/ppermute | solution.py:250
  12.9 0.7 collective-permute-start.4
  13.6 11.5 %collective-permute-start.2 = (bf16[384,512]{1,0:T(8,128)(2,1)}, bf16[384,512]{1,0:T(8,128)(2,1)}, u32[]{:S(2)}, u32[]{:S(2)}) collective-permute-start(bf16[384,512]{1,0:T(8,128)(2,1)} %get-tuple-element.45.q.q0), channel_id=1, source_target_pairs={{1,0},{0,1},{3,2},{2,3},{5,4},{4,5},{7,6},{6,7},{9,8},{8,9},{11,10... | collective-permute-start | bytes 1179656 | tf_op jit(solution)/shard_map/ppermute | solution.py:250
  25.1 0.7 collective-permute-start.7
  25.8 2.3 %shard_map.104 = (f32[384,256]{1,0:T(8,128)S(1)}, f32[384,512]{1,0:T(8,128)S(1)}) custom-call(bf16[384,640]{1,0:T(8,128)(2,1)S(1)} %get-tuple-element.40.q.qa.q0.a0, bf16[384,640]{1,0:T(8,128)(2,1)S(1)} %get-tuple-element.40.q.qa.q0.a0, bf16[384,1024]{1,0:T(8,128)(2,1)S(1)} %constant_dynamic-update-slice_fusion.kv.k0, f32[8,384]{1,0:T(8,128)S(1)} %get-tuple-element.42.rank), custom_call_target="tpu_custom_call" | custom-call | flops 3019898880 | bytes 1024 | tf_op jit(solution)/shard_map/pallas_call | solution.py:221
  28.1 3.3 %shard_map.105 = (f32[384,256]{1,0:T(8,128)S(1)}, f32[384,512]{1,0:T(8,128)S(1)}) custom-call(bf16[384,512]{1,0:T(8,128)(2,1)} %get-tuple-element.45.q.q0, bf16[384,640]{1,0:T(8,128)(2,1)S(1)} %get-tuple-element.40.q.qa.q0.a0, bf16[384,1024]{1,0:T(8,128)(2,1)S(1)} %constant_dynamic-update-slice_fusion.kv.k0, f32[8,384]{1,0:T(8,128)S(1)} %get-tuple-element.42.rank), custom_call_target="tpu_custom_call" | custom-call | flops 3019898880 | bytes 1024 | tf_op jit(solution)/shard_map/pallas_call | solution.py:221
  31.5 1.3 %collective-permute-start.3 = (bf16[384,640]{1,0:T(8,128)(2,1)S(1)}, bf16[384,640]{1,0:T(8,128)(2,1)S(1)}, u32[]{:S(2)}, u32[]{:S(2)}) collective-permute-start(bf16[384,640]{1,0:T(8,128)(2,1)S(1)} %collective-permute-done.q1.a1), channel_id=1, source_target_pairs={{3,1},{5,3},{7,5},{9,7},{11,9},{13,11},{15,13},{17,15},{19,17},{21... | collective-permute-start | bytes 1474568 | tf_op jit(solution)/shard_map/ppermute | solution.py:247
  32.8 0.5 collective-permute-done.1.k1
  33.2 4.0 %shard_map.106 = (f32[384,256]{1,0:T(8,128)S(1)}, f32[384,512]{1,0:T(8,128)S(1)}, bf16[384,256]{1,0:T(8,128)(2,1)S(1)}, f32[384,512]{1,0:T(8,128)S(1)}) custom-call(s32[1]{0:T(128)} %bitcast.odd, bf16[384,640]{1,0:T(8,128)(2,1)S(1)} %get-tuple-element.40.q.qa.q0.a0, bf16[384,640]{1,0:T(8,128)(2,1)S(1)} %get-tuple-element.40.q.qa.q0.a0, ...), custom_call_target="tpu_custom_call" | custom-call | flops 9059696640 | bytes 1024 | tf_op jit(solution)/shard_map/pallas_call | solution.py:221
  37.2 0.0 collective-permute-done.2.q1
  37.2 1.3 %collective-permute-start.6 = (bf16[384,512]{1,0:T(8,128)(2,1)}, bf16[384,512]{1,0:T(8,128)(2,1)S(1)}, u32[]{:S(2)}, u32[]{:S(2)}) collective-permute-start(bf16[384,512]{1,0:T(8,128)(2,1)} %collective-permute-done.2.q1), channel_id=1, source_target_pairs={{3,1},{5,3},{7,5},{9,7},{11,9},{13,11},{15,13},{17,15},{19,17},{21... | collective-permute-start | bytes 1179656 | tf_op jit(solution)/shard_map/ppermute | solution.py:247
  38.5 5.1 %shard_map.107 = (f32[384,256]{1,0:T(8,128)S(1)}, f32[384,512]{1,0:T(8,128)S(1)}, bf16[384,512]{1,0:T(8,128)(2,1)S(1)}, f32[384,512]{1,0:T(8,128)S(1)}) custom-call(s32[1]{0:T(128)} %bitcast.odd, bf16[384,512]{1,0:T(8,128)(2,1)} %get-tuple-element.45.q.q0, bf16[384,640]{1,0:T(8,128)(2,1)S(1)} %get-tuple-element.40.q.qa.q0.a0, ...), custom_call_target="tpu_custom_call" | custom-call | flops 9059696640 | bytes 1024 | tf_op jit(solution)/shard_map/pallas_call | solution.py:221
  43.7 0.0 collective-permute-done.4.edge
  43.7 2.2 %shard_map.108 = (bf16[384,256]{1,0:T(8,128)(2,1)S(1)}, bf16[384,512]{1,0:T(8,128)(2,1)S(1)}, bf16[384,640]{1,0:T(8,128)(2,1)S(1)}) custom-call(s32[1]{0:T(128)} %bitcast.odd, bf16[384,640]{1,0:T(8,128)(2,1)S(1)} %copy.14.q2_far, bf16[384,640]{1,0:T(8,128)(2,1)S(1)} %collective-permute-done.3.a2_far, ...), custom_call_target="tpu_custom_call", output_to_operand_aliasing={{2}: (1, {})} | custom-call | bytes 1024 | tf_op jit(solution)/shard_map/pallas_call | solution.py:221
  46.0 6.5 %collective-permute-start.5 = (bf16[384,512]{1,0:T(8,128)(2,1)S(1)}, bf16[384,512]{1,0:T(8,128)(2,1)S(1)}, u32[]{:S(2)}, u32[]{:S(2)}) collective-permute-start(bf16[384,512]{1,0:T(8,128)(2,1)S(1)} %get-tuple-element.62), channel_id=1, source_target_pairs={{1,0},{0,1},{3,2},{2,3},{5,4},{4,5},{7,6},{6,7},{9,8},{8,9},{11,10... | collective-permute-start | bytes 1179656 | tf_op jit(solution)/shard_map/ppermute | solution.py:250
  52.5 13.5 %collective-permute-start.9 = (bf16[384,512]{1,0:T(8,128)(2,1)S(1)}, bf16[384,512]{1,0:T(8,128)(2,1)S(1)}, u32[]{:S(2)}, u32[]{:S(2)}) collective-permute-start(bf16[384,512]{1,0:T(8,128)(2,1)S(1)} %get-tuple-element.67), channel_id=1, source_target_pairs={{2,0},{3,1},{4,2},{5,3},{6,4},{7,5},{8,6},{9,7},{10,8},{11,9},{12,... | collective-permute-start | bytes 1179656 | tf_op jit(solution)/shard_map/ppermute | solution.py:247
  66.0 2.2 %shard_map.109 = (bf16[384,512]{1,0:T(8,128)(2,1)S(1)}, bf16[384,512]{1,0:T(8,128)(2,1)S(1)}, bf16[384,512]{1,0:T(8,128)(2,1)S(1)}) custom-call(s32[1]{0:T(128)} %bitcast.odd, bf16[384,512]{1,0:T(8,128)(2,1)S(1)} %collective-permute-done.6.q2_far, bf16[384,640]{1,0:T(8,128)(2,1)S(1)} %get-tuple-element.63.a2_far, ...), custom_call_target="tpu_custom_call", output_to_operand_aliasing={{2}: (1, {})} | custom-call | bytes 1024 | tf_op jit(solution)/shard_map/pallas_call | solution.py:221
  68.2 1.3 %collective-permute-start.8 = (bf16[384,512]{1,0:T(8,128)(2,1)S(1)}, bf16[384,512]{1,0:T(8,128)(2,1)S(1)}, u32[]{:S(2)}, u32[]{:S(2)}) collective-permute-start(bf16[384,512]{1,0:T(8,128)(2,1)S(1)} %get-tuple-element.66), channel_id=1, source_target_pairs={{1,2},{3,4},{5,6},{7,8},{9,10},{11,12},{13,14},{15,16},{17,18},{19... | collective-permute-start | bytes 1179656 | tf_op jit(solution)/shard_map/ppermute | solution.py:312
  69.5 8.8 %collective-permute-start.10 = (bf16[384,512]{1,0:T(8,128)(2,1)S(1)}, bf16[384,512]{1,0:T(8,128)(2,1)S(1)}, u32[]{:S(2)}, u32[]{:S(2)}) collective-permute-start(bf16[384,512]{1,0:T(8,128)(2,1)S(1)} %get-tuple-element.72), channel_id=1, source_target_pairs={{2,0},{3,1},{4,2},{5,3},{6,4},{7,5},{8,6},{9,7},{10,8},{11,9},{12,... | collective-permute-start | bytes 1179656 | tf_op jit(solution)/shard_map/ppermute | solution.py:247
  78.4 4.1 %collective-permute-done.8.r2 = bf16[384,512]{1,0:T(8,128)(2,1)S(1)} collective-permute-done((bf16[384,512]{1,0:T(8,128)(2,1)S(1)}, bf16[384,512]{1,0:T(8,128)(2,1)S(1)}, u32[]{:S(2)}, u32[]{:S(2)}) %collective-permute-start.8) | collective-permute-done | bytes 393248 | tf_op jit(solution)/shard_map/ppermute | solution.py:312
  82.5 0.9 %shard_map.110 = (bf16[384,512]{1,0:T(8,128)(2,1)}, bf16[384,256]{1,0:T(8,128)(2,1)S(1)}, bf16[384,256]{1,0:T(8,128)(2,1)S(1)}) custom-call(f32[384,256]{1,0:T(8,128)S(1)} %get-tuple-element.51.dq_a, f32[384,256]{1,0:T(8,128)S(1)} %get-tuple-element.57.dq_b, f32[384,512]{1,0:T(8,128)S(1)} %get-tuple-element.58.dkv, ...), custom_call_target="tpu_custom_call" | custom-call | flops 21474836480 | bytes 1024 | tf_op jit(solution)/shard_map/pallas_call | solution.py:221
  83.4 4.7 %collective-permute-done.10.back = bf16[384,512]{1,0:T(8,128)(2,1)S(1)} collective-permute-done((bf16[384,512]{1,0:T(8,128)(2,1)S(1)}, bf16[384,512]{1,0:T(8,128)(2,1)S(1)}, u32[]{:S(2)}, u32[]{:S(2)}) %collective-permute-start.10) | collective-permute-done | bytes 393248 | tf_op jit(solution)/shard_map/ppermute | solution.py:247
  88.1 1.0 %shard_map.111 = (bf16[384,512]{1,0:T(8,128)(2,1)}, bf16[384,512]{1,0:T(8,128)(2,1)}) custom-call(bf16[384,256]{1,0:T(8,128)(2,1)S(1)} %get-tuple-element.69.pk, bf16[384,256]{1,0:T(8,128)(2,1)S(1)} %get-tuple-element.70.pv, f32[384,512]{1,0:T(8,128)S(1)} %get-tuple-element.71.dkv, bf16[384,512]{1,0:T(8,128)(2,1)S(1)} %collective-permute-done.10.back), custom_call_target="tpu_custom_call" | custom-call | flops 1048576 | bytes 1024 | tf_op jit(solution)/shard_map/pallas_call | solution.py:221
  (15 shorter events, 0.1 us)
Async XLA Ops:
  0.6 6.5 %copy-start.5 = (bf16[384,512]{1,0:T(8,128)(2,1)S(1)}, bf16[384,512]{1,0:T(8,128)(2,1)}, u32[]{:S(2)}) copy-start(bf16[384,512]{1,0:T(8,128)(2,1)} %param.8) | copy-start | bytes 1179652
  0.6 6.5 %copy-start.3 = (bf16[384,512]{1,0:T(8,128)(2,1)S(1)}, bf16[384,512]{1,0:T(8,128)(2,1)}, u32[]{:S(2)}) copy-start(bf16[384,512]{1,0:T(8,128)(2,1)} %param.11) | copy-start | bytes 1179652
  0.7 6.5 %copy-start.4 = (bf16[384,512]{1,0:T(8,128)(2,1)S(1)}, bf16[384,512]{1,0:T(8,128)(2,1)}, u32[]{:S(2)}) copy-start(bf16[384,512]{1,0:T(8,128)(2,1)} %param.12) | copy-start | bytes 1179652
  2.8 30.4 %collective-permute-start.1 = (bf16[384,1024]{1,0:T(8,128)(2,1)S(1)}, bf16[384,1024]{1,0:T(8,128)(2,1)S(1)}, u32[]{:S(2)}, u32[]{:S(2)}) collective-permute-start(bf16[384,1024]{1,0:T(8,128)(2,1)S(1)} %constant_dynamic-update-slice_fusion.kv.k0), channel_id=1, source_target_pairs={{0,2},{1,3},{2,4},{3,5},{4,6},{5,7},{6,8},{7,9},{8,10},{9,11},{10,... | collective-permute-start | bytes 2359304 | tf_op jit(solution)/shard_map/ppermute | solution.py:247
  7.2 0.7 copy-start
  7.2 0.7 copy-start.1
  7.2 0.7 copy-start.2
  9.6 21.9 %collective-permute-start = (bf16[384,640]{1,0:T(8,128)(2,1)S(1)}, bf16[384,640]{1,0:T(8,128)(2,1)S(1)}, u32[]{:S(2)}, u32[]{:S(2)}) collective-permute-start(bf16[384,640]{1,0:T(8,128)(2,1)S(1)} %get-tuple-element.40.q.qa.q0.a0), channel_id=1, source_target_pairs={{1,0},{0,1},{3,2},{2,3},{5,4},{4,5},{7,6},{6,7},{9,8},{8,9},{11,10... | collective-permute-start | bytes 1474568 | tf_op jit(solution)/shard_map/ppermute | solution.py:250
  12.9 30.9 %collective-permute-start.4 = (bf16[384,640]{1,0:T(8,128)(2,1)S(1)}, bf16[384,640]{1,0:T(8,128)(2,1)S(1)}, u32[]{:S(2)}, u32[]{:S(2)}) collective-permute-start(bf16[384,640]{1,0:T(8,128)(2,1)S(1)} %get-tuple-element.40.q.qa.q0.a0), channel_id=1, source_target_pairs={{128,127},{256,255},{384,383}} | collective-permute-start | bytes 1474568 | tf_op jit(solution)/shard_map/ppermute | solution.py:264
  13.6 23.7 %collective-permute-start.2 = (bf16[384,512]{1,0:T(8,128)(2,1)}, bf16[384,512]{1,0:T(8,128)(2,1)}, u32[]{:S(2)}, u32[]{:S(2)}) collective-permute-start(bf16[384,512]{1,0:T(8,128)(2,1)} %get-tuple-element.45.q.q0), channel_id=1, source_target_pairs={{1,0},{0,1},{3,2},{2,3},{5,4},{4,5},{7,6},{6,7},{9,8},{8,9},{11,10... | collective-permute-start | bytes 1179656 | tf_op jit(solution)/shard_map/ppermute | solution.py:250
  25.1 40.9 %collective-permute-start.7 = (bf16[384,512]{1,0:T(8,128)(2,1)}, bf16[384,512]{1,0:T(8,128)(2,1)S(1)}, u32[]{:S(2)}, u32[]{:S(2)}) collective-permute-start(bf16[384,512]{1,0:T(8,128)(2,1)} %get-tuple-element.45.q.q0), channel_id=1, source_target_pairs={{128,127},{256,255},{384,383}} | collective-permute-start | bytes 1179656 | tf_op jit(solution)/shard_map/ppermute | solution.py:264
  31.5 12.2 %collective-permute-start.3 = (bf16[384,640]{1,0:T(8,128)(2,1)S(1)}, bf16[384,640]{1,0:T(8,128)(2,1)S(1)}, u32[]{:S(2)}, u32[]{:S(2)}) collective-permute-start(bf16[384,640]{1,0:T(8,128)(2,1)S(1)} %collective-permute-done.q1.a1), channel_id=1, source_target_pairs={{3,1},{5,3},{7,5},{9,7},{11,9},{13,11},{15,13},{17,15},{19,17},{21... | collective-permute-start | bytes 1474568 | tf_op jit(solution)/shard_map/ppermute | solution.py:247
  37.2 28.7 %collective-permute-start.6 = (bf16[384,512]{1,0:T(8,128)(2,1)}, bf16[384,512]{1,0:T(8,128)(2,1)S(1)}, u32[]{:S(2)}, u32[]{:S(2)}) collective-permute-start(bf16[384,512]{1,0:T(8,128)(2,1)} %collective-permute-done.2.q1), channel_id=1, source_target_pairs={{3,1},{5,3},{7,5},{9,7},{11,9},{13,11},{15,13},{17,15},{19,17},{21... | collective-permute-start | bytes 1179656 | tf_op jit(solution)/shard_map/ppermute | solution.py:247
  46.0 32.4 %collective-permute-start.5 = (bf16[384,512]{1,0:T(8,128)(2,1)S(1)}, bf16[384,512]{1,0:T(8,128)(2,1)S(1)}, u32[]{:S(2)}, u32[]{:S(2)}) collective-permute-start(bf16[384,512]{1,0:T(8,128)(2,1)S(1)} %get-tuple-element.62), channel_id=1, source_target_pairs={{1,0},{0,1},{3,2},{2,3},{5,4},{4,5},{7,6},{6,7},{9,8},{8,9},{11,10... | collective-permute-start | bytes 1179656 | tf_op jit(solution)/shard_map/ppermute | solution.py:250
  52.5 25.9 %collective-permute-start.9 = (bf16[384,512]{1,0:T(8,128)(2,1)S(1)}, bf16[384,512]{1,0:T(8,128)(2,1)S(1)}, u32[]{:S(2)}, u32[]{:S(2)}) collective-permute-start(bf16[384,512]{1,0:T(8,128)(2,1)S(1)} %get-tuple-element.67), channel_id=1, source_target_pairs={{2,0},{3,1},{4,2},{5,3},{6,4},{7,5},{8,6},{9,7},{10,8},{11,9},{12,... | collective-permute-start | bytes 1179656 | tf_op jit(solution)/shard_map/ppermute | solution.py:247
  68.2 14.3 %collective-permute-start.8 = (bf16[384,512]{1,0:T(8,128)(2,1)S(1)}, bf16[384,512]{1,0:T(8,128)(2,1)S(1)}, u32[]{:S(2)}, u32[]{:S(2)}) collective-permute-start(bf16[384,512]{1,0:T(8,128)(2,1)S(1)} %get-tuple-element.66), channel_id=1, source_target_pairs={{1,2},{3,4},{5,6},{7,8},{9,10},{11,12},{13,14},{15,16},{17,18},{19... | collective-permute-start | bytes 1179656 | tf_op jit(solution)/shard_map/ppermute | solution.py:312
  69.5 18.6 %collective-permute-start.10 = (bf16[384,512]{1,0:T(8,128)(2,1)S(1)}, bf16[384,512]{1,0:T(8,128)(2,1)S(1)}, u32[]{:S(2)}, u32[]{:S(2)}) collective-permute-start(bf16[384,512]{1,0:T(8,128)(2,1)S(1)} %get-tuple-element.72), channel_id=1, source_target_pairs={{2,0},{3,1},{4,2},{5,3},{6,4},{7,5},{8,6},{9,7},{10,8},{11,9},{12,... | collective-permute-start | bytes 1179656 | tf_op jit(solution)/shard_map/ppermute | solution.py:247

commit v6 on v5

--- a/solution.py
+++ b/solution.py
@@ -197,15 +197,15 @@
     pairs(body)
 
 
-def first_sum(dq_a, dq_b, dkv, r1, r2, back, gq, gk, gv):
-    far = r1[...].astype(f32) + r2[...].astype(f32)
-    gq[:, :WC] = (dq_a[...] * 0.125 + far[:, :WC]).astype(bf16)
-    gq[:, WC:] = (dq_b[...] * 0.125 + far[:, WC:]).astype(bf16)
+def first_sum(dq_a, dq_b, dkv, r1, back, gq, gk, gv):
+    gq[:, :WC] = dq_a[...] * 0.125 + r1[:, :WC].astype(f32)
+    gq[:, WC:] = dq_b[...] * 0.125 + r1[:, WC:].astype(f32)
     gk[...] = (dkv[:, :WC] * 0.125 + back[:, :WC].astype(f32)).astype(bf16)
     gv[...] = (dkv[:, WC:] + back[:, WC:].astype(f32)).astype(bf16)
 
 
-def last_sum(pk, pv, dkv, back, gk, gv):
+def last_sum(pq, pk, pv, dkv, r2, back, gq, gk, gv):
+    gq[...] = (pq[...] + r2[...].astype(f32)).astype(bf16)
     gk[:, :WC] = pk[...]
     gv[:, :WC] = pv[...]
     gk[:, WC:] = (dkv[:, :WC] * 0.125 + back[:, :WC].astype(f32)).astype(bf16)
@@ -310,15 +310,16 @@
             back_q1 = swapped(dq1[0])
         back_kv.append(shifted(send, -2))
     back_q2 = lax.ppermute(dq2[0], AXES, [(i, i + 1) for i in range(1, n - 1, 2)])
-    gq, pk, pv = call(
+    part = call(
         first_sum,
-        [arr(HEADS * SIZE, bf16), arr(WC, bf16), arr(WC, bf16)],
+        [arr(HEADS * SIZE, f32), arr(WC, bf16), arr(WC, bf16)],
         0,
-        (*dqs, dkvs[0], back_q1, back_q2, back_kv[0]),
+        (*dqs, dkvs[0], back_q1, back_kv[0]),
         flops=20 << 30,
     )
-    gk, gv = call(last_sum, [arr(HEADS * SIZE, bf16)] * 2, 0, (pk, pv, dkvs[1], back_kv[1]), flops=1 << 20)
-    return gq, gk, gv
+    return tuple(
+        call(last_sum, [arr(HEADS * SIZE, bf16)] * 3, 0, (*part, dkvs[1], back_q2, back_kv[1]), flops=1 << 20)
+    )
 
 
 def solution(mesh):

time: 89.5 us -> 89.7 us (level)
  no operation moved by 1% of the time
where the time goes in v6:
time: 89.7 us; the launch traced here: 89.2 us
  starting transfers between devices  53.1 us (59%)
  Pallas kernels  22.3 us (25%)
  waiting for transfers between devices  10 us (11%)
  local copies, waits for them, and re-layouts  2.83 us (3%)
  between operations  0.96 us (1%)
    ppermute x5, starting transfers between devices, shifted(): lax.ppermute(x, AXES, [(i - by, i) for i in range(n) if 0 <= i - by < n a...  29.1 us
    pallas_call x9, Pallas kernels, call(): pl.pallas_call(kernel, out_shape=outs, in_specs=[SM] * n_smem + [VM] * ne...  22.3 us
    ppermute x3, starting transfers between devices, swapped(): return lax.ppermute(x, AXES, [(i ^ 1, i) for i in range(n)])  21.3 us
    ppermute x5, waiting for transfers between devices, shifted(): lax.ppermute(x, AXES, [(i - by, i) for i in range(n) if 0 <= i - by < n a...  6.08 us
    ppermute x1, waiting for transfers between devices, per_device(): lax.ppermute(dq2[0], AXES, [(i, i + 1) for i in range(1, n - 1, 2)])  3.95 us
  transfers between devices with their start and end apart: 11, of which 3 were waited for; matrix products, arithmetic and copies ran while one was open for 0% of the time, Pallas kernels for 24%

profile of v6, /device:TPU:40, one launch (start us, length us, event | category | flops | bytes accessed | tf_op | source)
XLA Modules:
  0.0 89.2 jit_solution(10625216580682798971)
XLA Ops:
  0.7 1.1 %constant_dynamic-update-slice_fusion.1 = bf16[384,1024]{1,0:T(8,128)(2,1)S(1)} fusion(bf16[384,512]{1,0:T(8,128)(2,1)} %param.9), kind=kLoop, calls=%fused_computation.2 | loop fusion | bytes 786432
  1.8 1.0 %constant_dynamic-update-slice_fusion.kv.k0 = bf16[384,1024]{1,0:T(8,128)(2,1)S(1)} fusion(bf16[384,1024]{1,0:T(8,128)(2,1)S(1)} %constant_dynamic-update-slice_fusion.1, bf16[384,512]{1,0:T(8,128)(2,1)} %param.10), kind=kLoop, calls=%fused_computation.1 | loop fusion | bytes 786432 | tf_op jit(solution)/shard_map/concatenate | solution.py:254
  2.8 4.3 %collective-permute-start.1 = (bf16[384,1024]{1,0:T(8,128)(2,1)S(1)}, bf16[384,1024]{1,0:T(8,128)(2,1)S(1)}, u32[]{:S(2)}, u32[]{:S(2)}) collective-permute-start(bf16[384,1024]{1,0:T(8,128)(2,1)S(1)} %constant_dynamic-update-slice_fusion.kv.k0), channel_id=1, source_target_pairs={{0,2},{1,3},{2,4},{3,5},{4,6},{5,7},{6,8},{7,9},{8,10},{9,11},{10,... | collective-permute-start | bytes 2359304 | tf_op jit(solution)/shard_map/ppermute | solution.py:247
  7.2 0.0 copy-start
  7.2 0.0 copy-start.1
  7.2 0.0 copy-start.2
  7.2 0.1 pad_maximum_fusion.everything
  7.3 0.6 copy-done
  7.9 1.7 %shard_map.103 = (bf16[384,640]{1,0:T(8,128)(2,1)S(1)}, bf16[384,512]{1,0:T(8,128)(2,1)}, f32[8,384]{1,0:T(8,128)S(1)}) custom-call(s32[1]{0:T(128)} %bitcast.1.blk, s32[1,3]{1,0:T(1,128)S(1)} %copy-done.2, f32[8,384]{1,0:T(8,128)S(1)} %copy-done, s32[1,384]{1,0:T(1,128)S(1)} %copy-done.1, bf16[384,1536]{1,0:T(8,128)(2,1)S(1)} %pad_maximum_fusion.everything), custom_call_target="tpu_custom_call" | custom-call | bytes 1024 | tf_op jit(solution)/shard_map/pallas_call | solution.py:221
  9.6 3.2 %collective-permute-start = (bf16[384,640]{1,0:T(8,128)(2,1)S(1)}, bf16[384,640]{1,0:T(8,128)(2,1)S(1)}, u32[]{:S(2)}, u32[]{:S(2)}) collective-permute-start(bf16[384,640]{1,0:T(8,128)(2,1)S(1)} %get-tuple-element.38.q.qa.q0.a0), channel_id=1, source_target_pairs={{1,0},{0,1},{3,2},{2,3},{5,4},{4,5},{7,6},{6,7},{9,8},{8,9},{11,10... | collective-permute-start | bytes 1474568 | tf_op jit(solution)/shard_map/ppermute | solution.py:250
  12.9 0.7 collective-permute-start.4
  13.6 11.5 %collective-permute-start.2 = (bf16[384,512]{1,0:T(8,128)(2,1)}, bf16[384,512]{1,0:T(8,128)(2,1)}, u32[]{:S(2)}, u32[]{:S(2)}) collective-permute-start(bf16[384,512]{1,0:T(8,128)(2,1)} %get-tuple-element.43.q.q0), channel_id=1, source_target_pairs={{1,0},{0,1},{3,2},{2,3},{5,4},{4,5},{7,6},{6,7},{9,8},{8,9},{11,10... | collective-permute-start | bytes 1179656 | tf_op jit(solution)/shard_map/ppermute | solution.py:250
  25.1 0.7 collective-permute-start.8
  25.8 2.3 %shard_map.104 = (f32[384,256]{1,0:T(8,128)S(1)}, f32[384,512]{1,0:T(8,128)S(1)}) custom-call(bf16[384,640]{1,0:T(8,128)(2,1)S(1)} %get-tuple-element.38.q.qa.q0.a0, bf16[384,640]{1,0:T(8,128)(2,1)S(1)} %get-tuple-element.38.q.qa.q0.a0, bf16[384,1024]{1,0:T(8,128)(2,1)S(1)} %constant_dynamic-update-slice_fusion.kv.k0, f32[8,384]{1,0:T(8,128)S(1)} %get-tuple-element.40.rank), custom_call_target="tpu_custom_call" | custom-call | flops 3019898880 | bytes 1024 | tf_op jit(solution)/shard_map/pallas_call | solution.py:221
  28.1 3.3 %shard_map.105 = (f32[384,256]{1,0:T(8,128)S(1)}, f32[384,512]{1,0:T(8,128)S(1)}) custom-call(bf16[384,512]{1,0:T(8,128)(2,1)} %get-tuple-element.43.q.q0, bf16[384,640]{1,0:T(8,128)(2,1)S(1)} %get-tuple-element.38.q.qa.q0.a0, bf16[384,1024]{1,0:T(8,128)(2,1)S(1)} %constant_dynamic-update-slice_fusion.kv.k0, f32[8,384]{1,0:T(8,128)S(1)} %get-tuple-element.40.rank), custom_call_target="tpu_custom_call" | custom-call | flops 3019898880 | bytes 1024 | tf_op jit(solution)/shard_map/pallas_call | solution.py:221
  31.5 1.3 %collective-permute-start.3 = (bf16[384,640]{1,0:T(8,128)(2,1)S(1)}, bf16[384,640]{1,0:T(8,128)(2,1)S(1)}, u32[]{:S(2)}, u32[]{:S(2)}) collective-permute-start(bf16[384,640]{1,0:T(8,128)(2,1)S(1)} %collective-permute-done.q1.a1), channel_id=1, source_target_pairs={{3,1},{5,3},{7,5},{9,7},{11,9},{13,11},{15,13},{17,15},{19,17},{21... | collective-permute-start | bytes 1474568 | tf_op jit(solution)/shard_map/ppermute | solution.py:247
  32.8 0.5 collective-permute-done.1.k1
  33.2 4.0 %shard_map.106 = (f32[384,256]{1,0:T(8,128)S(1)}, f32[384,512]{1,0:T(8,128)S(1)}, bf16[384,256]{1,0:T(8,128)(2,1)S(1)}, f32[384,512]{1,0:T(8,128)S(1)}) custom-call(s32[1]{0:T(128)} %bitcast.odd, bf16[384,640]{1,0:T(8,128)(2,1)S(1)} %get-tuple-element.38.q.qa.q0.a0, bf16[384,640]{1,0:T(8,128)(2,1)S(1)} %get-tuple-element.38.q.qa.q0.a0, ...), custom_call_target="tpu_custom_call" | custom-call | flops 9059696640 | bytes 1024 | tf_op jit(solution)/shard_map/pallas_call | solution.py:221
  37.2 0.0 collective-permute-done.2.q1
  37.2 1.3 %collective-permute-start.7 = (bf16[384,512]{1,0:T(8,128)(2,1)}, bf16[384,512]{1,0:T(8,128)(2,1)S(1)}, u32[]{:S(2)}, u32[]{:S(2)}) collective-permute-start(bf16[384,512]{1,0:T(8,128)(2,1)} %collective-permute-done.2.q1), channel_id=1, source_target_pairs={{3,1},{5,3},{7,5},{9,7},{11,9},{13,11},{15,13},{17,15},{19,17},{21... | collective-permute-start | bytes 1179656 | tf_op jit(solution)/shard_map/ppermute | solution.py:247
  38.5 5.1 %shard_map.107 = (f32[384,256]{1,0:T(8,128)S(1)}, f32[384,512]{1,0:T(8,128)S(1)}, bf16[384,512]{1,0:T(8,128)(2,1)S(1)}, f32[384,512]{1,0:T(8,128)S(1)}) custom-call(s32[1]{0:T(128)} %bitcast.odd, bf16[384,512]{1,0:T(8,128)(2,1)} %get-tuple-element.43.q.q0, bf16[384,640]{1,0:T(8,128)(2,1)S(1)} %get-tuple-element.38.q.qa.q0.a0, ...), custom_call_target="tpu_custom_call" | custom-call | flops 9059696640 | bytes 1024 | tf_op jit(solution)/shard_map/pallas_call | solution.py:221
  43.7 0.0 collective-permute-done.4.edge
  43.7 2.2 %shard_map.108 = (bf16[384,256]{1,0:T(8,128)(2,1)S(1)}, bf16[384,512]{1,0:T(8,128)(2,1)S(1)}, bf16[384,640]{1,0:T(8,128)(2,1)S(1)}) custom-call(s32[1]{0:T(128)} %bitcast.odd, bf16[384,640]{1,0:T(8,128)(2,1)S(1)} %copy.14.q2_far, bf16[384,640]{1,0:T(8,128)(2,1)S(1)} %collective-permute-done.3.a2_far, ...), custom_call_target="tpu_custom_call", output_to_operand_aliasing={{2}: (1, {})} | custom-call | bytes 1024 | tf_op jit(solution)/shard_map/pallas_call | solution.py:221
  46.0 6.5 %collective-permute-start.5 = (bf16[384,512]{1,0:T(8,128)(2,1)S(1)}, bf16[384,512]{1,0:T(8,128)(2,1)S(1)}, u32[]{:S(2)}, u32[]{:S(2)}) collective-permute-start(bf16[384,512]{1,0:T(8,128)(2,1)S(1)} %get-tuple-element.60), channel_id=1, source_target_pairs={{1,0},{0,1},{3,2},{2,3},{5,4},{4,5},{7,6},{6,7},{9,8},{8,9},{11,10... | collective-permute-start | bytes 1179656 | tf_op jit(solution)/shard_map/ppermute | solution.py:250
  52.5 13.5 %collective-permute-start.6 = (bf16[384,512]{1,0:T(8,128)(2,1)S(1)}, bf16[384,512]{1,0:T(8,128)(2,1)S(1)}, u32[]{:S(2)}, u32[]{:S(2)}) collective-permute-start(bf16[384,512]{1,0:T(8,128)(2,1)S(1)} %get-tuple-element.61), channel_id=1, source_target_pairs={{2,0},{3,1},{4,2},{5,3},{6,4},{7,5},{8,6},{9,7},{10,8},{11,9},{12,... | collective-permute-start | bytes 1179656 | tf_op jit(solution)/shard_map/ppermute | solution.py:247
  66.0 2.2 %shard_map.110 = (bf16[384,512]{1,0:T(8,128)(2,1)S(1)}, bf16[384,512]{1,0:T(8,128)(2,1)S(1)}, bf16[384,512]{1,0:T(8,128)(2,1)S(1)}) custom-call(s32[1]{0:T(128)} %bitcast.odd, bf16[384,512]{1,0:T(8,128)(2,1)S(1)} %collective-permute-done.7.q2_far, bf16[384,640]{1,0:T(8,128)(2,1)S(1)} %get-tuple-element.66.a2_far, ...), custom_call_target="tpu_custom_call", output_to_operand_aliasing={{2}: (1, {})} | custom-call | bytes 1024 | tf_op jit(solution)/shard_map/pallas_call | solution.py:221
  68.2 1.3 %collective-permute-start.9 = (bf16[384,512]{1,0:T(8,128)(2,1)S(1)}, bf16[384,512]{1,0:T(8,128)(2,1)S(1)}, u32[]{:S(2)}, u32[]{:S(2)}) collective-permute-start(bf16[384,512]{1,0:T(8,128)(2,1)S(1)} %get-tuple-element.69), channel_id=1, source_target_pairs={{1,2},{3,4},{5,6},{7,8},{9,10},{11,12},{13,14},{15,16},{17,18},{19... | collective-permute-start | bytes 1179656 | tf_op jit(solution)/shard_map/ppermute | solution.py:312
  69.5 8.8 %collective-permute-start.10 = (bf16[384,512]{1,0:T(8,128)(2,1)S(1)}, bf16[384,512]{1,0:T(8,128)(2,1)S(1)}, u32[]{:S(2)}, u32[]{:S(2)}) collective-permute-start(bf16[384,512]{1,0:T(8,128)(2,1)S(1)} %get-tuple-element.70), channel_id=1, source_target_pairs={{2,0},{3,1},{4,2},{5,3},{6,4},{7,5},{8,6},{9,7},{10,8},{11,9},{12,... | collective-permute-start | bytes 1179656 | tf_op jit(solution)/shard_map/ppermute | solution.py:247
  78.4 0.2 shard_map.109
  78.5 3.9 %collective-permute-done.9.r2 = bf16[384,512]{1,0:T(8,128)(2,1)S(1)} collective-permute-done((bf16[384,512]{1,0:T(8,128)(2,1)S(1)}, bf16[384,512]{1,0:T(8,128)(2,1)S(1)}, u32[]{:S(2)}, u32[]{:S(2)}) %collective-permute-start.9) | collective-permute-done | bytes 393248 | tf_op jit(solution)/shard_map/ppermute | solution.py:312
  82.5 5.6 %collective-permute-done.10.back = bf16[384,512]{1,0:T(8,128)(2,1)S(1)} collective-permute-done((bf16[384,512]{1,0:T(8,128)(2,1)S(1)}, bf16[384,512]{1,0:T(8,128)(2,1)S(1)}, u32[]{:S(2)}, u32[]{:S(2)}) %collective-permute-start.10) | collective-permute-done | bytes 393248 | tf_op jit(solution)/shard_map/ppermute | solution.py:247
  88.1 1.1 %shard_map.111 = (bf16[384,512]{1,0:T(8,128)(2,1)}, bf16[384,512]{1,0:T(8,128)(2,1)}, bf16[384,512]{1,0:T(8,128)(2,1)}) custom-call(f32[384,512]{1,0:T(8,128)S(1)} %get-tuple-element.62.pq, bf16[384,256]{1,0:T(8,128)(2,1)S(1)} %get-tuple-element.63.pk, bf16[384,256]{1,0:T(8,128)(2,1)S(1)} %get-tuple-element.64.pv, f32[384,512]{1,0:T(8,128)S(1)} %get-tuple-element.65.dkv, ...), custom_call_target="tpu_custom_call" | custom-call | flops 1048576 | bytes 1024 | tf_op jit(solution)/shard_map/pallas_call | solution.py:221
  (15 shorter events, 0.1 us)
Async XLA Ops:
  0.6 6.5 %copy-start.5 = (bf16[384,512]{1,0:T(8,128)(2,1)S(1)}, bf16[384,512]{1,0:T(8,128)(2,1)}, u32[]{:S(2)}) copy-start(bf16[384,512]{1,0:T(8,128)(2,1)} %param.8) | copy-start | bytes 1179652
  0.6 6.5 %copy-start.3 = (bf16[384,512]{1,0:T(8,128)(2,1)S(1)}, bf16[384,512]{1,0:T(8,128)(2,1)}, u32[]{:S(2)}) copy-start(bf16[384,512]{1,0:T(8,128)(2,1)} %param.11) | copy-start | bytes 1179652
  0.7 6.5 %copy-start.4 = (bf16[384,512]{1,0:T(8,128)(2,1)S(1)}, bf16[384,512]{1,0:T(8,128)(2,1)}, u32[]{:S(2)}) copy-start(bf16[384,512]{1,0:T(8,128)(2,1)} %param.12) | copy-start | bytes 1179652
  2.8 30.4 %collective-permute-start.1 = (bf16[384,1024]{1,0:T(8,128)(2,1)S(1)}, bf16[384,1024]{1,0:T(8,128)(2,1)S(1)}, u32[]{:S(2)}, u32[]{:S(2)}) collective-permute-start(bf16[384,1024]{1,0:T(8,128)(2,1)S(1)} %constant_dynamic-update-slice_fusion.kv.k0), channel_id=1, source_target_pairs={{0,2},{1,3},{2,4},{3,5},{4,6},{5,7},{6,8},{7,9},{8,10},{9,11},{10,... | collective-permute-start | bytes 2359304 | tf_op jit(solution)/shard_map/ppermute | solution.py:247
  7.2 0.7 copy-start
  7.2 0.7 copy-start.1
  7.2 0.7 copy-start.2
  9.6 21.9 %collective-permute-start = (bf16[384,640]{1,0:T(8,128)(2,1)S(1)}, bf16[384,640]{1,0:T(8,128)(2,1)S(1)}, u32[]{:S(2)}, u32[]{:S(2)}) collective-permute-start(bf16[384,640]{1,0:T(8,128)(2,1)S(1)} %get-tuple-element.38.q.qa.q0.a0), channel_id=1, source_target_pairs={{1,0},{0,1},{3,2},{2,3},{5,4},{4,5},{7,6},{6,7},{9,8},{8,9},{11,10... | collective-permute-start | bytes 1474568 | tf_op jit(solution)/shard_map/ppermute | solution.py:250
  12.9 30.9 %collective-permute-start.4 = (bf16[384,640]{1,0:T(8,128)(2,1)S(1)}, bf16[384,640]{1,0:T(8,128)(2,1)S(1)}, u32[]{:S(2)}, u32[]{:S(2)}) collective-permute-start(bf16[384,640]{1,0:T(8,128)(2,1)S(1)} %get-tuple-element.38.q.qa.q0.a0), channel_id=1, source_target_pairs={{128,127},{256,255},{384,383}} | collective-permute-start | bytes 1474568 | tf_op jit(solution)/shard_map/ppermute | solution.py:264
  13.6 23.7 %collective-permute-start.2 = (bf16[384,512]{1,0:T(8,128)(2,1)}, bf16[384,512]{1,0:T(8,128)(2,1)}, u32[]{:S(2)}, u32[]{:S(2)}) collective-permute-start(bf16[384,512]{1,0:T(8,128)(2,1)} %get-tuple-element.43.q.q0), channel_id=1, source_target_pairs={{1,0},{0,1},{3,2},{2,3},{5,4},{4,5},{7,6},{6,7},{9,8},{8,9},{11,10... | collective-permute-start | bytes 1179656 | tf_op jit(solution)/shard_map/ppermute | solution.py:250
  25.1 40.9 %collective-permute-start.8 = (bf16[384,512]{1,0:T(8,128)(2,1)}, bf16[384,512]{1,0:T(8,128)(2,1)S(1)}, u32[]{:S(2)}, u32[]{:S(2)}) collective-permute-start(bf16[384,512]{1,0:T(8,128)(2,1)} %get-tuple-element.43.q.q0), channel_id=1, source_target_pairs={{128,127},{256,255},{384,383}} | collective-permute-start | bytes 1179656 | tf_op jit(solution)/shard_map/ppermute | solution.py:264
  31.5 12.2 %collective-permute-start.3 = (bf16[384,640]{1,0:T(8,128)(2,1)S(1)}, bf16[384,640]{1,0:T(8,128)(2,1)S(1)}, u32[]{:S(2)}, u32[]{:S(2)}) collective-permute-start(bf16[384,640]{1,0:T(8,128)(2,1)S(1)} %collective-permute-done.q1.a1), channel_id=1, source_target_pairs={{3,1},{5,3},{7,5},{9,7},{11,9},{13,11},{15,13},{17,15},{19,17},{21... | collective-permute-start | bytes 1474568 | tf_op jit(solution)/shard_map/ppermute | solution.py:247
  37.2 28.7 %collective-permute-start.7 = (bf16[384,512]{1,0:T(8,128)(2,1)}, bf16[384,512]{1,0:T(8,128)(2,1)S(1)}, u32[]{:S(2)}, u32[]{:S(2)}) collective-permute-start(bf16[384,512]{1,0:T(8,128)(2,1)} %collective-permute-done.2.q1), channel_id=1, source_target_pairs={{3,1},{5,3},{7,5},{9,7},{11,9},{13,11},{15,13},{17,15},{19,17},{21... | collective-permute-start | bytes 1179656 | tf_op jit(solution)/shard_map/ppermute | solution.py:247
  46.0 32.4 %collective-permute-start.5 = (bf16[384,512]{1,0:T(8,128)(2,1)S(1)}, bf16[384,512]{1,0:T(8,128)(2,1)S(1)}, u32[]{:S(2)}, u32[]{:S(2)}) collective-permute-start(bf16[384,512]{1,0:T(8,128)(2,1)S(1)} %get-tuple-element.60), channel_id=1, source_target_pairs={{1,0},{0,1},{3,2},{2,3},{5,4},{4,5},{7,6},{6,7},{9,8},{8,9},{11,10... | collective-permute-start | bytes 1179656 | tf_op jit(solution)/shard_map/ppermute | solution.py:250
  52.5 25.9 %collective-permute-start.6 = (bf16[384,512]{1,0:T(8,128)(2,1)S(1)}, bf16[384,512]{1,0:T(8,128)(2,1)S(1)}, u32[]{:S(2)}, u32[]{:S(2)}) collective-permute-start(bf16[384,512]{1,0:T(8,128)(2,1)S(1)} %get-tuple-element.61), channel_id=1, source_target_pairs={{2,0},{3,1},{4,2},{5,3},{6,4},{7,5},{8,6},{9,7},{10,8},{11,9},{12,... | collective-permute-start | bytes 1179656 | tf_op jit(solution)/shard_map/ppermute | solution.py:247
  68.2 14.3 %collective-permute-start.9 = (bf16[384,512]{1,0:T(8,128)(2,1)S(1)}, bf16[384,512]{1,0:T(8,128)(2,1)S(1)}, u32[]{:S(2)}, u32[]{:S(2)}) collective-permute-start(bf16[384,512]{1,0:T(8,128)(2,1)S(1)} %get-tuple-element.69), channel_id=1, source_target_pairs={{1,2},{3,4},{5,6},{7,8},{9,10},{11,12},{13,14},{15,16},{17,18},{19... | collective-permute-start | bytes 1179656 | tf_op jit(solution)/shard_map/ppermute | solution.py:312
  69.5 18.6 %collective-permute-start.10 = (bf16[384,512]{1,0:T(8,128)(2,1)S(1)}, bf16[384,512]{1,0:T(8,128)(2,1)S(1)}, u32[]{:S(2)}, u32[]{:S(2)}) collective-permute-start(bf16[384,512]{1,0:T(8,128)(2,1)S(1)} %get-tuple-element.70), channel_id=1, source_target_pairs={{2,0},{3,1},{4,2},{5,3},{6,4},{7,5},{8,6},{9,7},{10,8},{11,9},{12,... | collective-permute-start | bytes 1179656 | tf_op jit(solution)/shard_map/ppermute | solution.py:247
